TPU v7x, 32 devices: a whole 2x2x4 slice. The times are simulated.
32 devices in a mesh: chain: 4 (over y, x), tok: 8 (over z, core).
Axes of the slice: x: 2, y: 2, z: 4, core: 2. Of those that a mesh axis runs over, the one named last changes fastest.
Arguments:
- layer_activations: bfloat16 [2048, 8192], P('tok'), may hold values from -6 to 6
- rotated_probes: bfloat16 [2048, 8192], P('tok'), may hold values from -6 to 6
- attended_contents: bfloat16 [2048, 1024], P('tok'), may hold values from -6 to 6
- attended_slope: bfloat16 [2048, 8192], P('tok'), may hold values from -6 to 6
- locked_projection: bfloat16 [8192, 1024], P('tok', 'chain'), may hold values from -0.044194174 to 0.044194174
- first_multipliers: float32 [8, 8192, 64], P('chain', 'tok'), may hold values from -6 to 6
- second_multipliers: float32 [8, 64, 1024], P('chain', None, 'tok'), may hold values from -6 to 6
- first_jitter: float32 [8, 8192, 64], P('chain', 'tok'), may hold values from -6 to 6
- second_jitter: float32 [8, 64, 1024], P('chain', None, 'tok'), may hold values from -6 to 6
- chain_heats: float32 [8], P('chain'), may hold values from 0.05 to 1
- donor_chain: int32 [8], replicated, may hold values from 0 to 7, each once
Outputs:
- new_a: float32 [8, 8192, 64], P('chain', 'tok')
- new_b: float32 [8, 64, 1024], P('chain', None, 'tok')
All inputs are finite; a program needn't handle non-finite values.
Results may differ from a plain program's by a relative error of at most 0.019.
Values may be sent and summed in bfloat16 or wider, within the bound.
No kernel may reach another device: no remote copies, remote signals or barrier semaphores. Data moves between devices by JAX's collectives and lax.ppermute only.
A program may use at most 128 MiB of HBM per device.

v0:
```python
import math

import jax
import jax.numpy as jnp
from jax import lax
from jax.sharding import PartitionSpec as P

MODEL_WIDTH = 8192
QUERY_HEADS = 64
KEY_HEADS = 8
HEAD_SIZE = 128
ADAPTER_RANK = 64


STRIDE_LENGTH = 0.2


def key_gradient(query_item, key_item, value_item, grad_item):
    score_scale = 1.0 / math.sqrt(HEAD_SIZE)
    scores = (
        jnp.einsum("tjd,sd->jts", query_item, key_item, preferred_element_type=jnp.float32)
        * score_scale
    )
    length = key_item.shape[0]
    future_mask = lax.broadcasted_iota(jnp.int32, (length, length), 1) > lax.broadcasted_iota(
        jnp.int32, (length, length), 0
    )
    scores = jnp.where(future_mask[None], -1e30, scores)
    row_max = jnp.max(scores, axis=-1, keepdims=True)
    expo = jnp.exp(scores - row_max)
    attn_weights = expo / jnp.sum(expo, axis=-1, keepdims=True)
    dweights = jnp.einsum("tjd,sd->jts", grad_item, value_item, preferred_element_type=jnp.float32)
    center = jnp.sum(attn_weights * dweights, axis=-1, keepdims=True)
    dscores = (attn_weights * (dweights - center)).astype(jnp.bfloat16)
    return (
        jnp.einsum("jts,tjd->sd", dscores, query_item, preferred_element_type=jnp.float32)
        * score_scale
    )


def per_device(
    layer_activations,
    rotated_probes,
    attended_contents,
    attended_slope,
    locked_projection,
    first_multipliers,
    second_multipliers,
    first_jitter,
    second_jitter,
    chain_heats,
    donor_chain,
):
    adapter_scale = 1.0 / math.sqrt(MODEL_WIDTH * ADAPTER_RANK)
    token_rows = layer_activations.shape[0]
    chain_local = first_multipliers.shape[0]
    query_group = QUERY_HEADS // KEY_HEADS
    whole_columns = lax.all_gather(locked_projection, "chain", axis=1, tiled=True)
    columns = layer_activations
    plain_keys = jnp.dot(
        columns,
        lax.all_gather(whole_columns, "tok", axis=0, tiled=True),
        preferred_element_type=jnp.float32,
    ).astype(jnp.bfloat16)
    a_low = first_multipliers.astype(jnp.bfloat16)
    columns = layer_activations
    low_rank_keys = jnp.einsum(
        "td,cdr->ctr",
        columns,
        lax.all_gather(a_low, "tok", axis=1, tiled=True),
        preferred_element_type=jnp.float32,
    ).astype(jnp.bfloat16)
    right_low_rank = lax.all_gather(
        second_multipliers.astype(jnp.bfloat16), "tok", axis=2, tiled=True
    )
    key_rows = (
        plain_keys.astype(jnp.float32)[None]
        + adapter_scale
        * jnp.einsum(
            "ctr,crk->ctk", low_rank_keys, right_low_rank, preferred_element_type=jnp.float32
        )
    ).astype(jnp.bfloat16)
    query_tensor = rotated_probes.reshape(token_rows, KEY_HEADS, query_group, HEAD_SIZE).transpose(
        1, 0, 2, 3
    )
    gradient_total = attended_slope.reshape(
        token_rows, KEY_HEADS, query_group, HEAD_SIZE
    ).transpose(1, 0, 2, 3)
    value_tensor = attended_contents.reshape(token_rows, KEY_HEADS, HEAD_SIZE).transpose(1, 0, 2)
    gradient_entries = []
    for replica_position in range(chain_local):
        key_tensor = (
            key_rows[replica_position].reshape(token_rows, KEY_HEADS, HEAD_SIZE).transpose(1, 0, 2)
        )
        step_result = lax.map(
            lambda items: key_gradient(*items),
            (query_tensor, key_tensor, value_tensor, gradient_total),
        )
        gradient_entries.append(
            step_result.transpose(1, 0, 2).reshape(token_rows, KEY_HEADS * HEAD_SIZE)
        )
    key_input_gradient = jnp.stack(gradient_entries).astype(jnp.bfloat16)
    low_rank_gradient = (
        adapter_scale
        * jnp.einsum(
            "bpo,bmo->bpm", key_input_gradient, right_low_rank, preferred_element_type=jnp.float32
        )
    ).astype(jnp.bfloat16)
    right_term = adapter_scale * jnp.einsum(
        "ctr,ctk->crk", low_rank_keys, key_input_gradient, preferred_element_type=jnp.float32
    )
    columns = layer_activations
    first_slope = lax.psum_scatter(
        jnp.einsum("td,ctr->dcr", columns, low_rank_gradient, preferred_element_type=jnp.float32),
        "tok",
        scatter_dimension=0,
        tiled=True,
    ).transpose(1, 0, 2)
    second_slope = lax.psum_scatter(right_term, "tok", scatter_dimension=2, tiled=True)
    chain_heat = jnp.sqrt(2.0 * STRIDE_LENGTH * chain_heats)
    shifted_first = (
        first_multipliers
        - STRIDE_LENGTH * (first_slope + first_multipliers)
        + chain_heat[:, None, None] * first_jitter
    )
    shifted_second = (
        second_multipliers
        - STRIDE_LENGTH * (second_slope + second_multipliers)
        + chain_heat[:, None, None] * second_jitter
    )
    every_a, every_b = (
        lax.all_gather(shifted_first, "chain", axis=0, tiled=True),
        lax.all_gather(shifted_second, "chain", axis=0, tiled=True),
    )
    slots = lax.axis_index("chain") * chain_local + jnp.arange(chain_local, dtype=jnp.int32)
    sources = jnp.take(donor_chain, slots, axis=0)
    return (jnp.take(every_a, sources, axis=0), jnp.take(every_b, sources, axis=0))


def solution(mesh):
    return jax.shard_map(
        per_device,
        mesh=mesh,
        in_specs=(
            P("tok", None),
            P("tok", None),
            P("tok", None),
            P("tok", None),
            P("tok", "chain"),
            P("chain", "tok", None),
            P("chain", None, "tok"),
            P("chain", "tok", None),
            P("chain", None, "tok"),
            P("chain"),
            P(),
        ),
        out_specs=(P("chain", "tok", None), P("chain", None, "tok")),
        check_vma=False,
    )
```

profile of v0, /device:TPU:8, one launch (start us, length us, event | category | flops | bytes accessed | tf_op | source)
XLA Modules:
  0.0 531.2 jit_solution(16706158480230333343)
XLA Ops:
  9.8 36.4 %all-gather.5.cloned.1.call-done = bf16[1024,1024]{1,0:T(8,128)(2,1)} async-done(((bf16[1024,256]{1,0:T(8,128)(2,1)}), bf16[1024,1024]{1,0:T(8,128)(2,1)}) %all-gather.5.cloned.1.call-update) | async-done | bytes 2097168 | tf_op jit(solution)/shard_map/all_gather | solution.py:58
  46.8 6.4 %copy.31 = bf16[256,8192]{0,1:T(8,128)(2,1)} copy(bf16[256,8192]{1,0:T(8,128)(2,1)} %param.16) | data formatting | bytes 8388608 | tf_op args[1]
  53.2 6.5 %copy.34 = bf16[8,256,8,128]{3,1,2,0:T(8,128)(2,1)} copy(bf16[8,256,8,128]{1,3,2,0:T(8,128)(2,1)} %bitcast.267) | data formatting | bytes 8388608 | tf_op jit(solution)/shard_map/while | solution.py:95
  59.7 6.4 %copy.33 = bf16[256,8192]{0,1:T(8,128)(2,1)} copy(bf16[256,8192]{1,0:T(8,128)(2,1)} %param.18) | data formatting | bytes 8388608 | tf_op args[3]
  66.1 6.5 %copy.36 = bf16[8,256,8,128]{3,1,2,0:T(8,128)(2,1)} copy(bf16[8,256,8,128]{1,3,2,0:T(8,128)(2,1)} %bitcast.268) | data formatting | bytes 8388608 | tf_op jit(solution)/shard_map/while | solution.py:95
  72.6 13.2 %all_gather.21 = bf16[2,64,1024]{2,1,0:T(8,128)(2,1)S(1)} all-gather(bf16[2,64,128]{2,1,0:T(8,128)(2,1)S(1)} %convert_element_type.33), channel_id=1, replica_groups=mesh['chain'=4,'tok'=8] {'tok'}, dimensions={2}, use_global_device_ids=true | all-gather | bytes 294912 | tf_op jit(solution)/shard_map/all_gather | solution.py:73
  85.8 5.2 fusion.123
  91.0 136.1 %all-gather.7.cloned.1.call-done = bf16[8192,1024]{1,0:T(8,128)(2,1)} async-done(((bf16[1024,1024]{1,0:T(8,128)(2,1)}), bf16[8192,1024]{1,0:T(8,128)(2,1)}) %all-gather.7.cloned.1.call-update) | async-done | bytes 16777232 | tf_op jit(solution)/shard_map/all_gather | solution.py:62
  227.1 9.3 %fusion.121 = f32[256,1024]{1,0:T(8,128)S(1)} fusion(bf16[256,8192]{1,0:T(8,128)(2,1)} %param.15, bf16[8192,1024]{1,0:T(8,128)(2,1)} %all-gather.7.cloned.1.call-done), kind=kOutput, calls=%fused_computation.93 | convolution fusion | flops 4295491584 | bytes 22020096 | tf_op jit(solution)/shard_map/dot_general | solution.py:60
  237.4 79.4 %while.21 = (s32[]{:T(128)}, bf16[8,256,128]{2,1,0:T(8,128)(2,1)S(1)}, bf16[8,256,128]{2,1,0:T(8,128)(2,1)S(1)}, bf16[8,256,8,128]{3,1,2,0:T(8,128)(2,1)}, bf16[...) while((s32[]{:T(128)}, bf16[8,256,128]{2,1,0:T(8,128)(2,1)S(1)}, ...), condition=%wide.region_9.10_spmd, body=%wide.region_5.9_spmd.sunk | while | flops 544309760 | bytes 11055189 | solution.py:95
  260.4 3.5 fusion.186
  270.3 3.5 fusion.186
  280.3 3.5 fusion.186
  290.2 3.5 fusion.186
  300.1 3.5 fusion.186
  310.0 3.5 fusion.186
  317.4 79.4 %while.20 = (s32[]{:T(128)}, bf16[8,256,128]{2,1,0:T(8,128)(2,1)S(1)}, bf16[8,256,128]{2,1,0:T(8,128)(2,1)S(1)}, bf16[8,256,8,128]{3,1,2,0:T(8,128)(2,1)}, bf16[...) while((s32[]{:T(128)}, bf16[8,256,128]{2,1,0:T(8,128)(2,1)S(1)}, ...), condition=%wide.region_4.5_spmd, body=%wide.region_0.4_spmd.sunk | while | flops 544309760 | bytes 11055189 | solution.py:95
  330.5 3.5 fusion.177
  340.5 3.5 fusion.177
  397.4 5.3 convolution_bitcast_fusion.2
  404.0 46.3 %reduce-scatter.3.cloned.1.call-done = f32[1024,2,64]{0,2,1:T(8,128)} async-done(((f32[8192,2,64]{0,2,1:T(8,128)}), f32[1024,2,64]{0,2,1:T(8,128)}) %reduce-scatter.3.cloned.1.call-update) | async-done | bytes 524304 | tf_op jit(solution)/shard_map/reduce_scatter | solution.py:113
  453.1 28.7 %reduce-scatter.5.cloned.1.call-done = f32[2,64,128]{2,1,0:T(8,128)} async-done(((f32[2,64,1024]{2,1,0:T(8,128)}), f32[2,64,128]{2,1,0:T(8,128)}) %reduce-scatter.5.cloned.1.call-update) | async-done | bytes 65552 | tf_op jit(solution)/shard_map/reduce_scatter | solution.py:119
  482.7 8.9 %all_gather.23 = f32[8,64,128]{2,1,0:T(8,128)S(1)} all-gather(f32[2,64,128]{2,1,0:T(8,128)S(1)} %multiply_add_fusion), channel_id=1, replica_groups=mesh['chain'=4,'tok'=8] {'chain'}, dimensions={0}, use_global_device_ids=true | all-gather | bytes 327680 | tf_op jit(solution)/shard_map/all_gather | solution.py:133
  492.8 28.4 %all-gather.11.cloned.1.call-done = f32[8,1024,64]{1,2,0:T(8,128)} async-done(((f32[2,1024,64]{1,2,0:T(8,128)}), f32[8,1024,64]{1,2,0:T(8,128)}) %all-gather.11.cloned.1.call-update) | async-done | bytes 2097168 | tf_op jit(solution)/shard_map/all_gather | solution.py:132
  (115 shorter events, 144.8 us)
Async XLA Ops:
  7.2 445.2 %copy-start = (s32[8]{0:T(128)S(1)}, s32[8]{0:T(128)}, u32[]{:S(2)}) copy-start(s32[8]{0:T(128)} %param.25) | copy-start | bytes 100
  7.2 39.1 %copy-start.4 = (f32[2,64,128]{2,1,0:T(8,128)S(1)}, f32[2,64,128]{2,1,0:T(8,128)}, u32[]{:S(2)}) copy-start(f32[2,64,128]{2,1,0:T(8,128)} %param.21) | copy-start | bytes 196612
  7.2 39.1 %copy-start.3 = (bf16[256,1024]{1,0:T(8,128)(2,1)S(1)}, bf16[256,1024]{1,0:T(8,128)(2,1)}, u32[]{:S(2)}) copy-start(bf16[256,1024]{1,0:T(8,128)(2,1)} %param.17) | copy-start | bytes 1572868
  7.2 39.0 %all-gather.5.cloned.1.call-start = ((), (), s32[]{:S(2)}) async-start(), calls=%async_computation.2 | async-start | bytes 2621440 | tf_op jit(solution)/shard_map/all_gather | solution.py:58
  7.9 77.8 %all-gather.9.cloned.1.call-start = ((), (), s32[]{:S(2)}) async-start(), calls=%async_computation.4 | async-start | bytes 2359296 | tf_op jit(solution)/shard_map/all_gather | solution.py:70
  9.8 217.3 %all-gather.7.cloned.1.call-start = ((), (), s32[]{:S(2)}) async-start(), calls=%async_computation.3 | async-start | bytes 18874368 | tf_op jit(solution)/shard_map/all_gather | solution.py:62
  46.2 404.0 %reduce-scatter.3.cloned.1.call-start = ((), (), s32[]{:S(2)}) async-start(), calls=%async_computation.5 | async-start | bytes 4718592 | tf_op jit(solution)/shard_map/reduce_scatter | solution.py:113
  402.7 1.3 copy-start.6
  402.7 47.6 %copy-start.1 = (f32[2,1024,64]{1,2,0:T(8,128)S(1)}, f32[2,1024,64]{1,2,0:T(8,128)}, u32[]{:S(2)}) copy-start(f32[2,1024,64]{1,2,0:T(8,128)} %param.20) | copy-start | bytes 1572868
  402.7 47.5 %copy-start.2 = (f32[2,1024,64]{1,2,0:T(8,128)S(1)}, f32[2,1024,64]{1,2,0:T(8,128)}, u32[]{:S(2)}) copy-start(f32[2,1024,64]{1,2,0:T(8,128)} %param.22) | copy-start | bytes 1572868
  402.8 79.0 %reduce-scatter.5.cloned.1.call-start = ((), (), s32[]{:S(2)}) async-start(), calls=%async_computation.7 | async-start | bytes 589824 | tf_op jit(solution)/shard_map/reduce_scatter | solution.py:119
  403.9 77.8 %copy-start.5 = (f32[2,64,128]{2,1,0:T(8,128)S(1)}, f32[2,64,128]{2,1,0:T(8,128)}, u32[]{:S(2)}) copy-start(f32[2,64,128]{2,1,0:T(8,128)} %param.23) | copy-start | bytes 196612
  403.9 117.4 %all-gather.11.cloned.1.call-start = ((), (), s32[]{:S(2)}) async-start(), calls=%async_computation.6 | async-start | bytes 2621440 | tf_op jit(solution)/shard_map/all_gather | solution.py:132
Sparse Core Ops, SparseCore 0:
  9.9 36.3 all-gather.4
  48.4 29.0 all-gather.8
  79.1 147.8 all-gather.6
  402.8 47.3 reduce-scatter.2
  452.4 29.2 reduce-scatter.4
  484.2 37.0 all-gather.10
where the time goes:
time: 535 us; the launch traced here: 531 us
  waiting for transfers between devices  277 us (52%)
  matrix products  179 us (33%)
  local copies, waits for them, and re-layouts  31.4 us (6%)
  blocking collectives  22.1 us (4%)
  between operations  14.4 us (3%)
  other arithmetic  6.82 us (1%)
    all_gather x1, waiting for transfers between devices, per_device(): lax.all_gather(whole_columns, 'tok', axis=0, tiled=True)  136 us
    dot_general x16, matrix products, key_gradient(): jnp.einsum('tjd,sd->jts', grad_item, value_item, preferred_element_type=j...  56.3 us
    dot_general x16, matrix products, key_gradient(): jnp.einsum('jts,tjd->sd', dscores, query_item, preferred_element_type=jnp...  50.9 us
    sub x16, matrix products, key_gradient(): expo = jnp.exp(scores - row_max)  50.7 us
    reduce_scatter x1, waiting for transfers between devices, per_device(): lax.psum_scatter(jnp.einsum('td,ctr->dcr', columns, low_rank_gradient, pr...  46.3 us
    all_gather x1, waiting for transfers between devices, per_device(): lax.all_gather(locked_projection, 'chain', axis=1, tiled=True)  36.4 us
    reduce_scatter x1, waiting for transfers between devices, per_device(): lax.psum_scatter(right_term, 'tok', scatter_dimension=2, tiled=True)  28.7 us
    all_gather x1, waiting for transfers between devices, per_device(): lax.all_gather(shifted_first, 'chain', axis=0, tiled=True)  28.4 us
  transfers between devices with their start and end apart: 6, of which 5 were waited for; matrix products, arithmetic and copies ran while one was open for 7% of the time, Pallas kernels for 0%

commit v1 on v0

v1 whole, which is shorter than its diff:
```python
import math, functools
import jax, jax.numpy as jnp
from jax import lax
from jax.experimental import pallas as pl
from jax.experimental.pallas import tpu as pltpu
HD=128; RANK=64
LOG2E=1.4426950408889634
f32=jnp.float32; bf16=jnp.bfloat16
NT=(((1,),(1,)),((),()))
NN=(((1,),(0,)),((),()))
TN=(((0,),(0,)),((),()))

def dot(a,b,dims):
    return lax.dot_general(a,b,dims,preferred_element_type=f32)

def attention_kernel(scale, nchain, group, pair, pos_ref, q_ref, do_ref, v_ref, base_ref, lr_ref, b_ref, lg_ref, rt_ref, acc_ref):
    T = q_ref.shape[0]
    nb = T // 128
    ss = 1.0 / math.sqrt(HD)
    step = pl.program_id(0)

    @pl.when(step == 0)
    def _():
        acc_ref[...] = jnp.zeros_like(acc_ref)

    per_head = HD // b_ref.shape[2]
    b = jnp.concatenate([b_ref[pos_ref[1 + step * per_head + i]] for i in range(per_head)], axis=1)
    b = [b[c * RANK:(c + 1) * RANK] for c in range(nchain)]
    lr = [lr_ref[:, c * RANK:(c + 1) * RANK] for c in range(nchain)]
    keys = [(base_ref[0].astype(f32) + scale * dot(lr[c], b[c], NN)).astype(bf16) for c in range(nchain)]
    keys = [jnp.concatenate([x[j * 128:(j + 1) * 128] for x in keys], axis=0) for j in range(nb)]
    row = lax.broadcasted_iota(jnp.int32, (128, 128), 0)
    col = lax.broadcasted_iota(jnp.int32, (128, 128), 1)
    future = row > col
    v = v_ref[...]
    kg = [jnp.zeros((nchain * 128, HD), f32) for _ in range(nb)]
    for h0 in range(0, group, pair):
        def heads(ref, j):
            return jnp.concatenate([ref[j * 128:, (h0 + h) * HD:(h0 + h + 1) * HD] for h in range(pair)], axis=0)

        qs = [heads(q_ref, j) for j in range(nb)]
        dp = [dot(v[j * 128:(j + 1) * 128], heads(do_ref, j), NT) for j in range(nb)]
        s = [dot(keys[j], qs[j], NT) for j in range(nb)]
        ds = [[[None] * (pair * (nb - j)) for _ in range(nchain)] for j in range(nb)]
        for h in range(pair):
            for c in range(nchain):
                for i in range(nb):
                    def at(x, j, c):
                        k = h * (nb - j) + i - j
                        return x[j][c * 128:(c + 1) * 128, k * 128:(k + 1) * 128]

                    blocks = [at(s, j, c) for j in range(i + 1)]
                    blocks[i] = jnp.where(future, -1e30, blocks[i])
                    top = jnp.max(functools.reduce(jnp.maximum, blocks), axis=0, keepdims=True)
                    e = [jnp.exp2((x - top) * (ss * LOG2E)) for x in blocks]
                    d = [at(dp, j, 0) for j in range(i + 1)]
                    r = 1.0 / jnp.sum(functools.reduce(jnp.add, e), axis=0, keepdims=True)
                    center = r * jnp.sum(functools.reduce(jnp.add, [x * y for x, y in zip(e, d)]), axis=0, keepdims=True)
                    for j in range(i + 1):
                        ds[j][c][h * (nb - j) + i - j] = ((e[j] * r) * (d[j] - center)).astype(bf16)
        for j in range(nb):
            dsj = jnp.concatenate([jnp.concatenate(x, axis=1) for x in ds[j]], axis=0)
            kg[j] = kg[j] + dot(dsj, qs[j], NN)
    for c in range(nchain):
        g = (jnp.concatenate([x[c * 128:(c + 1) * 128] for x in kg], axis=0) * ss).astype(bf16)
        acc_ref[:, c * RANK:(c + 1) * RANK] += dot(g, b[c], NT)
        rt_ref[0, c] = scale * dot(lr[c], g, TN)

    @pl.when(step == pl.num_programs(0) - 1)
    def _():
        lg_ref[...] = (scale * acc_ref[...]).astype(lg_ref.dtype)


def attention(pos, q, do, v, base, lr, b, scale):
    T, KW = v.shape
    nchain = lr.shape[1] // RANK
    KH, group = KW // HD, q.shape[1] // KW
    hp = base.shape[2] // HD
    grid = pltpu.PrefetchScalarGridSpec(
        num_scalar_prefetch=1, grid=(KH,),
        in_specs=[
            pl.BlockSpec((T, group * HD), lambda g, p: (0, g)),
            pl.BlockSpec((T, group * HD), lambda g, p: (0, g)),
            pl.BlockSpec((T, HD), lambda g, p: (0, g)),
            pl.BlockSpec((1, T, HD), lambda g, p: (p[0] ^ (g // hp), 0, g % hp)),
            pl.BlockSpec(lr.shape, lambda g, p: (0, 0)),
            pl.BlockSpec(b.shape, lambda g, p: (0, 0, 0)),
        ],
        out_specs=[
            pl.BlockSpec(lr.shape, lambda g, p: (0, 0)),
            pl.BlockSpec((1, nchain, RANK, HD), lambda g, p: (g, 0, 0, 0)),
        ],
        scratch_shapes=[pltpu.VMEM(lr.shape, f32)],
    )
    return pl.pallas_call(
        functools.partial(attention_kernel, scale, nchain, group, 4), grid_spec=grid,
        out_shape=[jax.ShapeDtypeStruct(lr.shape, bf16), jax.ShapeDtypeStruct((KH, nchain, RANK, HD), f32)],
        compiler_params=pltpu.CompilerParams(vmem_limit_bytes=28 * 1024 * 1024),
        cost_estimate=pl.CostEstimate(flops=10_000_000_000, bytes_accessed=20_000_000, transcendentals=T * T * 64 * nchain),
        name="attention",
    )(pos, q, do, v, base, lr, b)


from jax.sharding import PartitionSpec as P

STRIDE_LENGTH = 0.2


def gradient_kernel(own, nrank, pos_ref, x_ref, lg_ref, rt_ref, out_ref):
    g = dot(lg_ref[...], x_ref[...], TN)
    for c in range(nrank // RANK):
        out_ref[0, c] = jnp.concatenate([g[c * RANK:(c + 1) * RANK], rt_ref[0, c]], axis=1).astype(out_ref.dtype)


def gradients(pos, x, lg, rt, n, dtype):
    T, width = x.shape
    nrank = lg.shape[1]
    shards = 2 * n
    heads, nchain, _, kcols = rt.shape
    cols, kcols = width // shards, heads * kcols // shards
    if heads != shards:
        rt = rt.reshape(heads, nchain, RANK, -1, kcols).transpose(0, 3, 1, 2, 4).reshape(shards, nchain, RANK, kcols)
    grid = pltpu.PrefetchScalarGridSpec(
        num_scalar_prefetch=1, grid=(n,),
        in_specs=[
            pl.BlockSpec((T, cols), lambda i, p: (0, p[i])),
            pl.BlockSpec((T, nrank), lambda i, p: (0, 0)),
            pl.BlockSpec((1, nchain, RANK, kcols), lambda i, p: (p[i], 0, 0, 0)),
        ],
        out_specs=pl.BlockSpec((1, nchain, RANK, cols + kcols), lambda i, p: (i, 0, 0, 0)),
    )
    return pl.pallas_call(
        functools.partial(gradient_kernel, n, nrank), grid_spec=grid,
        out_shape=jax.ShapeDtypeStruct((n, nchain, RANK, cols + kcols), dtype),
        compiler_params=pltpu.CompilerParams(vmem_limit_bytes=24 * 1024 * 1024),
        cost_estimate=pl.CostEstimate(flops=T * width * nrank, bytes_accessed=3_000_000, transcendentals=0),
        name="gradients",
    )(pos, x, lg, rt)


def reorder_kernel(pos_ref, x_ref, out_ref):
    out_ref[...] = x_ref[...]


def reorder(pos, x, cols):
    T, width = x.shape
    grid = pltpu.PrefetchScalarGridSpec(
        num_scalar_prefetch=1, grid=(width // cols,),
        in_specs=[pl.BlockSpec((T, cols), lambda i, p: (0, p[i]))],
        out_specs=pl.BlockSpec((T, cols), lambda i, p: (0, i)),
    )
    return pl.pallas_call(
        reorder_kernel, grid_spec=grid, out_shape=jax.ShapeDtypeStruct(x.shape, x.dtype),
        compiler_params=pltpu.CompilerParams(vmem_limit_bytes=8 * 1024 * 1024),
        cost_estimate=pl.CostEstimate(flops=0, bytes_accessed=4 * T * width, transcendentals=0), name="reorder",
    )(pos, x)


def per_device(layer_activations, rotated_probes, attended_contents, attended_slope, locked_projection,
               first_multipliers, second_multipliers, first_jitter, second_jitter, chain_heats, donor_chain):
    T, width = layer_activations.shape
    scale = 1.0 / math.sqrt(width * RANK)
    nchain, arows, _ = first_multipliers.shape
    nc = lax.axis_size("chain")
    nt = lax.axis_size("tok")
    nz = nt // 2
    p = lax.axis_index("chain")
    t = lax.axis_index("tok")
    z, core = t // 2, t % 2

    def shift(x, k):
        return lax.ppermute(x, "tok", [(i, (i + 2 * k) % nt) for i in range(nt)])

    def swap_cores(x):
        return lax.ppermute(x, "tok", [(i, i ^ 1) for i in range(nt)])

    def exchange(x, k):
        return lax.ppermute(x, "chain", [(i, i ^ k) for i in range(nc)])

    source = lax.dynamic_slice_in_dim(donor_chain, p * nchain, nchain)

    def take_slots(own):
        every = jnp.concatenate([own] + [exchange(own, k) for k in range(1, nc)])
        return jnp.concatenate([
            lax.dynamic_slice_in_dim(every, (source[j] // nchain ^ p) * nchain + source[j] % nchain, 1)
            for j in range(nchain)
        ])

    heat = jnp.sqrt(2.0 * STRIDE_LENGTH * chain_heats)[:, None, None]
    first = first_multipliers.transpose(0, 2, 1)
    pre_a = (1.0 - STRIDE_LENGTH) * first + heat * first_jitter.transpose(0, 2, 1)
    pre_b = (1.0 - STRIDE_LENGTH) * second_multipliers + heat * second_jitter
    kcols = second_multipliers.shape[2]

    half = arows // 2
    order = []
    for s in range(nz):
        for c in (core, 1 - core):
            order += [((z - s) % nz * 2 + c) * 2, ((z + s) % nz * 2 + c) * 2 + 1]
    x_ordered = reorder(jnp.stack(order).astype(jnp.int32), layer_activations, half)

    def both_cores(pieces, axis):
        here = jnp.concatenate(pieces, axis=axis)
        return jnp.concatenate([here, swap_cores(here)], axis=axis)

    def x_piece(s):
        return x_ordered[:, s * 2 * arows:(s + 1) * 2 * arows]

    w = (locked_projection[:half], locked_projection[half:])
    a = None
    plain = low_rank = 0.0
    b_low = []
    for s in range(nz + 1):
        if s < nz:
            plain = plain + jnp.dot(x_piece(s), both_cores(w, 0), preferred_element_type=f32)
        if a is not None:
            here = jnp.concatenate([a[0], a[1]], axis=1)
            there = swap_cores(here)
            parts = [here[:, :half], here[:, half + kcols:], there[:, :half], there[:, half + kcols:]]
            low_rank = low_rank + dot(x_piece(s - 1), jnp.concatenate(parts, axis=1), NT)
            b_low += [here[:, half:half + kcols], there[:, half:half + kcols]]
        if s < nz - 1:
            w = (shift(w[0], 1), shift(w[1], -1))
        if s == 0:
            ab = take_slots(jnp.concatenate([first[:, :, :half], second_multipliers, first[:, :, half:]], axis=2).astype(bf16))
            w, ab = lax.optimization_barrier((w, ab))
            ab = ab.reshape(nchain * RANK, arows + kcols)
            a = (ab[:, :half + kcols], ab[:, half + kcols:])
        elif s < nz:
            a = (shift(a[0], 1), shift(a[1], -1))
    plain = plain.astype(bf16)
    low_rank = low_rank.astype(bf16)
    base = jnp.stack([plain] + [exchange(plain, k) for k in range(1, nc)])
    shards = jnp.arange(nt, dtype=jnp.int32)
    places = (z - shards // 2) % nz * 2 + (shards % 2 != core).astype(jnp.int32)
    pos = jnp.concatenate([p[None], places]).astype(jnp.int32)
    rest = take_slots(jnp.concatenate([pre_a, pre_b], axis=2).astype(bf16))
    base, rest = lax.optimization_barrier((base, rest))

    low_grad, right = attention(pos, rotated_probes, attended_slope, attended_contents, base, low_rank, jnp.stack(b_low), scale)

    around = (z + jnp.arange(nz, dtype=jnp.int32)) % nz
    theirs = swap_cores(gradients(around * 2 + 1 - core, layer_activations, low_grad, right, nz, bf16))
    mine = gradients(around * 2 + core, layer_activations, low_grad, right, nz, f32)
    total = mine[0] + theirs[0]
    send = (mine[1:] + theirs[1:]).astype(bf16)
    for k in range(1, nz):
        total = total + shift(send[k - 1], k).astype(f32)
    new = rest.astype(f32) - STRIDE_LENGTH * total
    return new[:, :, :arows].transpose(0, 2, 1), new[:, :, arows:]


def solution(mesh):
    return jax.shard_map(
        per_device,
        mesh=mesh,
        in_specs=(
            P("tok", None), P("tok", None), P("tok", None), P("tok", None), P("tok", "chain"),
            P("chain", "tok", None), P("chain", None, "tok"), P("chain", "tok", None), P("chain", None, "tok"),
            P("chain"), P(),
        ),
        out_specs=(P("chain", "tok", None), P("chain", None, "tok")),
        check_vma=False,
    )
```

time: 535 us -> 152 us (0.28)
  waiting for transfers between devices: 277 us -> 75.4 us
  matrix products: 179 us -> 3.55 us
  starting transfers between devices: 0.24 us -> 31.7 us
  local copies, waits for them, and re-layouts: 31.4 us -> 6.08 us
  Pallas kernels: 0 us -> 23.9 us
  blocking collectives: 22.1 us -> 0 us
  between operations: 14.4 us -> 6.39 us
    all_gather x4 -> x0, waiting for transfers between devices: 201 us -> none  [the longest x1 136 us: per_device(): lax.all_gather(whole_columns, 'tok', axis=0, tiled=True)]
    dot_general x37 -> x8, matrix products: 129 us -> 3.55 us  [the longest x4 1.81 us: per_device(): jnp.dot(x_piece(s), both_cores(w, 0), preferred_element_type=f32)]
    ppermute x0 -> x33, waiting for transfers between devices: none -> 75.4 us  [the longest x15 58.3 us: shift(): return lax.ppermute(x, 'tok', [(i, (i + 2 * k) % nt) for i in range(nt)])]
    reduce_scatter x2 -> x0, waiting for transfers between devices: 75 us -> none  [the longest x1 46.3 us: per_device(): lax.psum_scatter(jnp.einsum('td,ctr->dcr', columns, low_rank_gradient, pr...]
    sub x16 -> x0, matrix products: 50.7 us -> none  [key_gradient(): expo = jnp.exp(scores - row_max)]
    ppermute x0 -> x33, starting transfers between devices: none -> 31.7 us  [the longest x15 19.7 us: shift(): return lax.ppermute(x, 'tok', [(i, (i + 2 * k) % nt) for i in range(nt)])]
    pallas_call x0 -> x4, Pallas kernels: none -> 23.9 us  [the longest x1 18.7 us: attention(): pl.pallas_call(functools.partial(attention_kernel, scale, nchain, group,...]
    all_gather x2 -> x0, blocking collectives: 22.1 us -> none  [the longest x1 13.2 us: per_device(): lax.all_gather(second_multipliers.astype(jnp.bfloat16), 'tok', axis=2, ti...]
  transfers between devices with their start and end apart: 6 -> 33, of which waited for: 5 -> 15; matrix products, arithmetic and copies ran while one was open for 7% -> 4% of each run, Pallas kernels for 0% -> 2%
where the time goes in v1:
time: 152 us; the launch traced here: 151 us
  waiting for transfers between devices  75.4 us (50%)
  starting transfers between devices  31.7 us (21%)
  Pallas kernels  23.9 us (16%)
  between operations  6.39 us (4%)
  local copies, waits for them, and re-layouts  6.08 us (4%)
  other arithmetic  4.39 us (3%)
  matrix products  3.55 us (2%)
    ppermute x15, waiting for transfers between devices, shift(): return lax.ppermute(x, 'tok', [(i, (i + 2 * k) % nt) for i in range(nt)])  58.3 us
    ppermute x15, starting transfers between devices, shift(): return lax.ppermute(x, 'tok', [(i, (i + 2 * k) % nt) for i in range(nt)])  19.7 us
    pallas_call x1, Pallas kernels, attention(): pl.pallas_call(functools.partial(attention_kernel, scale, nchain, group,...  18.7 us
    ppermute x9, waiting for transfers between devices, exchange(): return lax.ppermute(x, 'chain', [(i, i ^ k) for i in range(nc)])  14.8 us
    ppermute x9, starting transfers between devices, exchange(): return lax.ppermute(x, 'chain', [(i, i ^ k) for i in range(nc)])  10.7 us
    pallas_call x2, Pallas kernels, gradients(): pl.pallas_call(functools.partial(gradient_kernel, n, nrank), grid_spec=gr...  3.54 us
  transfers between devices with their start and end apart: 33, of which 15 were waited for; matrix products, arithmetic and copies ran while one was open for 4% of the time, Pallas kernels for 2%

profile of v1, /device:TPU:8, one launch (start us, length us, event | category | flops | bytes accessed | tf_op | source)
XLA Modules:
  0.0 151.5 jit_solution(6178921441889659335)
XLA Ops:
  7.5 1.6 %collective-permute-start.16 = (bf16[2,64,1152]{2,1,0:T(8,128)(2,1)S(1)}, bf16[2,64,1152]{2,1,0:T(8,128)(2,1)S(1)}, u32[]{:S(2)}, u32[]{:S(2)}) collective-permute-start(bf16[2,64,1152]{2,1,0:T(8,128)(2,1)S(1)} %pad_maximum_fusion.8), channel_id=1, source_target_pairs={{0,8},{8,0},{16,24},{24,16},{1,9},{9,1},{17,25},{25,17},{2,10},{10... | collective-permute-start | bytes 884744 | tf_op jit(solution)/shard_map/ppermute | solution.py:178
  18.0 2.2 %copy-done = bf16[256,8192]{1,0:T(8,128)(2,1)S(1)} copy-done((bf16[256,8192]{1,0:T(8,128)(2,1)S(1)}, bf16[256,8192]{1,0:T(8,128)(2,1)}, u32[]{:S(2)}) %copy-start) | copy-done | bytes 4194328
  20.2 1.7 %reorder.1 = bf16[256,8192]{1,0:T(8,128)(2,1)S(1)} custom-call(s32[16]{0:T(128)S(1)} %stack.109.pos_ref, bf16[256,8192]{1,0:T(8,128)(2,1)S(1)} %copy-done), custom_call_target="tpu_custom_call" | custom-call | bytes 8388608 | tf_op jit(solution)/shard_map/reorder/pallas_call | solution.py:152
  22.0 1.6 %collective-permute-start.1 = (bf16[512,256]{1,0:T(8,128)(2,1)S(1)}, bf16[512,256]{1,0:T(8,128)(2,1)S(1)}, u32[]{:S(2)}, u32[]{:S(2)}) collective-permute-start(bf16[512,256]{1,0:T(8,128)(2,1)S(1)} %copy-done.8), channel_id=1, source_target_pairs={{0,2},{1,3},{2,4},{3,5},{4,6},{5,7},{6,0},{7,1},{8,10},{9,11},{10,... | collective-permute-start | bytes 786440 | tf_op jit(solution)/shard_map/ppermute | solution.py:172
  24.2 2.4 %collective-permute-done.16 = bf16[2,64,1152]{2,1,0:T(8,128)(2,1)S(1)} collective-permute-done((bf16[2,64,1152]{2,1,0:T(8,128)(2,1)S(1)}, bf16[2,64,1152]{2,1,0:T(8,128)(2,1)S(1)}, u32[]{:S(2)}, u32[]{:S(2)}) %collective-permute-start.16) | collective-permute-done | bytes 294944 | tf_op jit(solution)/shard_map/ppermute | solution.py:178
  26.6 6.3 %collective-permute-done.17 = bf16[2,64,1152]{2,1,0:T(8,128)(2,1)S(1)} collective-permute-done((bf16[2,64,1152]{2,1,0:T(8,128)(2,1)S(1)}, bf16[2,64,1152]{2,1,0:T(8,128)(2,1)S(1)}, u32[]{:S(2)}, u32[]{:S(2)}) %collective-permute-start.17) | collective-permute-done | bytes 294944 | tf_op jit(solution)/shard_map/ppermute | solution.py:178
  33.2 1.7 %collective-permute-done.2 = bf16[512,256]{1,0:T(8,128)(2,1)S(1)} collective-permute-done((bf16[512,256]{1,0:T(8,128)(2,1)S(1)}, bf16[512,256]{1,0:T(8,128)(2,1)S(1)}, u32[]{:S(2)}, u32[]{:S(2)}) %collective-permute-start.2) | collective-permute-done | bytes 262176 | tf_op jit(solution)/shard_map/ppermute | solution.py:172
  37.7 2.0 %collective-permute-start.8 = (bf16[512,256]{1,0:T(8,128)(2,1)S(1)}, bf16[512,256]{1,0:T(8,128)(2,1)S(1)}, u32[]{:S(2)}, u32[]{:S(2)}) collective-permute-start(bf16[512,256]{1,0:T(8,128)(2,1)S(1)} %collective-permute-done.2), channel_id=1, source_target_pairs={{0,6},{1,7},{2,0},{3,1},{4,2},{5,3},{6,4},{7,5},{8,14},{9,15},{10,... | collective-permute-start | bytes 786440 | tf_op jit(solution)/shard_map/ppermute | solution.py:172
  39.8 6.0 %collective-permute-done.21 = bf16[128,512]{1,0:T(8,128)(2,1)S(1)} collective-permute-done((bf16[128,512]{1,0:T(8,128)(2,1)S(1)}, bf16[128,512]{1,0:T(8,128)(2,1)S(1)}, u32[]{:S(2)}, u32[]{:S(2)}) %collective-permute-start.21) | collective-permute-done | bytes 131104 | tf_op jit(solution)/shard_map/ppermute | solution.py:172
  47.0 3.5 %collective-permute-done.7 = bf16[512,256]{1,0:T(8,128)(2,1)S(1)} collective-permute-done((bf16[512,256]{1,0:T(8,128)(2,1)S(1)}, bf16[512,256]{1,0:T(8,128)(2,1)S(1)}, u32[]{:S(2)}, u32[]{:S(2)}) %collective-permute-start.7) | collective-permute-done | bytes 262176 | tf_op jit(solution)/shard_map/ppermute | solution.py:172
  50.4 6.3 %collective-permute-done.8 = bf16[512,256]{1,0:T(8,128)(2,1)S(1)} collective-permute-done((bf16[512,256]{1,0:T(8,128)(2,1)S(1)}, bf16[512,256]{1,0:T(8,128)(2,1)S(1)}, u32[]{:S(2)}, u32[]{:S(2)}) %collective-permute-start.8) | collective-permute-done | bytes 262176 | tf_op jit(solution)/shard_map/ppermute | solution.py:172
  60.2 3.7 %collective-permute-done.23 = bf16[128,640]{1,0:T(8,128)(2,1)S(1)} collective-permute-done((bf16[128,640]{1,0:T(8,128)(2,1)S(1)}, bf16[128,640]{1,0:T(8,128)(2,1)S(1)}, u32[]{:S(2)}, u32[]{:S(2)}) %collective-permute-start.23) | collective-permute-done | bytes 163872 | tf_op jit(solution)/shard_map/ppermute | solution.py:172
  63.9 3.2 %collective-permute-start.27 = (bf16[128,512]{1,0:T(8,128)(2,1)S(1)}, bf16[128,512]{1,0:T(8,128)(2,1)S(1)}, u32[]{:S(2)}, u32[]{:S(2)}) collective-permute-start(bf16[128,512]{1,0:T(8,128)(2,1)S(1)} %collective-permute-done.24), channel_id=1, source_target_pairs={{0,6},{1,7},{2,0},{3,1},{4,2},{5,3},{6,4},{7,5},{8,14},{9,15},{10,... | collective-permute-start | bytes 393224 | tf_op jit(solution)/shard_map/ppermute | solution.py:172
  67.8 11.8 %collective-permute-done.26 = bf16[128,640]{1,0:T(8,128)(2,1)S(1)} collective-permute-done((bf16[128,640]{1,0:T(8,128)(2,1)S(1)}, bf16[128,640]{1,0:T(8,128)(2,1)S(1)}, u32[]{:S(2)}, u32[]{:S(2)}) %collective-permute-start.26) | collective-permute-done | bytes 163872 | tf_op jit(solution)/shard_map/ppermute | solution.py:172
  89.5 2.4 %collective-permute-done.13 = bf16[256,256]{1,0:T(8,128)(2,1)S(1)} collective-permute-done((bf16[256,256]{1,0:T(8,128)(2,1)S(1)}, bf16[256,256]{1,0:T(8,128)(2,1)S(1)}, u32[]{:S(2)}, u32[]{:S(2)}) %collective-permute-start.13) | collective-permute-done | bytes 131104 | tf_op jit(solution)/shard_map/ppermute | solution.py:178
  91.9 3.7 %collective-permute-done.14 = bf16[256,256]{1,0:T(8,128)(2,1)S(1)} collective-permute-done((bf16[256,256]{1,0:T(8,128)(2,1)S(1)}, bf16[256,256]{1,0:T(8,128)(2,1)S(1)}, u32[]{:S(2)}, u32[]{:S(2)}) %collective-permute-start.14) | collective-permute-done | bytes 131104 | tf_op jit(solution)/shard_map/ppermute | solution.py:178
  95.7 18.7 %attention.1 = (bf16[256,128]{1,0:T(8,128)(2,1)S(1)}, f32[8,2,64,128]{3,2,1,0:T(8,128)S(1)}) custom-call(s32[9]{0:T(128)S(1)} %pad_add_fusion.pos_ref, bf16[256,8192]{1,0:T(8,128)(2,1)S(1)} %copy-done.2, bf16[256,8192]{1,0:T(8,128)(2,1)S(1)} %copy-done.3, bf16[256,1024]{1,0:T(8,128)(2,1)S(1)} %copy-done.4, ...), custom_call_target="tpu_custom_call" | custom-call | flops 10000000000 | bytes 20000000 | tf_op jit(solution)/shard_map/attention/pallas_call | solution.py:95
  114.4 1.8 %gradients.3 = bf16[4,2,64,1152]{3,2,1,0:T(8,128)(2,1)S(1)} custom-call(s32[4]{0:T(128)S(1)} %add_subtract_fusion.pos_ref, bf16[256,8192]{1,0:T(8,128)(2,1)S(1)} %copy-done.1, bf16[256,128]{1,0:T(8,128)(2,1)S(1)} %get-tuple-element.14.lg_ref, f32[8,2,64,128]{3,2,1,0:T(8,128)S(1)} %get-tuple-element.15.rt_ref), custom_call_target="tpu_custom_call" | custom-call | flops 268435456 | bytes 3000000 | tf_op jit(solution)/shard_map/gradients/pallas_call | solution.py:132
  116.3 1.8 %gradients.2 = f32[4,2,64,1152]{3,2,1,0:T(8,128)S(1)} custom-call(s32[4]{0:T(128)S(1)} %broadcast_add_fusion.pos_ref, bf16[256,8192]{1,0:T(8,128)(2,1)S(1)} %copy-done.1, bf16[256,128]{1,0:T(8,128)(2,1)S(1)} %get-tuple-element.14.lg_ref, f32[8,2,64,128]{3,2,1,0:T(8,128)S(1)} %get-tuple-element.15.rt_ref), custom_call_target="tpu_custom_call" | custom-call | flops 268435456 | bytes 3000000 | tf_op jit(solution)/shard_map/gradients/pallas_call | solution.py:132
  119.4 1.6 %collective-permute-start.30 = (bf16[2,64,1152]{2,1,0:T(8,128)(2,1)S(1)}, bf16[2,64,1152]{2,1,0:T(8,128)(2,1)S(1)}, u32[]{:S(2)}, u32[]{:S(2)}) collective-permute-start(bf16[2,64,1152]{2,1,0:T(8,128)(2,1)S(1)} %get-tuple-element.20), channel_id=1, source_target_pairs={{0,2},{1,3},{2,4},{3,5},{4,6},{5,7},{6,0},{7,1},{8,10},{9,11},{10,... | collective-permute-start | bytes 884744 | tf_op jit(solution)/shard_map/ppermute | solution.py:172
  121.0 3.6 %collective-permute-start.31 = (bf16[2,64,1152]{2,1,0:T(8,128)(2,1)S(1)}, bf16[2,64,1152]{2,1,0:T(8,128)(2,1)S(1)}, u32[]{:S(2)}, u32[]{:S(2)}) collective-permute-start(bf16[2,64,1152]{2,1,0:T(8,128)(2,1)S(1)} %get-tuple-element.22), channel_id=1, source_target_pairs={{0,4},{1,5},{2,6},{3,7},{4,0},{5,1},{6,2},{7,3},{8,12},{9,13},{10,... | collective-permute-start | bytes 884744 | tf_op jit(solution)/shard_map/ppermute | solution.py:172
  124.5 5.4 %collective-permute-done.30 = bf16[2,64,1152]{2,1,0:T(8,128)(2,1)S(1)} collective-permute-done((bf16[2,64,1152]{2,1,0:T(8,128)(2,1)S(1)}, bf16[2,64,1152]{2,1,0:T(8,128)(2,1)S(1)}, u32[]{:S(2)}, u32[]{:S(2)}) %collective-permute-start.30) | collective-permute-done | bytes 294944 | tf_op jit(solution)/shard_map/ppermute | solution.py:172
  130.0 16.5 %collective-permute-done.31 = bf16[2,64,1152]{2,1,0:T(8,128)(2,1)S(1)} collective-permute-done((bf16[2,64,1152]{2,1,0:T(8,128)(2,1)S(1)}, bf16[2,64,1152]{2,1,0:T(8,128)(2,1)S(1)}, u32[]{:S(2)}, u32[]{:S(2)}) %collective-permute-start.31) | collective-permute-done | bytes 294944 | tf_op jit(solution)/shard_map/ppermute | solution.py:172
  146.5 3.2 %collective-permute-done.32 = bf16[2,64,1152]{2,1,0:T(8,128)(2,1)S(1)} collective-permute-done((bf16[2,64,1152]{2,1,0:T(8,128)(2,1)S(1)}, bf16[2,64,1152]{2,1,0:T(8,128)(2,1)S(1)}, u32[]{:S(2)}, u32[]{:S(2)}) %collective-permute-start.32) | collective-permute-done | bytes 294944 | tf_op jit(solution)/shard_map/ppermute | solution.py:172
  (123 shorter events, 32.4 us)
Async XLA Ops:
  3.9 13.5 %collective-permute-start.3 = (bf16[2,64,1152]{2,1,0:T(8,128)(2,1)S(1)}, bf16[2,64,1152]{2,1,0:T(8,128)(2,1)S(1)}, u32[]{:S(2)}, u32[]{:S(2)}) collective-permute-start(bf16[2,64,1152]{2,1,0:T(8,128)(2,1)S(1)} %pad_maximum_fusion.6), channel_id=1, source_target_pairs={{0,8},{8,0},{16,24},{24,16},{1,9},{9,1},{17,25},{25,17},{2,10},{10... | collective-permute-start | bytes 884744 | tf_op jit(solution)/shard_map/ppermute | solution.py:178
  5.5 16.5 %collective-permute-start.4 = (bf16[2,64,1152]{2,1,0:T(8,128)(2,1)S(1)}, bf16[2,64,1152]{2,1,0:T(8,128)(2,1)S(1)}, u32[]{:S(2)}, u32[]{:S(2)}) collective-permute-start(bf16[2,64,1152]{2,1,0:T(8,128)(2,1)S(1)} %pad_maximum_fusion.6), channel_id=1, source_target_pairs={{0,16},{8,24},{16,0},{24,8},{1,17},{9,25},{17,1},{25,9},{2,18},{10... | collective-permute-start | bytes 884744 | tf_op jit(solution)/shard_map/ppermute | solution.py:178
  7.0 16.6 %collective-permute-start.5 = (bf16[2,64,1152]{2,1,0:T(8,128)(2,1)S(1)}, bf16[2,64,1152]{2,1,0:T(8,128)(2,1)S(1)}, u32[]{:S(2)}, u32[]{:S(2)}) collective-permute-start(bf16[2,64,1152]{2,1,0:T(8,128)(2,1)S(1)} %pad_maximum_fusion.6), channel_id=1, source_target_pairs={{0,24},{8,16},{16,8},{24,0},{1,25},{9,17},{17,9},{25,1},{2,26},{10... | collective-permute-start | bytes 884744 | tf_op jit(solution)/shard_map/ppermute | solution.py:178
  7.5 19.1 %collective-permute-start.16 = (bf16[2,64,1152]{2,1,0:T(8,128)(2,1)S(1)}, bf16[2,64,1152]{2,1,0:T(8,128)(2,1)S(1)}, u32[]{:S(2)}, u32[]{:S(2)}) collective-permute-start(bf16[2,64,1152]{2,1,0:T(8,128)(2,1)S(1)} %pad_maximum_fusion.8), channel_id=1, source_target_pairs={{0,8},{8,0},{16,24},{24,16},{1,9},{9,1},{17,25},{25,17},{2,10},{10... | collective-permute-start | bytes 884744 | tf_op jit(solution)/shard_map/ppermute | solution.py:178
  9.1 23.8 %collective-permute-start.17 = (bf16[2,64,1152]{2,1,0:T(8,128)(2,1)S(1)}, bf16[2,64,1152]{2,1,0:T(8,128)(2,1)S(1)}, u32[]{:S(2)}, u32[]{:S(2)}) collective-permute-start(bf16[2,64,1152]{2,1,0:T(8,128)(2,1)S(1)} %pad_maximum_fusion.8), channel_id=1, source_target_pairs={{0,16},{8,24},{16,0},{24,8},{1,17},{9,25},{17,1},{25,9},{2,18},{10... | collective-permute-start | bytes 884744 | tf_op jit(solution)/shard_map/ppermute | solution.py:178
  17.4 15.5 %collective-permute-start.18 = (bf16[2,64,1152]{2,1,0:T(8,128)(2,1)S(1)}, bf16[2,64,1152]{2,1,0:T(8,128)(2,1)S(1)}, u32[]{:S(2)}, u32[]{:S(2)}) collective-permute-start(bf16[2,64,1152]{2,1,0:T(8,128)(2,1)S(1)} %pad_maximum_fusion.8), channel_id=1, source_target_pairs={{0,24},{8,16},{16,8},{24,0},{1,25},{9,17},{17,9},{25,1},{2,26},{10... | collective-permute-start | bytes 884744 | tf_op jit(solution)/shard_map/ppermute | solution.py:178
  22.0 11.2 %collective-permute-start.1 = (bf16[512,256]{1,0:T(8,128)(2,1)S(1)}, bf16[512,256]{1,0:T(8,128)(2,1)S(1)}, u32[]{:S(2)}, u32[]{:S(2)}) collective-permute-start(bf16[512,256]{1,0:T(8,128)(2,1)S(1)} %copy-done.8), channel_id=1, source_target_pairs={{0,2},{1,3},{2,4},{3,5},{4,6},{5,7},{6,0},{7,1},{8,10},{9,11},{10,... | collective-permute-start | bytes 786440 | tf_op jit(solution)/shard_map/ppermute | solution.py:172
  23.6 11.2 %collective-permute-start.2 = (bf16[512,256]{1,0:T(8,128)(2,1)S(1)}, bf16[512,256]{1,0:T(8,128)(2,1)S(1)}, u32[]{:S(2)}, u32[]{:S(2)}) collective-permute-start(bf16[512,256]{1,0:T(8,128)(2,1)S(1)} %copy-done.7), channel_id=1, source_target_pairs={{0,6},{1,7},{2,0},{3,1},{4,2},{5,3},{6,4},{7,5},{8,14},{9,15},{10,... | collective-permute-start | bytes 786440 | tf_op jit(solution)/shard_map/ppermute | solution.py:172
  34.9 23.1 %collective-permute-start.19 = (bf16[128,1152]{1,0:T(8,128)(2,1)S(1)}, bf16[128,1152]{1,0:T(8,128)(2,1)S(1)}, u32[]{:S(2)}, u32[]{:S(2)}) collective-permute-start(bf16[128,1152]{1,0:T(8,128)(2,1)S(1)} %bitcast.80), channel_id=1, source_target_pairs={{0,1},{1,0},{2,3},{3,2},{4,5},{5,4},{6,7},{7,6},{8,9},{9,8},{10,11... | collective-permute-start | bytes 884744 | tf_op jit(solution)/shard_map/ppermute | solution.py:175
  34.9 10.9 %collective-permute-start.20 = (bf16[128,640]{1,0:T(8,128)(2,1)S(1)}, bf16[128,640]{1,0:T(8,128)(2,1)S(1)}, u32[]{:S(2)}, u32[]{:S(2)}) collective-permute-start(bf16[128,640]{1,0:T(8,128)(2,1)S(1)} %slice.191), channel_id=1, source_target_pairs={{0,2},{1,3},{2,4},{3,5},{4,6},{5,7},{6,0},{7,1},{8,10},{9,11},{10,... | collective-permute-start | bytes 491528 | tf_op jit(solution)/shard_map/ppermute | solution.py:172
  35.7 10.1 %collective-permute-start.21 = (bf16[128,512]{1,0:T(8,128)(2,1)S(1)}, bf16[128,512]{1,0:T(8,128)(2,1)S(1)}, u32[]{:S(2)}, u32[]{:S(2)}) collective-permute-start(bf16[128,512]{1,0:T(8,128)(2,1)S(1)} %get-tuple-element.28), channel_id=1, source_target_pairs={{0,6},{1,7},{2,0},{3,1},{4,2},{5,3},{6,4},{7,5},{8,14},{9,15},{10,... | collective-permute-start | bytes 393224 | tf_op jit(solution)/shard_map/ppermute | solution.py:172
  37.0 13.4 %collective-permute-start.7 = (bf16[512,256]{1,0:T(8,128)(2,1)S(1)}, bf16[512,256]{1,0:T(8,128)(2,1)S(1)}, u32[]{:S(2)}, u32[]{:S(2)}) collective-permute-start(bf16[512,256]{1,0:T(8,128)(2,1)S(1)} %collective-permute-done.1), channel_id=1, source_target_pairs={{0,2},{1,3},{2,4},{3,5},{4,6},{5,7},{6,0},{7,1},{8,10},{9,11},{10,... | collective-permute-start | bytes 786440 | tf_op jit(solution)/shard_map/ppermute | solution.py:172
  37.7 19.1 %collective-permute-start.8 = (bf16[512,256]{1,0:T(8,128)(2,1)S(1)}, bf16[512,256]{1,0:T(8,128)(2,1)S(1)}, u32[]{:S(2)}, u32[]{:S(2)}) collective-permute-start(bf16[512,256]{1,0:T(8,128)(2,1)S(1)} %collective-permute-done.2), channel_id=1, source_target_pairs={{0,6},{1,7},{2,0},{3,1},{4,2},{5,3},{6,4},{7,5},{8,14},{9,15},{10,... | collective-permute-start | bytes 786440 | tf_op jit(solution)/shard_map/ppermute | solution.py:172
  45.8 35.0 %collective-permute-start.6 = (bf16[1024,256]{1,0:T(8,128)(2,1)S(1)}, bf16[1024,256]{1,0:T(8,128)(2,1)S(1)}, u32[]{:S(2)}, u32[]{:S(2)}) collective-permute-start(bf16[1024,256]{1,0:T(8,128)(2,1)S(1)} %pad_maximum_fusion.2), channel_id=1, source_target_pairs={{0,1},{1,0},{2,3},{3,2},{4,5},{5,4},{6,7},{7,6},{8,9},{9,8},{10,11... | collective-permute-start | bytes 1572872 | tf_op jit(solution)/shard_map/ppermute | solution.py:175
  45.8 13.3 %collective-permute-start.24 = (bf16[128,512]{1,0:T(8,128)(2,1)S(1)}, bf16[128,512]{1,0:T(8,128)(2,1)S(1)}, u32[]{:S(2)}, u32[]{:S(2)}) collective-permute-start(bf16[128,512]{1,0:T(8,128)(2,1)S(1)} %collective-permute-done.21), channel_id=1, source_target_pairs={{0,6},{1,7},{2,0},{3,1},{4,2},{5,3},{6,4},{7,5},{8,14},{9,15},{10,... | collective-permute-start | bytes 393224 | tf_op jit(solution)/shard_map/ppermute | solution.py:172
  50.4 16.8 %collective-permute-start.22 = (bf16[128,1152]{1,0:T(8,128)(2,1)S(1)}, bf16[128,1152]{1,0:T(8,128)(2,1)S(1)}, u32[]{:S(2)}, u32[]{:S(2)}) collective-permute-start(bf16[128,1152]{1,0:T(8,128)(2,1)S(1)} %pad_maximum_fusion.10), channel_id=1, source_target_pairs={{0,1},{1,0},{2,3},{3,2},{4,5},{5,4},{6,7},{7,6},{8,9},{9,8},{10,11... | collective-permute-start | bytes 884744 | tf_op jit(solution)/shard_map/ppermute | solution.py:175
  57.9 22.2 %collective-permute-start.10 = (bf16[512,256]{1,0:T(8,128)(2,1)S(1)}, bf16[512,256]{1,0:T(8,128)(2,1)S(1)}, u32[]{:S(2)}, u32[]{:S(2)}) collective-permute-start(bf16[512,256]{1,0:T(8,128)(2,1)S(1)} %collective-permute-done.7), channel_id=1, source_target_pairs={{0,2},{1,3},{2,4},{3,5},{4,6},{5,7},{6,0},{7,1},{8,10},{9,11},{10,... | collective-permute-start | bytes 786440 | tf_op jit(solution)/shard_map/ppermute | solution.py:172
  59.1 21.1 %collective-permute-start.11 = (bf16[512,256]{1,0:T(8,128)(2,1)S(1)}, bf16[512,256]{1,0:T(8,128)(2,1)S(1)}, u32[]{:S(2)}, u32[]{:S(2)}) collective-permute-start(bf16[512,256]{1,0:T(8,128)(2,1)S(1)} %collective-permute-done.8), channel_id=1, source_target_pairs={{0,6},{1,7},{2,0},{3,1},{4,2},{5,3},{6,4},{7,5},{8,14},{9,15},{10,... | collective-permute-start | bytes 786440 | tf_op jit(solution)/shard_map/ppermute | solution.py:172
  63.9 15.7 %collective-permute-start.27 = (bf16[128,512]{1,0:T(8,128)(2,1)S(1)}, bf16[128,512]{1,0:T(8,128)(2,1)S(1)}, u32[]{:S(2)}, u32[]{:S(2)}) collective-permute-start(bf16[128,512]{1,0:T(8,128)(2,1)S(1)} %collective-permute-done.24), channel_id=1, source_target_pairs={{0,6},{1,7},{2,0},{3,1},{4,2},{5,3},{6,4},{7,5},{8,14},{9,15},{10,... | collective-permute-start | bytes 393224 | tf_op jit(solution)/shard_map/ppermute | solution.py:172
  67.2 12.4 %collective-permute-start.26 = (bf16[128,640]{1,0:T(8,128)(2,1)S(1)}, bf16[128,640]{1,0:T(8,128)(2,1)S(1)}, u32[]{:S(2)}, u32[]{:S(2)}) collective-permute-start(bf16[128,640]{1,0:T(8,128)(2,1)S(1)} %collective-permute-done.23), channel_id=1, source_target_pairs={{0,2},{1,3},{2,4},{3,5},{4,6},{5,7},{6,0},{7,1},{8,10},{9,11},{10,... | collective-permute-start | bytes 491528 | tf_op jit(solution)/shard_map/ppermute | solution.py:172
  87.5 8.1 %collective-permute-start.14 = (bf16[256,256]{1,0:T(8,128)(2,1)S(1)}, bf16[256,256]{1,0:T(8,128)(2,1)S(1)}, u32[]{:S(2)}, u32[]{:S(2)}) collective-permute-start(bf16[256,256]{1,0:T(8,128)(2,1)S(1)} %fusion.3), channel_id=1, source_target_pairs={{0,16},{8,24},{16,0},{24,8},{1,17},{9,25},{17,1},{25,9},{2,18},{10... | collective-permute-start | bytes 393224 | tf_op jit(solution)/shard_map/ppermute | solution.py:178
  119.4 10.6 %collective-permute-start.30 = (bf16[2,64,1152]{2,1,0:T(8,128)(2,1)S(1)}, bf16[2,64,1152]{2,1,0:T(8,128)(2,1)S(1)}, u32[]{:S(2)}, u32[]{:S(2)}) collective-permute-start(bf16[2,64,1152]{2,1,0:T(8,128)(2,1)S(1)} %get-tuple-element.20), channel_id=1, source_target_pairs={{0,2},{1,3},{2,4},{3,5},{4,6},{5,7},{6,0},{7,1},{8,10},{9,11},{10,... | collective-permute-start | bytes 884744 | tf_op jit(solution)/shard_map/ppermute | solution.py:172
  121.0 25.5 %collective-permute-start.31 = (bf16[2,64,1152]{2,1,0:T(8,128)(2,1)S(1)}, bf16[2,64,1152]{2,1,0:T(8,128)(2,1)S(1)}, u32[]{:S(2)}, u32[]{:S(2)}) collective-permute-start(bf16[2,64,1152]{2,1,0:T(8,128)(2,1)S(1)} %get-tuple-element.22), channel_id=1, source_target_pairs={{0,4},{1,5},{2,6},{3,7},{4,0},{5,1},{6,2},{7,3},{8,12},{9,13},{10,... | collective-permute-start | bytes 884744 | tf_op jit(solution)/shard_map/ppermute | solution.py:172
  124.5 25.2 %collective-permute-start.32 = (bf16[2,64,1152]{2,1,0:T(8,128)(2,1)S(1)}, bf16[2,64,1152]{2,1,0:T(8,128)(2,1)S(1)}, u32[]{:S(2)}, u32[]{:S(2)}) collective-permute-start(bf16[2,64,1152]{2,1,0:T(8,128)(2,1)S(1)} %get-tuple-element.21), channel_id=1, source_target_pairs={{0,6},{1,7},{2,0},{3,1},{4,2},{5,3},{6,4},{7,5},{8,14},{9,15},{10,... | collective-permute-start | bytes 884744 | tf_op jit(solution)/shard_map/ppermute | solution.py:172
  (20 other events, 129.7 us)

commit v2 on v1

--- a/solution.py
+++ b/solution.py
@@ -152,7 +152,7 @@
     return pl.pallas_call(
         reorder_kernel, grid_spec=grid, out_shape=jax.ShapeDtypeStruct(x.shape, x.dtype),
         compiler_params=pltpu.CompilerParams(vmem_limit_bytes=8 * 1024 * 1024),
-        cost_estimate=pl.CostEstimate(flops=0, bytes_accessed=4 * T * width, transcendentals=0), name="reorder",
+        cost_estimate=pl.CostEstimate(flops=0, bytes_accessed=64 * T * width, transcendentals=0), name="reorder",
     )(pos, x)
 
 
@@ -179,66 +179,90 @@
 
     source = lax.dynamic_slice_in_dim(donor_chain, p * nchain, nchain)
 
-    def take_slots(own):
-        every = jnp.concatenate([own] + [exchange(own, k) for k in range(1, nc)])
+    def gather_slots(own):
+        return [own] + [exchange(own, k) for k in range(1, nc)]
+
+    def take_slots(parts, source):
+        every = jnp.concatenate(parts)
         return jnp.concatenate([
             lax.dynamic_slice_in_dim(every, (source[j] // nchain ^ p) * nchain + source[j] % nchain, 1)
             for j in range(nchain)
         ])
 
-    heat = jnp.sqrt(2.0 * STRIDE_LENGTH * chain_heats)[:, None, None]
     first = first_multipliers.transpose(0, 2, 1)
+    kcols = second_multipliers.shape[2]
+    nrank = nchain * RANK
+
+    offsets = [0]
+    for k in range(1, nz // 2):
+        offsets += [-k, k]
+    offsets.append(nz // 2)
+    order = []
+    for k in offsets:
+        order += [(z + k) % nz * 2 + core, (z + k) % nz * 2 + 1 - core]
+
+    def onward(shards, k):
+        if k < nz // 2:
+            up, down = (shards[-2], shards[-1]) if k > 1 else (shards[0], shards[0])
+            return [shift(up, 1), shift(down, -1)]
+        return [shift(shards[-2], 1)]
+
+    w = [locked_projection]
+    w += onward(w, 1)
+    ab_own = jnp.concatenate([first, second_multipliers], axis=2).astype(bf16)
+    ab = take_slots(gather_slots(ab_own), source).reshape(nrank, arows + kcols)
+    heats, w, ab = lax.optimization_barrier((chain_heats, w, ab))
+    up, down = [ab], [ab]
+    for k in range(2, nz // 2 + 1):
+        w += onward(w, k)
+        up.append(shift(up[-1], 1))
+    w_there = [swap_cores(x) for x in w[:-1]]
+    heat = jnp.sqrt(2.0 * STRIDE_LENGTH * heats)[:, None, None]
     pre_a = (1.0 - STRIDE_LENGTH) * first + heat * first_jitter.transpose(0, 2, 1)
     pre_b = (1.0 - STRIDE_LENGTH) * second_multipliers + heat * second_jitter
-    kcols = second_multipliers.shape[2]
-
-    half = arows // 2
-    order = []
+    rest_own = jnp.concatenate([pre_a, pre_b], axis=2).astype(bf16)
+    rest_own, w_there, order = lax.optimization_barrier((rest_own, w_there, jnp.stack(order).astype(jnp.int32)))
+    x_ordered = reorder(order, layer_activations, arows)
+    rest_parts = gather_slots(rest_own)
+    w, up, w_there, x_ordered, down = lax.optimization_barrier((w, up, w_there, x_ordered, down))
+    up.append(shift(up[-1], 1))
+    for k in range(1, nz // 2):
+        down.append(shift(down[-1], -1))
+    def x_piece(s, theirs):
+        return x_ordered[:, (2 * s + theirs) * arows:(2 * s + theirs + 1) * arows]
+
+    def add(total, s, here, there, dims):
+        for i, x in enumerate((here, there)):
+            total = total + dot(x_piece(s, i), x, dims)
+        return total
+
+    w_there.append(swap_cores(w[-1]))
+    plain = 0.0
     for s in range(nz):
-        for c in (core, 1 - core):
-            order += [((z - s) % nz * 2 + c) * 2, ((z + s) % nz * 2 + c) * 2 + 1]
-    x_ordered = reorder(jnp.stack(order).astype(jnp.int32), layer_activations, half)
-
-    def both_cores(pieces, axis):
-        here = jnp.concatenate(pieces, axis=axis)
-        return jnp.concatenate([here, swap_cores(here)], axis=axis)
-
-    def x_piece(s):
-        return x_ordered[:, s * 2 * arows:(s + 1) * 2 * arows]
-
-    w = (locked_projection[:half], locked_projection[half:])
-    a = None
-    plain = low_rank = 0.0
-    b_low = []
-    for s in range(nz + 1):
-        if s < nz:
-            plain = plain + jnp.dot(x_piece(s), both_cores(w, 0), preferred_element_type=f32)
-        if a is not None:
-            here = jnp.concatenate([a[0], a[1]], axis=1)
-            there = swap_cores(here)
-            parts = [here[:, :half], here[:, half + kcols:], there[:, :half], there[:, half + kcols:]]
-            low_rank = low_rank + dot(x_piece(s - 1), jnp.concatenate(parts, axis=1), NT)
-            b_low += [here[:, half:half + kcols], there[:, half:half + kcols]]
-        if s < nz - 1:
-            w = (shift(w[0], 1), shift(w[1], -1))
-        if s == 0:
-            ab = take_slots(jnp.concatenate([first[:, :, :half], second_multipliers, first[:, :, half:]], axis=2).astype(bf16))
-            w, ab = lax.optimization_barrier((w, ab))
-            ab = ab.reshape(nchain * RANK, arows + kcols)
-            a = (ab[:, :half + kcols], ab[:, half + kcols:])
-        elif s < nz:
-            a = (shift(a[0], 1), shift(a[1], -1))
+        plain = add(plain, s, w[s], w_there[s], NN)
     plain = plain.astype(bf16)
+    base = jnp.stack([plain] + [exchange(plain, k) for k in range(1, nc)])
+    a = [ab]
+    for k in range(1, nz // 2):
+        a += [up[k], down[k]]
+    a.append(up[-1])
+    low_rank, b_low = 0.0, []
+    for s in range(nz):
+        if s == 2:
+            base, a, low_rank = lax.optimization_barrier((base, a, low_rank))
+        there = swap_cores(a[s])
+        low_rank = add(low_rank, s, a[s][:, :arows], there[:, :arows], NT)
+        b_low += [a[s][:, arows:], there[:, arows:]]
     low_rank = low_rank.astype(bf16)
-    base = jnp.stack([plain] + [exchange(plain, k) for k in range(1, nc)])
     shards = jnp.arange(nt, dtype=jnp.int32)
-    places = (z - shards // 2) % nz * 2 + (shards % 2 != core).astype(jnp.int32)
+    step_of = jnp.array([[k % nz for k in offsets].index(d) for d in range(nz)], jnp.int32)
+    places = step_of[(shards // 2 - z) % nz] * 2 + (shards % 2 != core).astype(jnp.int32)
     pos = jnp.concatenate([p[None], places]).astype(jnp.int32)
-    rest = take_slots(jnp.concatenate([pre_a, pre_b], axis=2).astype(bf16))
-    base, rest = lax.optimization_barrier((base, rest))
 
     low_grad, right = attention(pos, rotated_probes, attended_slope, attended_contents, base, low_rank, jnp.stack(b_low), scale)
 
+    low_grad, right, rest_parts = lax.optimization_barrier((low_grad, right, rest_parts))
+    rest = take_slots(rest_parts, source)
     around = (z + jnp.arange(nz, dtype=jnp.int32)) % nz
     theirs = swap_cores(gradients(around * 2 + 1 - core, layer_activations, low_grad, right, nz, bf16))
     mine = gradients(around * 2 + core, layer_activations, low_grad, right, nz, f32)

time: 152 us -> 125 us (0.82); the launches traced: 151 us -> 123 us
  waiting for transfers between devices: 75.4 us -> 52.8 us
  starting transfers between devices: 31.7 us -> 27.1 us
  local copies, waits for them, and re-layouts: 6.08 us -> 4.56 us
    ppermute x15 -> x9, waiting for transfers between devices: 58.3 us -> 42.9 us  [shift(): return lax.ppermute(x, 'tok', [(i, (i + 2 * k) % nt) for i in range(nt)])]
    ppermute x15 -> x9, starting transfers between devices: 19.7 us -> 12.1 us  [shift(): return lax.ppermute(x, 'tok', [(i, (i + 2 * k) % nt) for i in range(nt)])]
    ppermute x9, waiting for transfers between devices: 14.8 us -> 7.43 us  [exchange(): return lax.ppermute(x, 'chain', [(i, i ^ k) for i in range(nc)])]
    dot_general x4 -> x16, matrix products: 1.74 us -> 4.89 us  [dot(): return lax.dot_general(a, b, dims, preferred_element_type=f32)]
    unnamed x27 -> x30, local copies, waits for them, and re-layouts: 2.3 us -> 0.2 us
    dot_general x4 -> x0, matrix products: 1.81 us -> none  [per_device(): jnp.dot(x_piece(s), both_cores(w, 0), preferred_element_type=f32)]
    ppermute x9, starting transfers between devices: 10.7 us -> 12.3 us  [exchange(): return lax.ppermute(x, 'chain', [(i, i ^ k) for i in range(nc)])]
  transfers between devices with their start and end apart: 33 -> 27, of which waited for: 15 -> 12; matrix products, arithmetic and copies ran while one was open for 4% -> 9% of each run, Pallas kernels for 2% -> 18%
where the time goes in v2:
time: 125 us; the launch traced here: 123 us
  waiting for transfers between devices  52.8 us (42%)
  starting transfers between devices  27.1 us (22%)
  Pallas kernels  23.8 us (19%)
  between operations  6.15 us (5%)
  matrix products  4.89 us (4%)
  local copies, waits for them, and re-layouts  4.56 us (4%)
  other arithmetic  3.69 us (3%)
    ppermute x9, waiting for transfers between devices, shift(): return lax.ppermute(x, 'tok', [(i, (i + 2 * k) % nt) for i in range(nt)])  42.9 us
    pallas_call x1, Pallas kernels, attention(): pl.pallas_call(functools.partial(attention_kernel, scale, nchain, group,...  18.7 us
    ppermute x9, starting transfers between devices, exchange(): return lax.ppermute(x, 'chain', [(i, i ^ k) for i in range(nc)])  12.3 us
    ppermute x9, starting transfers between devices, shift(): return lax.ppermute(x, 'tok', [(i, (i + 2 * k) % nt) for i in range(nt)])  12.1 us
    ppermute x9, waiting for transfers between devices, exchange(): return lax.ppermute(x, 'chain', [(i, i ^ k) for i in range(nc)])  7.43 us
    dot_general x16, matrix products, dot(): return lax.dot_general(a, b, dims, preferred_element_type=f32)  4.89 us
    pallas_call x2, Pallas kernels, gradients(): pl.pallas_call(functools.partial(gradient_kernel, n, nrank), grid_spec=gr...  3.54 us
    ppermute x9, starting transfers between devices, swap_cores(): return lax.ppermute(x, 'tok', [(i, i ^ 1) for i in range(nt)])  2.72 us
  transfers between devices with their start and end apart: 27, of which 12 were waited for; matrix products, arithmetic and copies ran while one was open for 9% of the time, Pallas kernels for 18%

profile of v2, /device:TPU:8, one launch (start us, length us, event | category | flops | bytes accessed | tf_op | source)
XLA Modules:
  0.0 122.9 jit_solution(14924512690910272373)
XLA Ops:
  0.6 1.6 %collective-permute-start = (bf16[1024,256]{1,0:T(8,128)(2,1)}, bf16[1024,256]{1,0:T(8,128)(2,1)S(1)}, u32[]{:S(2)}, u32[]{:S(2)}) collective-permute-start(bf16[1024,256]{1,0:T(8,128)(2,1)} %param.16), channel_id=1, source_target_pairs={{0,2},{1,3},{2,4},{3,5},{4,6},{5,7},{6,0},{7,1},{8,10},{9,11},{10,... | collective-permute-start | bytes 1572872 | tf_op jit(solution)/shard_map/ppermute | solution.py:172
  3.6 1.1 convert_bitcast_fusion
  5.4 2.4 %collective-permute-start.4 = (bf16[2,64,1152]{2,1,0:T(8,128)(2,1)}, bf16[2,64,1152]{2,1,0:T(8,128)(2,1)S(1)}, u32[]{:S(2)}, u32[]{:S(2)}) collective-permute-start(bf16[2,64,1152]{2,1,0:T(8,128)(2,1)} %pad_maximum_fusion.2), channel_id=1, source_target_pairs={{0,24},{8,16},{16,8},{24,0},{1,25},{9,17},{17,9},{25,1},{2,26},{10... | collective-permute-start | bytes 884744 | tf_op jit(solution)/shard_map/ppermute | solution.py:178
  15.3 1.3 %gather_fusion = s32[8]{0:T(128)S(1)} fusion(s32[4]{0:T(128)} %constant.144.clone, s32[1024]{0:T(1024)S(1)} %pad_clamp_fusion), kind=kCustom, calls=%fused_computation | custom fusion | bytes 96 | tf_op jit(solution)/shard_map/gather | solution.py:259
  16.8 4.2 %collective-permute-done.3 = bf16[2,64,1152]{2,1,0:T(8,128)(2,1)S(1)} collective-permute-done((bf16[2,64,1152]{2,1,0:T(8,128)(2,1)}, bf16[2,64,1152]{2,1,0:T(8,128)(2,1)S(1)}, u32[]{:S(2)}, u32[]{:S(2)}) %collective-permute-start.3) | collective-permute-done | bytes 294944 | tf_op jit(solution)/shard_map/ppermute | solution.py:178
  21.3 5.3 %collective-permute-done.1 = bf16[1024,256]{1,0:T(8,128)(2,1)S(1)} collective-permute-done((bf16[1024,256]{1,0:T(8,128)(2,1)}, bf16[1024,256]{1,0:T(8,128)(2,1)S(1)}, u32[]{:S(2)}, u32[]{:S(2)}) %collective-permute-start.1) | collective-permute-done | bytes 524320 | tf_op jit(solution)/shard_map/ppermute | solution.py:172
  28.8 0.9 collective-permute-done.16
  29.7 1.6 %collective-permute-start.6 = (bf16[128,1152]{1,0:T(8,128)(2,1)S(1)}, bf16[128,1152]{1,0:T(8,128)(2,1)S(1)}, u32[]{:S(2)}, u32[]{:S(2)}) collective-permute-start(bf16[128,1152]{1,0:T(8,128)(2,1)S(1)} %bitcast.76), channel_id=1, source_target_pairs={{0,2},{1,3},{2,4},{3,5},{4,6},{5,7},{6,0},{7,1},{8,10},{9,11},{10,... | collective-permute-start | bytes 884744 | tf_op jit(solution)/shard_map/ppermute | solution.py:172
  31.3 1.6 %reorder.1 = bf16[256,8192]{1,0:T(8,128)(2,1)S(1)} custom-call(s32[8]{0:T(128)S(1)} %stack.77.pos_ref, bf16[256,8192]{1,0:T(8,128)(2,1)S(1)} %copy-done), custom_call_target="tpu_custom_call" | custom-call | bytes 134217728 | tf_op jit(solution)/shard_map/reorder/pallas_call | solution.py:152
  32.9 13.9 %collective-permute-done.6 = bf16[128,1152]{1,0:T(8,128)(2,1)S(1)} collective-permute-done((bf16[128,1152]{1,0:T(8,128)(2,1)S(1)}, bf16[128,1152]{1,0:T(8,128)(2,1)S(1)}, u32[]{:S(2)}, u32[]{:S(2)}) %collective-permute-start.6) | collective-permute-done | bytes 294944 | tf_op jit(solution)/shard_map/ppermute | solution.py:172
  49.2 1.8 %collective-permute-start.14 = (bf16[128,1152]{1,0:T(8,128)(2,1)S(1)}, bf16[128,1152]{1,0:T(8,128)(2,1)S(1)}, u32[]{:S(2)}, u32[]{:S(2)}) collective-permute-start(bf16[128,1152]{1,0:T(8,128)(2,1)S(1)} %bitcast.78), channel_id=1, source_target_pairs={{0,6},{1,7},{2,0},{3,1},{4,2},{5,3},{6,4},{7,5},{8,14},{9,15},{10,... | collective-permute-start | bytes 884744 | tf_op jit(solution)/shard_map/ppermute | solution.py:172
  53.3 2.5 %collective-permute-start.13 = (bf16[256,256]{1,0:T(8,128)(2,1)S(1)}, bf16[256,256]{1,0:T(8,128)(2,1)S(1)}, u32[]{:S(2)}, u32[]{:S(2)}) collective-permute-start(bf16[256,256]{1,0:T(8,128)(2,1)S(1)} %fusion.7), channel_id=1, source_target_pairs={{0,24},{8,16},{16,8},{24,0},{1,25},{9,17},{17,9},{25,1},{2,26},{10... | collective-permute-start | bytes 393224 | tf_op jit(solution)/shard_map/ppermute | solution.py:178
  56.8 2.9 %collective-permute-done.13 = bf16[256,256]{1,0:T(8,128)(2,1)S(1)} collective-permute-done((bf16[256,256]{1,0:T(8,128)(2,1)S(1)}, bf16[256,256]{1,0:T(8,128)(2,1)S(1)}, u32[]{:S(2)}, u32[]{:S(2)}) %collective-permute-start.13) | collective-permute-done | bytes 131104 | tf_op jit(solution)/shard_map/ppermute | solution.py:178
  59.8 2.4 %collective-permute-start.20 = (bf16[2,64,1152]{2,1,0:T(8,128)(2,1)S(1)}, bf16[2,64,1152]{2,1,0:T(8,128)(2,1)S(1)}, u32[]{:S(2)}, u32[]{:S(2)}) collective-permute-start(bf16[2,64,1152]{2,1,0:T(8,128)(2,1)S(1)} %pad_maximum_fusion.4), channel_id=1, source_target_pairs={{0,8},{8,0},{16,24},{24,16},{1,9},{9,1},{17,25},{25,17},{2,10},{10... | collective-permute-start | bytes 884744 | tf_op jit(solution)/shard_map/ppermute | solution.py:178
  62.2 1.5 %collective-permute-start.21 = (bf16[2,64,1152]{2,1,0:T(8,128)(2,1)S(1)}, bf16[2,64,1152]{2,1,0:T(8,128)(2,1)S(1)}, u32[]{:S(2)}, u32[]{:S(2)}) collective-permute-start(bf16[2,64,1152]{2,1,0:T(8,128)(2,1)S(1)} %pad_maximum_fusion.4), channel_id=1, source_target_pairs={{0,16},{8,24},{16,0},{24,8},{1,17},{9,25},{17,1},{25,9},{2,18},{10... | collective-permute-start | bytes 884744 | tf_op jit(solution)/shard_map/ppermute | solution.py:178
  63.8 1.4 %collective-permute-start.22 = (bf16[2,64,1152]{2,1,0:T(8,128)(2,1)S(1)}, bf16[2,64,1152]{2,1,0:T(8,128)(2,1)S(1)}, u32[]{:S(2)}, u32[]{:S(2)}) collective-permute-start(bf16[2,64,1152]{2,1,0:T(8,128)(2,1)S(1)} %pad_maximum_fusion.4), channel_id=1, source_target_pairs={{0,24},{8,16},{16,8},{24,0},{1,25},{9,17},{17,9},{25,1},{2,26},{10... | collective-permute-start | bytes 884744 | tf_op jit(solution)/shard_map/ppermute | solution.py:178
  68.2 18.7 %attention.1 = (bf16[256,128]{1,0:T(8,128)(2,1)S(1)}, f32[8,2,64,128]{3,2,1,0:T(8,128)S(1)}) custom-call(s32[9]{0:T(128)S(1)} %pad_add_fusion.pos_ref, bf16[256,8192]{1,0:T(8,128)(2,1)S(1)} %copy-done.1, bf16[256,8192]{1,0:T(8,128)(2,1)S(1)} %copy-done.2, bf16[256,1024]{1,0:T(8,128)(2,1)S(1)} %copy-done.3, ...), custom_call_target="tpu_custom_call" | custom-call | flops 10000000000 | bytes 20000000 | tf_op jit(solution)/shard_map/attention/pallas_call | solution.py:95
  86.9 1.8 %gradients.3 = bf16[4,2,64,1152]{3,2,1,0:T(8,128)(2,1)S(1)} custom-call(s32[4]{0:T(128)S(1)} %add_subtract_fusion.pos_ref, bf16[256,8192]{1,0:T(8,128)(2,1)S(1)} %copy-done, bf16[256,128]{1,0:T(8,128)(2,1)S(1)} %get-tuple-element.64.lg_ref, f32[8,2,64,128]{3,2,1,0:T(8,128)S(1)} %get-tuple-element.65.rt_ref), custom_call_target="tpu_custom_call" | custom-call | flops 268435456 | bytes 3000000 | tf_op jit(solution)/shard_map/gradients/pallas_call | solution.py:132
  89.1 1.8 %gradients.2 = f32[4,2,64,1152]{3,2,1,0:T(8,128)S(1)} custom-call(s32[4]{0:T(128)S(1)} %broadcast_add_fusion.pos_ref, bf16[256,8192]{1,0:T(8,128)(2,1)S(1)} %copy-done, bf16[256,128]{1,0:T(8,128)(2,1)S(1)} %get-tuple-element.64.lg_ref, f32[8,2,64,128]{3,2,1,0:T(8,128)S(1)} %get-tuple-element.65.rt_ref), custom_call_target="tpu_custom_call" | custom-call | flops 268435456 | bytes 3000000 | tf_op jit(solution)/shard_map/gradients/pallas_call | solution.py:132
  91.9 3.8 %collective-permute-start.26 = (bf16[2,64,1152]{2,1,0:T(8,128)(2,1)S(1)}, bf16[2,64,1152]{2,1,0:T(8,128)(2,1)S(1)}, u32[]{:S(2)}, u32[]{:S(2)}) collective-permute-start(bf16[2,64,1152]{2,1,0:T(8,128)(2,1)S(1)} %get-tuple-element.71), channel_id=1, source_target_pairs={{0,6},{1,7},{2,0},{3,1},{4,2},{5,3},{6,4},{7,5},{8,14},{9,15},{10,... | collective-permute-start | bytes 884744 | tf_op jit(solution)/shard_map/ppermute | solution.py:172
  95.7 1.8 %collective-permute-start.24 = (bf16[2,64,1152]{2,1,0:T(8,128)(2,1)S(1)}, bf16[2,64,1152]{2,1,0:T(8,128)(2,1)S(1)}, u32[]{:S(2)}, u32[]{:S(2)}) collective-permute-start(bf16[2,64,1152]{2,1,0:T(8,128)(2,1)S(1)} %get-tuple-element.70), channel_id=1, source_target_pairs={{0,2},{1,3},{2,4},{3,5},{4,6},{5,7},{6,0},{7,1},{8,10},{9,11},{10,... | collective-permute-start | bytes 884744 | tf_op jit(solution)/shard_map/ppermute | solution.py:172
  97.5 5.9 %collective-permute-done.26 = bf16[2,64,1152]{2,1,0:T(8,128)(2,1)S(1)} collective-permute-done((bf16[2,64,1152]{2,1,0:T(8,128)(2,1)S(1)}, bf16[2,64,1152]{2,1,0:T(8,128)(2,1)S(1)}, u32[]{:S(2)}, u32[]{:S(2)}) %collective-permute-start.26) | collective-permute-done | bytes 294944 | tf_op jit(solution)/shard_map/ppermute | solution.py:172
  103.4 11.5 %collective-permute-done.25 = bf16[2,64,1152]{2,1,0:T(8,128)(2,1)S(1)} collective-permute-done((bf16[2,64,1152]{2,1,0:T(8,128)(2,1)S(1)}, bf16[2,64,1152]{2,1,0:T(8,128)(2,1)S(1)}, u32[]{:S(2)}, u32[]{:S(2)}) %collective-permute-start.25) | collective-permute-done | bytes 294944 | tf_op jit(solution)/shard_map/ppermute | solution.py:172
  115.0 6.3 %collective-permute-done.24 = bf16[2,64,1152]{2,1,0:T(8,128)(2,1)S(1)} collective-permute-done((bf16[2,64,1152]{2,1,0:T(8,128)(2,1)S(1)}, bf16[2,64,1152]{2,1,0:T(8,128)(2,1)S(1)}, u32[]{:S(2)}, u32[]{:S(2)}) %collective-permute-start.24) | collective-permute-done | bytes 294944 | tf_op jit(solution)/shard_map/ppermute | solution.py:172
  (109 shorter events, 18.8 us)
Async XLA Ops:
  0.6 20.7 %collective-permute-start = (bf16[1024,256]{1,0:T(8,128)(2,1)}, bf16[1024,256]{1,0:T(8,128)(2,1)S(1)}, u32[]{:S(2)}, u32[]{:S(2)}) collective-permute-start(bf16[1024,256]{1,0:T(8,128)(2,1)} %param.16), channel_id=1, source_target_pairs={{0,2},{1,3},{2,4},{3,5},{4,6},{5,7},{6,0},{7,1},{8,10},{9,11},{10,... | collective-permute-start | bytes 1572872 | tf_op jit(solution)/shard_map/ppermute | solution.py:172
  2.3 24.4 %collective-permute-start.1 = (bf16[1024,256]{1,0:T(8,128)(2,1)}, bf16[1024,256]{1,0:T(8,128)(2,1)S(1)}, u32[]{:S(2)}, u32[]{:S(2)}) collective-permute-start(bf16[1024,256]{1,0:T(8,128)(2,1)} %param.16), channel_id=1, source_target_pairs={{0,6},{1,7},{2,0},{3,1},{4,2},{5,3},{6,4},{7,5},{8,14},{9,15},{10,... | collective-permute-start | bytes 1572872 | tf_op jit(solution)/shard_map/ppermute | solution.py:172
  5.4 11.4 %collective-permute-start.4 = (bf16[2,64,1152]{2,1,0:T(8,128)(2,1)}, bf16[2,64,1152]{2,1,0:T(8,128)(2,1)S(1)}, u32[]{:S(2)}, u32[]{:S(2)}) collective-permute-start(bf16[2,64,1152]{2,1,0:T(8,128)(2,1)} %pad_maximum_fusion.2), channel_id=1, source_target_pairs={{0,24},{8,16},{16,8},{24,0},{1,25},{9,17},{17,9},{25,1},{2,26},{10... | collective-permute-start | bytes 884744 | tf_op jit(solution)/shard_map/ppermute | solution.py:178
  7.9 13.2 %collective-permute-start.3 = (bf16[2,64,1152]{2,1,0:T(8,128)(2,1)}, bf16[2,64,1152]{2,1,0:T(8,128)(2,1)S(1)}, u32[]{:S(2)}, u32[]{:S(2)}) collective-permute-start(bf16[2,64,1152]{2,1,0:T(8,128)(2,1)} %pad_maximum_fusion.2), channel_id=1, source_target_pairs={{0,16},{8,24},{16,0},{24,8},{1,17},{9,25},{17,1},{25,9},{2,18},{10... | collective-permute-start | bytes 884744 | tf_op jit(solution)/shard_map/ppermute | solution.py:178
  8.4 12.8 %collective-permute-start.2 = (bf16[2,64,1152]{2,1,0:T(8,128)(2,1)}, bf16[2,64,1152]{2,1,0:T(8,128)(2,1)S(1)}, u32[]{:S(2)}, u32[]{:S(2)}) collective-permute-start(bf16[2,64,1152]{2,1,0:T(8,128)(2,1)} %pad_maximum_fusion.2), channel_id=1, source_target_pairs={{0,8},{8,0},{16,24},{24,16},{1,9},{9,1},{17,25},{25,17},{2,10},{10... | collective-permute-start | bytes 884744 | tf_op jit(solution)/shard_map/ppermute | solution.py:178
  26.6 20.2 %collective-permute-start.5 = (bf16[1024,256]{1,0:T(8,128)(2,1)S(1)}, bf16[1024,256]{1,0:T(8,128)(2,1)S(1)}, u32[]{:S(2)}, u32[]{:S(2)}) collective-permute-start(bf16[1024,256]{1,0:T(8,128)(2,1)S(1)} %collective-permute-done), channel_id=1, source_target_pairs={{0,2},{1,3},{2,4},{3,5},{4,6},{5,7},{6,0},{7,1},{8,10},{9,11},{10,... | collective-permute-start | bytes 1572872 | tf_op jit(solution)/shard_map/ppermute | solution.py:172
  27.4 3.9 %collective-permute-start.8 = (bf16[1024,256]{1,0:T(8,128)(2,1)S(1)}, bf16[1024,256]{1,0:T(8,128)(2,1)S(1)}, u32[]{:S(2)}, u32[]{:S(2)}) collective-permute-start(bf16[1024,256]{1,0:T(8,128)(2,1)S(1)} %collective-permute-done), channel_id=1, source_target_pairs={{0,1},{1,0},{2,3},{3,2},{4,5},{5,4},{6,7},{7,6},{8,9},{9,8},{10,11... | collective-permute-start | bytes 1572872 | tf_op jit(solution)/shard_map/ppermute | solution.py:175
  28.2 3.1 %collective-permute-start.7 = (bf16[1024,256]{1,0:T(8,128)(2,1)S(1)}, bf16[1024,256]{1,0:T(8,128)(2,1)S(1)}, u32[]{:S(2)}, u32[]{:S(2)}) collective-permute-start(bf16[1024,256]{1,0:T(8,128)(2,1)S(1)} %copy-done.6), channel_id=1, source_target_pairs={{0,1},{1,0},{2,3},{3,2},{4,5},{5,4},{6,7},{7,6},{8,9},{9,8},{10,11... | collective-permute-start | bytes 1572872 | tf_op jit(solution)/shard_map/ppermute | solution.py:175
  28.3 3.0 %collective-permute-start.9 = (bf16[1024,256]{1,0:T(8,128)(2,1)S(1)}, bf16[1024,256]{1,0:T(8,128)(2,1)S(1)}, u32[]{:S(2)}, u32[]{:S(2)}) collective-permute-start(bf16[1024,256]{1,0:T(8,128)(2,1)S(1)} %collective-permute-done.1), channel_id=1, source_target_pairs={{0,1},{1,0},{2,3},{3,2},{4,5},{5,4},{6,7},{7,6},{8,9},{9,8},{10,11... | collective-permute-start | bytes 1572872 | tf_op jit(solution)/shard_map/ppermute | solution.py:175
  29.7 17.1 %collective-permute-start.6 = (bf16[128,1152]{1,0:T(8,128)(2,1)S(1)}, bf16[128,1152]{1,0:T(8,128)(2,1)S(1)}, u32[]{:S(2)}, u32[]{:S(2)}) collective-permute-start(bf16[128,1152]{1,0:T(8,128)(2,1)S(1)} %bitcast.76), channel_id=1, source_target_pairs={{0,2},{1,3},{2,4},{3,5},{4,6},{5,7},{6,0},{7,1},{8,10},{9,11},{10,... | collective-permute-start | bytes 884744 | tf_op jit(solution)/shard_map/ppermute | solution.py:172
  46.8 18.5 %collective-permute-start.15 = (bf16[128,1152]{1,0:T(8,128)(2,1)S(1)}, bf16[128,1152]{1,0:T(8,128)(2,1)S(1)}, u32[]{:S(2)}, u32[]{:S(2)}) collective-permute-start(bf16[128,1152]{1,0:T(8,128)(2,1)S(1)} %collective-permute-done.6), channel_id=1, source_target_pairs={{0,2},{1,3},{2,4},{3,5},{4,6},{5,7},{6,0},{7,1},{8,10},{9,11},{10,... | collective-permute-start | bytes 884744 | tf_op jit(solution)/shard_map/ppermute | solution.py:172
  47.1 5.2 %collective-permute-start.17 = (bf16[128,1152]{1,0:T(8,128)(2,1)S(1)}, bf16[128,1152]{1,0:T(8,128)(2,1)S(1)}, u32[]{:S(2)}, u32[]{:S(2)}) collective-permute-start(bf16[128,1152]{1,0:T(8,128)(2,1)S(1)} %collective-permute-done.6), channel_id=1, source_target_pairs={{0,1},{1,0},{2,3},{3,2},{4,5},{5,4},{6,7},{7,6},{8,9},{9,8},{10,11... | collective-permute-start | bytes 884744 | tf_op jit(solution)/shard_map/ppermute | solution.py:175
  47.1 5.5 %collective-permute-start.10 = (bf16[1024,256]{1,0:T(8,128)(2,1)S(1)}, bf16[1024,256]{1,0:T(8,128)(2,1)S(1)}, u32[]{:S(2)}, u32[]{:S(2)}) collective-permute-start(bf16[1024,256]{1,0:T(8,128)(2,1)S(1)} %collective-permute-done.5), channel_id=1, source_target_pairs={{0,1},{1,0},{2,3},{3,2},{4,5},{5,4},{6,7},{7,6},{8,9},{9,8},{10,11... | collective-permute-start | bytes 1572872 | tf_op jit(solution)/shard_map/ppermute | solution.py:175
  49.2 16.1 %collective-permute-start.14 = (bf16[128,1152]{1,0:T(8,128)(2,1)S(1)}, bf16[128,1152]{1,0:T(8,128)(2,1)S(1)}, u32[]{:S(2)}, u32[]{:S(2)}) collective-permute-start(bf16[128,1152]{1,0:T(8,128)(2,1)S(1)} %bitcast.78), channel_id=1, source_target_pairs={{0,6},{1,7},{2,0},{3,1},{4,2},{5,3},{6,4},{7,5},{8,14},{9,15},{10,... | collective-permute-start | bytes 884744 | tf_op jit(solution)/shard_map/ppermute | solution.py:172
  53.3 6.5 %collective-permute-start.13 = (bf16[256,256]{1,0:T(8,128)(2,1)S(1)}, bf16[256,256]{1,0:T(8,128)(2,1)S(1)}, u32[]{:S(2)}, u32[]{:S(2)}) collective-permute-start(bf16[256,256]{1,0:T(8,128)(2,1)S(1)} %fusion.7), channel_id=1, source_target_pairs={{0,24},{8,16},{16,8},{24,0},{1,25},{9,17},{17,9},{25,1},{2,26},{10... | collective-permute-start | bytes 393224 | tf_op jit(solution)/shard_map/ppermute | solution.py:178
  55.8 6.5 %collective-permute-start.12 = (bf16[256,256]{1,0:T(8,128)(2,1)S(1)}, bf16[256,256]{1,0:T(8,128)(2,1)S(1)}, u32[]{:S(2)}, u32[]{:S(2)}) collective-permute-start(bf16[256,256]{1,0:T(8,128)(2,1)S(1)} %fusion.7), channel_id=1, source_target_pairs={{0,16},{8,24},{16,0},{24,8},{1,17},{9,25},{17,1},{25,9},{2,18},{10... | collective-permute-start | bytes 393224 | tf_op jit(solution)/shard_map/ppermute | solution.py:178
  56.3 7.5 %collective-permute-start.11 = (bf16[256,256]{1,0:T(8,128)(2,1)S(1)}, bf16[256,256]{1,0:T(8,128)(2,1)S(1)}, u32[]{:S(2)}, u32[]{:S(2)}) collective-permute-start(bf16[256,256]{1,0:T(8,128)(2,1)S(1)} %fusion.7), channel_id=1, source_target_pairs={{0,8},{8,0},{16,24},{24,16},{1,9},{9,1},{17,25},{25,17},{2,10},{10... | collective-permute-start | bytes 393224 | tf_op jit(solution)/shard_map/ppermute | solution.py:178
  59.8 27.1 %collective-permute-start.20 = (bf16[2,64,1152]{2,1,0:T(8,128)(2,1)S(1)}, bf16[2,64,1152]{2,1,0:T(8,128)(2,1)S(1)}, u32[]{:S(2)}, u32[]{:S(2)}) collective-permute-start(bf16[2,64,1152]{2,1,0:T(8,128)(2,1)S(1)} %pad_maximum_fusion.4), channel_id=1, source_target_pairs={{0,8},{8,0},{16,24},{24,16},{1,9},{9,1},{17,25},{25,17},{2,10},{10... | collective-permute-start | bytes 884744 | tf_op jit(solution)/shard_map/ppermute | solution.py:178
  62.2 24.6 %collective-permute-start.21 = (bf16[2,64,1152]{2,1,0:T(8,128)(2,1)S(1)}, bf16[2,64,1152]{2,1,0:T(8,128)(2,1)S(1)}, u32[]{:S(2)}, u32[]{:S(2)}) collective-permute-start(bf16[2,64,1152]{2,1,0:T(8,128)(2,1)S(1)} %pad_maximum_fusion.4), channel_id=1, source_target_pairs={{0,16},{8,24},{16,0},{24,8},{1,17},{9,25},{17,1},{25,9},{2,18},{10... | collective-permute-start | bytes 884744 | tf_op jit(solution)/shard_map/ppermute | solution.py:178
  63.8 23.1 %collective-permute-start.22 = (bf16[2,64,1152]{2,1,0:T(8,128)(2,1)S(1)}, bf16[2,64,1152]{2,1,0:T(8,128)(2,1)S(1)}, u32[]{:S(2)}, u32[]{:S(2)}) collective-permute-start(bf16[2,64,1152]{2,1,0:T(8,128)(2,1)S(1)} %pad_maximum_fusion.4), channel_id=1, source_target_pairs={{0,24},{8,16},{16,8},{24,0},{1,25},{9,17},{17,9},{25,1},{2,26},{10... | collective-permute-start | bytes 884744 | tf_op jit(solution)/shard_map/ppermute | solution.py:178
  88.6 2.9 %collective-permute-start.23 = (bf16[4,2,64,1152]{3,2,1,0:T(8,128)(2,1)S(1)}, bf16[4,2,64,1152]{3,2,1,0:T(8,128)(2,1)S(1)}, u32[]{:S(2)}, u32[]{:S(2)}) collective-permute-start(bf16[4,2,64,1152]{3,2,1,0:T(8,128)(2,1)S(1)} %gradients.3), channel_id=1, source_target_pairs={{0,1},{1,0},{2,3},{3,2},{4,5},{5,4},{6,7},{7,6},{8,9},{9,8},{10,11... | collective-permute-start | bytes 3538952 | tf_op jit(solution)/shard_map/ppermute | solution.py:175
  91.9 11.6 %collective-permute-start.26 = (bf16[2,64,1152]{2,1,0:T(8,128)(2,1)S(1)}, bf16[2,64,1152]{2,1,0:T(8,128)(2,1)S(1)}, u32[]{:S(2)}, u32[]{:S(2)}) collective-permute-start(bf16[2,64,1152]{2,1,0:T(8,128)(2,1)S(1)} %get-tuple-element.71), channel_id=1, source_target_pairs={{0,6},{1,7},{2,0},{3,1},{4,2},{5,3},{6,4},{7,5},{8,14},{9,15},{10,... | collective-permute-start | bytes 884744 | tf_op jit(solution)/shard_map/ppermute | solution.py:172
  95.7 19.3 %collective-permute-start.25 = (bf16[2,64,1152]{2,1,0:T(8,128)(2,1)S(1)}, bf16[2,64,1152]{2,1,0:T(8,128)(2,1)S(1)}, u32[]{:S(2)}, u32[]{:S(2)}) collective-permute-start(bf16[2,64,1152]{2,1,0:T(8,128)(2,1)S(1)} %get-tuple-element.72), channel_id=1, source_target_pairs={{0,4},{1,5},{2,6},{3,7},{4,0},{5,1},{6,2},{7,3},{8,12},{9,13},{10,... | collective-permute-start | bytes 884744 | tf_op jit(solution)/shard_map/ppermute | solution.py:172
  95.7 25.5 %collective-permute-start.24 = (bf16[2,64,1152]{2,1,0:T(8,128)(2,1)S(1)}, bf16[2,64,1152]{2,1,0:T(8,128)(2,1)S(1)}, u32[]{:S(2)}, u32[]{:S(2)}) collective-permute-start(bf16[2,64,1152]{2,1,0:T(8,128)(2,1)S(1)} %get-tuple-element.70), channel_id=1, source_target_pairs={{0,2},{1,3},{2,4},{3,5},{4,6},{5,7},{6,0},{7,1},{8,10},{9,11},{10,... | collective-permute-start | bytes 884744 | tf_op jit(solution)/shard_map/ppermute | solution.py:172
  (13 other events, 145.6 us)

commit v3 on v2

--- a/solution.py
+++ b/solution.py
@@ -71,7 +71,7 @@
         lg_ref[...] = (scale * acc_ref[...]).astype(lg_ref.dtype)
 
 
-def attention(pos, q, do, v, base, lr, b, scale):
+def attention(pos, q, do, v, base, lr, b, scale, pair=4):
     T, KW = v.shape
     nchain = lr.shape[1] // RANK
     KH, group = KW // HD, q.shape[1] // KW
@@ -93,7 +93,7 @@
         scratch_shapes=[pltpu.VMEM(lr.shape, f32)],
     )
     return pl.pallas_call(
-        functools.partial(attention_kernel, scale, nchain, group, 4), grid_spec=grid,
+        functools.partial(attention_kernel, scale, nchain, group, pair), grid_spec=grid,
         out_shape=[jax.ShapeDtypeStruct(lr.shape, bf16), jax.ShapeDtypeStruct((KH, nchain, RANK, HD), f32)],
         compiler_params=pltpu.CompilerParams(vmem_limit_bytes=28 * 1024 * 1024),
         cost_estimate=pl.CostEstimate(flops=10_000_000_000, bytes_accessed=20_000_000, transcendentals=T * T * 64 * nchain),
@@ -223,11 +223,7 @@
     rest_own = jnp.concatenate([pre_a, pre_b], axis=2).astype(bf16)
     rest_own, w_there, order = lax.optimization_barrier((rest_own, w_there, jnp.stack(order).astype(jnp.int32)))
     x_ordered = reorder(order, layer_activations, arows)
-    rest_parts = gather_slots(rest_own)
-    w, up, w_there, x_ordered, down = lax.optimization_barrier((w, up, w_there, x_ordered, down))
-    up.append(shift(up[-1], 1))
-    for k in range(1, nz // 2):
-        down.append(shift(down[-1], -1))
+
     def x_piece(s, theirs):
         return x_ordered[:, (2 * s + theirs) * arows:(2 * s + theirs + 1) * arows]
 
@@ -236,11 +232,15 @@
             total = total + dot(x_piece(s, i), x, dims)
         return total
 
-    w_there.append(swap_cores(w[-1]))
     plain = 0.0
-    for s in range(nz):
+    for s in range(nz - 1):
         plain = add(plain, s, w[s], w_there[s], NN)
-    plain = plain.astype(bf16)
+    rest_parts = gather_slots(rest_own)
+    w[-1], up, w_there, down, rest_parts = lax.optimization_barrier((w[-1], up, w_there, down, rest_parts))
+    up.append(shift(up[-1], 1))
+    for k in range(1, nz // 2):
+        down.append(shift(down[-1], -1))
+    plain = add(plain, nz - 1, w[-1], swap_cores(w[-1]), NN).astype(bf16)
     base = jnp.stack([plain] + [exchange(plain, k) for k in range(1, nc)])
     a = [ab]
     for k in range(1, nz // 2):

time: 125 us -> 123 us (0.984)
  the two profiles are of different devices: /device:TPU:8 before, /device:TPU:0 now
where the time goes in v3:
time: 123 us
  waiting for transfers between devices  53.2 us (43%)
  starting transfers between devices  26.7 us (22%)
  Pallas kernels  23.8 us (19%)
  between operations  6.1 us (5%)
  matrix products  4.9 us (4%)
  local copies, waits for them, and re-layouts  4.56 us (4%)
  other arithmetic  3.69 us (3%)
    ppermute x9, waiting for transfers between devices, shift(): return lax.ppermute(x, 'tok', [(i, (i + 2 * k) % nt) for i in range(nt)])  38.4 us
    pallas_call x1, Pallas kernels, attention(): pl.pallas_call(functools.partial(attention_kernel, scale, nchain, group,...  18.7 us
    ppermute x9, starting transfers between devices, shift(): return lax.ppermute(x, 'tok', [(i, (i + 2 * k) % nt) for i in range(nt)])  13.5 us
    ppermute x9, waiting for transfers between devices, exchange(): return lax.ppermute(x, 'chain', [(i, i ^ k) for i in range(nc)])  10.8 us
    ppermute x9, starting transfers between devices, exchange(): return lax.ppermute(x, 'chain', [(i, i ^ k) for i in range(nc)])  10.6 us
    dot_general x16, matrix products, dot(): return lax.dot_general(a, b, dims, preferred_element_type=f32)  4.9 us
    ppermute x9, waiting for transfers between devices, swap_cores(): return lax.ppermute(x, 'tok', [(i, i ^ 1) for i in range(nt)])  3.95 us
    pallas_call x2, Pallas kernels, gradients(): pl.pallas_call(functools.partial(gradient_kernel, n, nrank), grid_spec=gr...  3.54 us
  transfers between devices with their start and end apart: 27, of which 14 were waited for; matrix products, arithmetic and copies ran while one was open for 9% of the time, Pallas kernels for 3%

profile of v3, /device:TPU:0, one launch (start us, length us, event | category | flops | bytes accessed | tf_op | source)
XLA Modules:
  0.0 122.9 jit_solution(14655289287726237308)
XLA Ops:
  0.6 3.1 %collective-permute-start = (bf16[1024,256]{1,0:T(8,128)(2,1)}, bf16[1024,256]{1,0:T(8,128)(2,1)S(1)}, u32[]{:S(2)}, u32[]{:S(2)}) collective-permute-start(bf16[1024,256]{1,0:T(8,128)(2,1)} %param.16), channel_id=1, source_target_pairs={{0,2},{1,3},{2,4},{3,5},{4,6},{5,7},{6,0},{7,1},{8,10},{9,11},{10,... | collective-permute-start | bytes 1572872 | tf_op jit(solution)/shard_map/ppermute | solution.py:172
  3.7 2.1 %collective-permute-start.1 = (bf16[1024,256]{1,0:T(8,128)(2,1)}, bf16[1024,256]{1,0:T(8,128)(2,1)S(1)}, u32[]{:S(2)}, u32[]{:S(2)}) collective-permute-start(bf16[1024,256]{1,0:T(8,128)(2,1)} %param.16), channel_id=1, source_target_pairs={{0,6},{1,7},{2,0},{3,1},{4,2},{5,3},{6,4},{7,5},{8,14},{9,15},{10,... | collective-permute-start | bytes 1572872 | tf_op jit(solution)/shard_map/ppermute | solution.py:172
  6.6 1.1 convert_bitcast_fusion
  8.5 2.6 %collective-permute-start.4 = (bf16[2,64,1152]{2,1,0:T(8,128)(2,1)}, bf16[2,64,1152]{2,1,0:T(8,128)(2,1)S(1)}, u32[]{:S(2)}, u32[]{:S(2)}) collective-permute-start(bf16[2,64,1152]{2,1,0:T(8,128)(2,1)} %pad_maximum_fusion.2), channel_id=1, source_target_pairs={{0,24},{8,16},{16,8},{24,0},{1,25},{9,17},{17,9},{25,1},{2,26},{10... | collective-permute-start | bytes 884744 | tf_op jit(solution)/shard_map/ppermute | solution.py:178
  18.4 1.3 %gather_fusion = s32[8]{0:T(128)S(1)} fusion(s32[4]{0:T(128)} %constant.144.clone, s32[1024]{0:T(1024)S(1)} %pad_clamp_fusion), kind=kCustom, calls=%fused_computation | custom fusion | bytes 96 | tf_op jit(solution)/shard_map/gather | solution.py:259
  19.9 4.5 %collective-permute-done.3 = bf16[2,64,1152]{2,1,0:T(8,128)(2,1)S(1)} collective-permute-done((bf16[2,64,1152]{2,1,0:T(8,128)(2,1)}, bf16[2,64,1152]{2,1,0:T(8,128)(2,1)S(1)}, u32[]{:S(2)}, u32[]{:S(2)}) %collective-permute-start.3) | collective-permute-done | bytes 294944 | tf_op jit(solution)/shard_map/ppermute | solution.py:178
  24.7 3.8 %collective-permute-done.1 = bf16[1024,256]{1,0:T(8,128)(2,1)S(1)} collective-permute-done((bf16[1024,256]{1,0:T(8,128)(2,1)}, bf16[1024,256]{1,0:T(8,128)(2,1)S(1)}, u32[]{:S(2)}, u32[]{:S(2)}) %collective-permute-start.1) | collective-permute-done | bytes 524320 | tf_op jit(solution)/shard_map/ppermute | solution.py:172
  28.5 1.1 collective-permute-start.8
  31.1 2.4 %collective-permute-done.19 = bf16[128,1152]{1,0:T(8,128)(2,1)S(1)} collective-permute-done((bf16[128,1152]{1,0:T(8,128)(2,1)S(1)}, bf16[128,1152]{1,0:T(8,128)(2,1)S(1)}, u32[]{:S(2)}, u32[]{:S(2)}) %collective-permute-start.19) | collective-permute-done | bytes 294944 | tf_op jit(solution)/shard_map/ppermute | solution.py:175
  34.3 1.6 %collective-permute-start.10 = (bf16[2,64,1152]{2,1,0:T(8,128)(2,1)S(1)}, bf16[2,64,1152]{2,1,0:T(8,128)(2,1)S(1)}, u32[]{:S(2)}, u32[]{:S(2)}) collective-permute-start(bf16[2,64,1152]{2,1,0:T(8,128)(2,1)S(1)} %pad_maximum_fusion.4), channel_id=1, source_target_pairs={{0,8},{8,0},{16,24},{24,16},{1,9},{9,1},{17,25},{25,17},{2,10},{10... | collective-permute-start | bytes 884744 | tf_op jit(solution)/shard_map/ppermute | solution.py:178
  35.8 1.5 %collective-permute-start.11 = (bf16[2,64,1152]{2,1,0:T(8,128)(2,1)S(1)}, bf16[2,64,1152]{2,1,0:T(8,128)(2,1)S(1)}, u32[]{:S(2)}, u32[]{:S(2)}) collective-permute-start(bf16[2,64,1152]{2,1,0:T(8,128)(2,1)S(1)} %pad_maximum_fusion.4), channel_id=1, source_target_pairs={{0,16},{8,24},{16,0},{24,8},{1,17},{9,25},{17,1},{25,9},{2,18},{10... | collective-permute-start | bytes 884744 | tf_op jit(solution)/shard_map/ppermute | solution.py:178
  37.8 1.6 %reorder.1 = bf16[256,8192]{1,0:T(8,128)(2,1)S(1)} custom-call(s32[8]{0:T(128)S(1)} %stack.77.pos_ref, bf16[256,8192]{1,0:T(8,128)(2,1)S(1)} %copy-done), custom_call_target="tpu_custom_call" | custom-call | bytes 134217728 | tf_op jit(solution)/shard_map/reorder/pallas_call | solution.py:152
  41.6 8.3 %collective-permute-done.9 = bf16[128,1152]{1,0:T(8,128)(2,1)S(1)} collective-permute-done((bf16[128,1152]{1,0:T(8,128)(2,1)S(1)}, bf16[128,1152]{1,0:T(8,128)(2,1)S(1)}, u32[]{:S(2)}, u32[]{:S(2)}) %collective-permute-start.9) | collective-permute-done | bytes 294944 | tf_op jit(solution)/shard_map/ppermute | solution.py:172
  50.6 1.6 %collective-permute-start.18 = (bf16[128,1152]{1,0:T(8,128)(2,1)S(1)}, bf16[128,1152]{1,0:T(8,128)(2,1)S(1)}, u32[]{:S(2)}, u32[]{:S(2)}) collective-permute-start(bf16[128,1152]{1,0:T(8,128)(2,1)S(1)} %collective-permute-done.9), channel_id=1, source_target_pairs={{0,2},{1,3},{2,4},{3,5},{4,6},{5,7},{6,0},{7,1},{8,10},{9,11},{10,... | collective-permute-start | bytes 884744 | tf_op jit(solution)/shard_map/ppermute | solution.py:172
  52.7 2.2 %collective-permute-start.17 = (bf16[128,1152]{1,0:T(8,128)(2,1)S(1)}, bf16[128,1152]{1,0:T(8,128)(2,1)S(1)}, u32[]{:S(2)}, u32[]{:S(2)}) collective-permute-start(bf16[128,1152]{1,0:T(8,128)(2,1)S(1)} %bitcast.79), channel_id=1, source_target_pairs={{0,6},{1,7},{2,0},{3,1},{4,2},{5,3},{6,4},{7,5},{8,14},{9,15},{10,... | collective-permute-start | bytes 884744 | tf_op jit(solution)/shard_map/ppermute | solution.py:172
  56.6 1.8 %collective-permute-start.16 = (bf16[256,256]{1,0:T(8,128)(2,1)S(1)}, bf16[256,256]{1,0:T(8,128)(2,1)S(1)}, u32[]{:S(2)}, u32[]{:S(2)}) collective-permute-start(bf16[256,256]{1,0:T(8,128)(2,1)S(1)} %fusion.7), channel_id=1, source_target_pairs={{0,24},{8,16},{16,8},{24,0},{1,25},{9,17},{17,9},{25,1},{2,26},{10... | collective-permute-start | bytes 393224 | tf_op jit(solution)/shard_map/ppermute | solution.py:178
  60.2 3.6 %collective-permute-done.16 = bf16[256,256]{1,0:T(8,128)(2,1)S(1)} collective-permute-done((bf16[256,256]{1,0:T(8,128)(2,1)S(1)}, bf16[256,256]{1,0:T(8,128)(2,1)S(1)}, u32[]{:S(2)}, u32[]{:S(2)}) %collective-permute-start.16) | collective-permute-done | bytes 131104 | tf_op jit(solution)/shard_map/ppermute | solution.py:178
  63.8 1.7 %collective-permute-done.15 = bf16[256,256]{1,0:T(8,128)(2,1)S(1)} collective-permute-done((bf16[256,256]{1,0:T(8,128)(2,1)S(1)}, bf16[256,256]{1,0:T(8,128)(2,1)S(1)}, u32[]{:S(2)}, u32[]{:S(2)}) %collective-permute-start.15) | collective-permute-done | bytes 131104 | tf_op jit(solution)/shard_map/ppermute | solution.py:178
  69.2 18.7 %attention.1 = (bf16[256,128]{1,0:T(8,128)(2,1)S(1)}, f32[8,2,64,128]{3,2,1,0:T(8,128)S(1)}) custom-call(s32[9]{0:T(128)S(1)} %pad_add_fusion.pos_ref, bf16[256,8192]{1,0:T(8,128)(2,1)S(1)} %copy-done.1, bf16[256,8192]{1,0:T(8,128)(2,1)S(1)} %copy-done.2, bf16[256,1024]{1,0:T(8,128)(2,1)S(1)} %copy-done.3, ...), custom_call_target="tpu_custom_call" | custom-call | flops 10000000000 | bytes 20000000 | tf_op jit(solution)/shard_map/attention/pallas_call | solution.py:95
  87.9 1.8 %gradients.3 = bf16[4,2,64,1152]{3,2,1,0:T(8,128)(2,1)S(1)} custom-call(s32[4]{0:T(128)S(1)} %add_subtract_fusion.pos_ref, bf16[256,8192]{1,0:T(8,128)(2,1)S(1)} %copy-done, bf16[256,128]{1,0:T(8,128)(2,1)S(1)} %get-tuple-element.58.lg_ref, f32[8,2,64,128]{3,2,1,0:T(8,128)S(1)} %get-tuple-element.59.rt_ref), custom_call_target="tpu_custom_call" | custom-call | flops 268435456 | bytes 3000000 | tf_op jit(solution)/shard_map/gradients/pallas_call | solution.py:132
  90.1 1.8 %gradients.2 = f32[4,2,64,1152]{3,2,1,0:T(8,128)S(1)} custom-call(s32[4]{0:T(128)S(1)} %broadcast_add_fusion.pos_ref, bf16[256,8192]{1,0:T(8,128)(2,1)S(1)} %copy-done, bf16[256,128]{1,0:T(8,128)(2,1)S(1)} %get-tuple-element.58.lg_ref, f32[8,2,64,128]{3,2,1,0:T(8,128)S(1)} %get-tuple-element.59.rt_ref), custom_call_target="tpu_custom_call" | custom-call | flops 268435456 | bytes 3000000 | tf_op jit(solution)/shard_map/gradients/pallas_call | solution.py:132
  92.9 1.7 %collective-permute-start.26 = (bf16[2,64,1152]{2,1,0:T(8,128)(2,1)S(1)}, bf16[2,64,1152]{2,1,0:T(8,128)(2,1)S(1)}, u32[]{:S(2)}, u32[]{:S(2)}) collective-permute-start(bf16[2,64,1152]{2,1,0:T(8,128)(2,1)S(1)} %get-tuple-element.65), channel_id=1, source_target_pairs={{0,6},{1,7},{2,0},{3,1},{4,2},{5,3},{6,4},{7,5},{8,14},{9,15},{10,... | collective-permute-start | bytes 884744 | tf_op jit(solution)/shard_map/ppermute | solution.py:172
  95.7 6.8 %collective-permute-done.26 = bf16[2,64,1152]{2,1,0:T(8,128)(2,1)S(1)} collective-permute-done((bf16[2,64,1152]{2,1,0:T(8,128)(2,1)S(1)}, bf16[2,64,1152]{2,1,0:T(8,128)(2,1)S(1)}, u32[]{:S(2)}, u32[]{:S(2)}) %collective-permute-start.26) | collective-permute-done | bytes 294944 | tf_op jit(solution)/shard_map/ppermute | solution.py:172
  102.4 18.8 %collective-permute-done.25 = bf16[2,64,1152]{2,1,0:T(8,128)(2,1)S(1)} collective-permute-done((bf16[2,64,1152]{2,1,0:T(8,128)(2,1)S(1)}, bf16[2,64,1152]{2,1,0:T(8,128)(2,1)S(1)}, u32[]{:S(2)}, u32[]{:S(2)}) %collective-permute-start.25) | collective-permute-done | bytes 294944 | tf_op jit(solution)/shard_map/ppermute | solution.py:172
  (109 shorter events, 21.4 us)
Async XLA Ops:
  0.6 24.1 %collective-permute-start = (bf16[1024,256]{1,0:T(8,128)(2,1)}, bf16[1024,256]{1,0:T(8,128)(2,1)S(1)}, u32[]{:S(2)}, u32[]{:S(2)}) collective-permute-start(bf16[1024,256]{1,0:T(8,128)(2,1)} %param.16), channel_id=1, source_target_pairs={{0,2},{1,3},{2,4},{3,5},{4,6},{5,7},{6,0},{7,1},{8,10},{9,11},{10,... | collective-permute-start | bytes 1572872 | tf_op jit(solution)/shard_map/ppermute | solution.py:172
  3.7 24.8 %collective-permute-start.1 = (bf16[1024,256]{1,0:T(8,128)(2,1)}, bf16[1024,256]{1,0:T(8,128)(2,1)S(1)}, u32[]{:S(2)}, u32[]{:S(2)}) collective-permute-start(bf16[1024,256]{1,0:T(8,128)(2,1)} %param.16), channel_id=1, source_target_pairs={{0,6},{1,7},{2,0},{3,1},{4,2},{5,3},{6,4},{7,5},{8,14},{9,15},{10,... | collective-permute-start | bytes 1572872 | tf_op jit(solution)/shard_map/ppermute | solution.py:172
  8.5 11.4 %collective-permute-start.4 = (bf16[2,64,1152]{2,1,0:T(8,128)(2,1)}, bf16[2,64,1152]{2,1,0:T(8,128)(2,1)S(1)}, u32[]{:S(2)}, u32[]{:S(2)}) collective-permute-start(bf16[2,64,1152]{2,1,0:T(8,128)(2,1)} %pad_maximum_fusion.2), channel_id=1, source_target_pairs={{0,24},{8,16},{16,8},{24,0},{1,25},{9,17},{17,9},{25,1},{2,26},{10... | collective-permute-start | bytes 884744 | tf_op jit(solution)/shard_map/ppermute | solution.py:178
  11.1 13.3 %collective-permute-start.3 = (bf16[2,64,1152]{2,1,0:T(8,128)(2,1)}, bf16[2,64,1152]{2,1,0:T(8,128)(2,1)S(1)}, u32[]{:S(2)}, u32[]{:S(2)}) collective-permute-start(bf16[2,64,1152]{2,1,0:T(8,128)(2,1)} %pad_maximum_fusion.2), channel_id=1, source_target_pairs={{0,16},{8,24},{16,0},{24,8},{1,17},{9,25},{17,1},{25,9},{2,18},{10... | collective-permute-start | bytes 884744 | tf_op jit(solution)/shard_map/ppermute | solution.py:178
  11.6 12.9 %collective-permute-start.2 = (bf16[2,64,1152]{2,1,0:T(8,128)(2,1)}, bf16[2,64,1152]{2,1,0:T(8,128)(2,1)S(1)}, u32[]{:S(2)}, u32[]{:S(2)}) collective-permute-start(bf16[2,64,1152]{2,1,0:T(8,128)(2,1)} %pad_maximum_fusion.2), channel_id=1, source_target_pairs={{0,8},{8,0},{16,24},{24,16},{1,9},{9,1},{17,25},{25,17},{2,10},{10... | collective-permute-start | bytes 884744 | tf_op jit(solution)/shard_map/ppermute | solution.py:178
  28.5 21.3 %collective-permute-start.8 = (bf16[1024,256]{1,0:T(8,128)(2,1)S(1)}, bf16[1024,256]{1,0:T(8,128)(2,1)S(1)}, u32[]{:S(2)}, u32[]{:S(2)}) collective-permute-start(bf16[1024,256]{1,0:T(8,128)(2,1)S(1)} %collective-permute-done), channel_id=1, source_target_pairs={{0,2},{1,3},{2,4},{3,5},{4,6},{5,7},{6,0},{7,1},{8,10},{9,11},{10,... | collective-permute-start | bytes 1572872 | tf_op jit(solution)/shard_map/ppermute | solution.py:172
  29.7 4.6 %collective-permute-start.6 = (bf16[1024,256]{1,0:T(8,128)(2,1)S(1)}, bf16[1024,256]{1,0:T(8,128)(2,1)S(1)}, u32[]{:S(2)}, u32[]{:S(2)}) collective-permute-start(bf16[1024,256]{1,0:T(8,128)(2,1)S(1)} %collective-permute-done), channel_id=1, source_target_pairs={{0,1},{1,0},{2,3},{3,2},{4,5},{5,4},{6,7},{7,6},{8,9},{9,8},{10,11... | collective-permute-start | bytes 1572872 | tf_op jit(solution)/shard_map/ppermute | solution.py:175
  30.0 4.3 %collective-permute-start.5 = (bf16[1024,256]{1,0:T(8,128)(2,1)S(1)}, bf16[1024,256]{1,0:T(8,128)(2,1)S(1)}, u32[]{:S(2)}, u32[]{:S(2)}) collective-permute-start(bf16[1024,256]{1,0:T(8,128)(2,1)S(1)} %copy-done.6), channel_id=1, source_target_pairs={{0,1},{1,0},{2,3},{3,2},{4,5},{5,4},{6,7},{7,6},{8,9},{9,8},{10,11... | collective-permute-start | bytes 1572872 | tf_op jit(solution)/shard_map/ppermute | solution.py:175
  30.5 3.7 %collective-permute-start.7 = (bf16[1024,256]{1,0:T(8,128)(2,1)S(1)}, bf16[1024,256]{1,0:T(8,128)(2,1)S(1)}, u32[]{:S(2)}, u32[]{:S(2)}) collective-permute-start(bf16[1024,256]{1,0:T(8,128)(2,1)S(1)} %collective-permute-done.1), channel_id=1, source_target_pairs={{0,1},{1,0},{2,3},{3,2},{4,5},{5,4},{6,7},{7,6},{8,9},{9,8},{10,11... | collective-permute-start | bytes 1572872 | tf_op jit(solution)/shard_map/ppermute | solution.py:175
  33.5 16.4 %collective-permute-start.9 = (bf16[128,1152]{1,0:T(8,128)(2,1)S(1)}, bf16[128,1152]{1,0:T(8,128)(2,1)S(1)}, u32[]{:S(2)}, u32[]{:S(2)}) collective-permute-start(bf16[128,1152]{1,0:T(8,128)(2,1)S(1)} %bitcast.77), channel_id=1, source_target_pairs={{0,2},{1,3},{2,4},{3,5},{4,6},{5,7},{6,0},{7,1},{8,10},{9,11},{10,... | collective-permute-start | bytes 884744 | tf_op jit(solution)/shard_map/ppermute | solution.py:172
  34.3 15.6 %collective-permute-start.10 = (bf16[2,64,1152]{2,1,0:T(8,128)(2,1)S(1)}, bf16[2,64,1152]{2,1,0:T(8,128)(2,1)S(1)}, u32[]{:S(2)}, u32[]{:S(2)}) collective-permute-start(bf16[2,64,1152]{2,1,0:T(8,128)(2,1)S(1)} %pad_maximum_fusion.4), channel_id=1, source_target_pairs={{0,8},{8,0},{16,24},{24,16},{1,9},{9,1},{17,25},{25,17},{2,10},{10... | collective-permute-start | bytes 884744 | tf_op jit(solution)/shard_map/ppermute | solution.py:178
  35.8 14.8 %collective-permute-start.11 = (bf16[2,64,1152]{2,1,0:T(8,128)(2,1)S(1)}, bf16[2,64,1152]{2,1,0:T(8,128)(2,1)S(1)}, u32[]{:S(2)}, u32[]{:S(2)}) collective-permute-start(bf16[2,64,1152]{2,1,0:T(8,128)(2,1)S(1)} %pad_maximum_fusion.4), channel_id=1, source_target_pairs={{0,16},{8,24},{16,0},{24,8},{1,17},{9,25},{17,1},{25,9},{2,18},{10... | collective-permute-start | bytes 884744 | tf_op jit(solution)/shard_map/ppermute | solution.py:178
  37.3 13.3 %collective-permute-start.12 = (bf16[2,64,1152]{2,1,0:T(8,128)(2,1)S(1)}, bf16[2,64,1152]{2,1,0:T(8,128)(2,1)S(1)}, u32[]{:S(2)}, u32[]{:S(2)}) collective-permute-start(bf16[2,64,1152]{2,1,0:T(8,128)(2,1)S(1)} %pad_maximum_fusion.4), channel_id=1, source_target_pairs={{0,24},{8,16},{16,8},{24,0},{1,25},{9,17},{17,9},{25,1},{2,26},{10... | collective-permute-start | bytes 884744 | tf_op jit(solution)/shard_map/ppermute | solution.py:178
  50.6 15.8 %collective-permute-start.18 = (bf16[128,1152]{1,0:T(8,128)(2,1)S(1)}, bf16[128,1152]{1,0:T(8,128)(2,1)S(1)}, u32[]{:S(2)}, u32[]{:S(2)}) collective-permute-start(bf16[128,1152]{1,0:T(8,128)(2,1)S(1)} %collective-permute-done.9), channel_id=1, source_target_pairs={{0,2},{1,3},{2,4},{3,5},{4,6},{5,7},{6,0},{7,1},{8,10},{9,11},{10,... | collective-permute-start | bytes 884744 | tf_op jit(solution)/shard_map/ppermute | solution.py:172
  52.2 3.4 %collective-permute-start.20 = (bf16[128,1152]{1,0:T(8,128)(2,1)S(1)}, bf16[128,1152]{1,0:T(8,128)(2,1)S(1)}, u32[]{:S(2)}, u32[]{:S(2)}) collective-permute-start(bf16[128,1152]{1,0:T(8,128)(2,1)S(1)} %collective-permute-done.9), channel_id=1, source_target_pairs={{0,1},{1,0},{2,3},{3,2},{4,5},{5,4},{6,7},{7,6},{8,9},{9,8},{10,11... | collective-permute-start | bytes 884744 | tf_op jit(solution)/shard_map/ppermute | solution.py:175
  52.2 3.7 %collective-permute-start.13 = (bf16[1024,256]{1,0:T(8,128)(2,1)S(1)}, bf16[1024,256]{1,0:T(8,128)(2,1)S(1)}, u32[]{:S(2)}, u32[]{:S(2)}) collective-permute-start(bf16[1024,256]{1,0:T(8,128)(2,1)S(1)} %collective-permute-done.8), channel_id=1, source_target_pairs={{0,1},{1,0},{2,3},{3,2},{4,5},{5,4},{6,7},{7,6},{8,9},{9,8},{10,11... | collective-permute-start | bytes 1572872 | tf_op jit(solution)/shard_map/ppermute | solution.py:175
  52.7 13.7 %collective-permute-start.17 = (bf16[128,1152]{1,0:T(8,128)(2,1)S(1)}, bf16[128,1152]{1,0:T(8,128)(2,1)S(1)}, u32[]{:S(2)}, u32[]{:S(2)}) collective-permute-start(bf16[128,1152]{1,0:T(8,128)(2,1)S(1)} %bitcast.79), channel_id=1, source_target_pairs={{0,6},{1,7},{2,0},{3,1},{4,2},{5,3},{6,4},{7,5},{8,14},{9,15},{10,... | collective-permute-start | bytes 884744 | tf_op jit(solution)/shard_map/ppermute | solution.py:172
  56.6 7.2 %collective-permute-start.16 = (bf16[256,256]{1,0:T(8,128)(2,1)S(1)}, bf16[256,256]{1,0:T(8,128)(2,1)S(1)}, u32[]{:S(2)}, u32[]{:S(2)}) collective-permute-start(bf16[256,256]{1,0:T(8,128)(2,1)S(1)} %fusion.7), channel_id=1, source_target_pairs={{0,24},{8,16},{16,8},{24,0},{1,25},{9,17},{17,9},{25,1},{2,26},{10... | collective-permute-start | bytes 393224 | tf_op jit(solution)/shard_map/ppermute | solution.py:178
  58.4 7.1 %collective-permute-start.15 = (bf16[256,256]{1,0:T(8,128)(2,1)S(1)}, bf16[256,256]{1,0:T(8,128)(2,1)S(1)}, u32[]{:S(2)}, u32[]{:S(2)}) collective-permute-start(bf16[256,256]{1,0:T(8,128)(2,1)S(1)} %fusion.7), channel_id=1, source_target_pairs={{0,16},{8,24},{16,0},{24,8},{1,17},{9,25},{17,1},{25,9},{2,18},{10... | collective-permute-start | bytes 393224 | tf_op jit(solution)/shard_map/ppermute | solution.py:178
  59.4 6.2 %collective-permute-start.14 = (bf16[256,256]{1,0:T(8,128)(2,1)S(1)}, bf16[256,256]{1,0:T(8,128)(2,1)S(1)}, u32[]{:S(2)}, u32[]{:S(2)}) collective-permute-start(bf16[256,256]{1,0:T(8,128)(2,1)S(1)} %fusion.7), channel_id=1, source_target_pairs={{0,8},{8,0},{16,24},{24,16},{1,9},{9,1},{17,25},{25,17},{2,10},{10... | collective-permute-start | bytes 393224 | tf_op jit(solution)/shard_map/ppermute | solution.py:178
  89.7 2.9 %collective-permute-start.23 = (bf16[4,2,64,1152]{3,2,1,0:T(8,128)(2,1)S(1)}, bf16[4,2,64,1152]{3,2,1,0:T(8,128)(2,1)S(1)}, u32[]{:S(2)}, u32[]{:S(2)}) collective-permute-start(bf16[4,2,64,1152]{3,2,1,0:T(8,128)(2,1)S(1)} %gradients.3), channel_id=1, source_target_pairs={{0,1},{1,0},{2,3},{3,2},{4,5},{5,4},{6,7},{7,6},{8,9},{9,8},{10,11... | collective-permute-start | bytes 3538952 | tf_op jit(solution)/shard_map/ppermute | solution.py:175
  92.9 9.5 %collective-permute-start.26 = (bf16[2,64,1152]{2,1,0:T(8,128)(2,1)S(1)}, bf16[2,64,1152]{2,1,0:T(8,128)(2,1)S(1)}, u32[]{:S(2)}, u32[]{:S(2)}) collective-permute-start(bf16[2,64,1152]{2,1,0:T(8,128)(2,1)S(1)} %get-tuple-element.65), channel_id=1, source_target_pairs={{0,6},{1,7},{2,0},{3,1},{4,2},{5,3},{6,4},{7,5},{8,14},{9,15},{10,... | collective-permute-start | bytes 884744 | tf_op jit(solution)/shard_map/ppermute | solution.py:172
  94.6 26.6 %collective-permute-start.25 = (bf16[2,64,1152]{2,1,0:T(8,128)(2,1)S(1)}, bf16[2,64,1152]{2,1,0:T(8,128)(2,1)S(1)}, u32[]{:S(2)}, u32[]{:S(2)}) collective-permute-start(bf16[2,64,1152]{2,1,0:T(8,128)(2,1)S(1)} %get-tuple-element.66), channel_id=1, source_target_pairs={{0,4},{1,5},{2,6},{3,7},{4,0},{5,1},{6,2},{7,3},{8,12},{9,13},{10,... | collective-permute-start | bytes 884744 | tf_op jit(solution)/shard_map/ppermute | solution.py:172
  95.0 26.2 %collective-permute-start.24 = (bf16[2,64,1152]{2,1,0:T(8,128)(2,1)S(1)}, bf16[2,64,1152]{2,1,0:T(8,128)(2,1)S(1)}, u32[]{:S(2)}, u32[]{:S(2)}) collective-permute-start(bf16[2,64,1152]{2,1,0:T(8,128)(2,1)S(1)} %get-tuple-element.64), channel_id=1, source_target_pairs={{0,2},{1,3},{2,4},{3,5},{4,6},{5,7},{6,0},{7,1},{8,10},{9,11},{10,... | collective-permute-start | bytes 884744 | tf_op jit(solution)/shard_map/ppermute | solution.py:172
  (13 other events, 163.7 us)

commit v4 on v3

--- a/solution.py
+++ b/solution.py
@@ -24,47 +24,49 @@
         acc_ref[...] = jnp.zeros_like(acc_ref)
 
     per_head = HD // b_ref.shape[2]
-    b = jnp.concatenate([b_ref[pos_ref[1 + step * per_head + i]] for i in range(per_head)], axis=1)
-    b = [b[c * RANK:(c + 1) * RANK] for c in range(nchain)]
-    lr = [lr_ref[:, c * RANK:(c + 1) * RANK] for c in range(nchain)]
-    keys = [(base_ref[0].astype(f32) + scale * dot(lr[c], b[c], NN)).astype(bf16) for c in range(nchain)]
-    keys = [jnp.concatenate([x[j * 128:(j + 1) * 128] for x in keys], axis=0) for j in range(nb)]
     row = lax.broadcasted_iota(jnp.int32, (128, 128), 0)
     col = lax.broadcasted_iota(jnp.int32, (128, 128), 1)
     future = row > col
-    v = v_ref[...]
-    kg = [jnp.zeros((nchain * 128, HD), f32) for _ in range(nb)]
-    for h0 in range(0, group, pair):
-        def heads(ref, j):
-            return jnp.concatenate([ref[j * 128:, (h0 + h) * HD:(h0 + h + 1) * HD] for h in range(pair)], axis=0)
-
-        qs = [heads(q_ref, j) for j in range(nb)]
-        dp = [dot(v[j * 128:(j + 1) * 128], heads(do_ref, j), NT) for j in range(nb)]
-        s = [dot(keys[j], qs[j], NT) for j in range(nb)]
-        ds = [[[None] * (pair * (nb - j)) for _ in range(nchain)] for j in range(nb)]
-        for h in range(pair):
-            for c in range(nchain):
-                for i in range(nb):
-                    def at(x, j, c):
-                        k = h * (nb - j) + i - j
-                        return x[j][c * 128:(c + 1) * 128, k * 128:(k + 1) * 128]
-
-                    blocks = [at(s, j, c) for j in range(i + 1)]
-                    blocks[i] = jnp.where(future, -1e30, blocks[i])
-                    top = jnp.max(functools.reduce(jnp.maximum, blocks), axis=0, keepdims=True)
-                    e = [jnp.exp2((x - top) * (ss * LOG2E)) for x in blocks]
-                    d = [at(dp, j, 0) for j in range(i + 1)]
-                    r = 1.0 / jnp.sum(functools.reduce(jnp.add, e), axis=0, keepdims=True)
-                    center = r * jnp.sum(functools.reduce(jnp.add, [x * y for x, y in zip(e, d)]), axis=0, keepdims=True)
-                    for j in range(i + 1):
-                        ds[j][c][h * (nb - j) + i - j] = ((e[j] * r) * (d[j] - center)).astype(bf16)
-        for j in range(nb):
-            dsj = jnp.concatenate([jnp.concatenate(x, axis=1) for x in ds[j]], axis=0)
-            kg[j] = kg[j] + dot(dsj, qs[j], NN)
-    for c in range(nchain):
-        g = (jnp.concatenate([x[c * 128:(c + 1) * 128] for x in kg], axis=0) * ss).astype(bf16)
-        acc_ref[:, c * RANK:(c + 1) * RANK] += dot(g, b[c], NT)
-        rt_ref[0, c] = scale * dot(lr[c], g, TN)
+    heads_here = v_ref.shape[1] // HD
+    for n in range(heads_here):
+        b = jnp.concatenate([b_ref[pos_ref[1 + (step * heads_here + n) * per_head + i]] for i in range(per_head)], axis=1)
+        b = [b[c * RANK:(c + 1) * RANK] for c in range(nchain)]
+        lr = [lr_ref[:, c * RANK:(c + 1) * RANK] for c in range(nchain)]
+        keys = [(base_ref[0, :, n * HD:(n + 1) * HD].astype(f32) + scale * dot(lr[c], b[c], NN)).astype(bf16) for c in range(nchain)]
+        keys = [jnp.concatenate([x[j * 128:(j + 1) * 128] for x in keys], axis=0) for j in range(nb)]
+        v = v_ref[:, n * HD:(n + 1) * HD]
+        kg = [jnp.zeros((nchain * 128, HD), f32) for _ in range(nb)]
+        for h0 in range(0, group, pair):
+            def heads(ref, j):
+                return jnp.concatenate([ref[j * 128:, (n * group + h0 + h) * HD:(n * group + h0 + h + 1) * HD] for h in range(pair)], axis=0)
+
+            qs = [heads(q_ref, j) for j in range(nb)]
+            dp = [dot(v[j * 128:(j + 1) * 128], heads(do_ref, j), NT) for j in range(nb)]
+            s = [dot(keys[j], qs[j], NT) for j in range(nb)]
+            ds = [[[None] * (pair * (nb - j)) for _ in range(nchain)] for j in range(nb)]
+            for h in range(pair):
+                for c in range(nchain):
+                    for i in range(nb):
+                        def at(x, j, c):
+                            k = h * (nb - j) + i - j
+                            return x[j][c * 128:(c + 1) * 128, k * 128:(k + 1) * 128]
+
+                        blocks = [at(s, j, c) for j in range(i + 1)]
+                        blocks[i] = jnp.where(future, -1e30, blocks[i])
+                        top = jnp.max(functools.reduce(jnp.maximum, blocks), axis=0, keepdims=True)
+                        e = [jnp.exp2((x - top) * (ss * LOG2E)) for x in blocks]
+                        d = [at(dp, j, 0) for j in range(i + 1)]
+                        r = 1.0 / jnp.sum(functools.reduce(jnp.add, e), axis=0, keepdims=True)
+                        center = r * jnp.sum(functools.reduce(jnp.add, [x * y for x, y in zip(e, d)]), axis=0, keepdims=True)
+                        for j in range(i + 1):
+                            ds[j][c][h * (nb - j) + i - j] = ((e[j] * r) * (d[j] - center)).astype(bf16)
+            for j in range(nb):
+                dsj = jnp.concatenate([jnp.concatenate(x, axis=1) for x in ds[j]], axis=0)
+                kg[j] = kg[j] + dot(dsj, qs[j], NN)
+        for c in range(nchain):
+            g = (jnp.concatenate([x[c * 128:(c + 1) * 128] for x in kg], axis=0) * ss).astype(bf16)
+            acc_ref[:, c * RANK:(c + 1) * RANK] += dot(g, b[c], NT)
+            rt_ref[n, c] = scale * dot(lr[c], g, TN)
 
     @pl.when(step == pl.num_programs(0) - 1)
     def _():
@@ -77,25 +79,25 @@
     KH, group = KW // HD, q.shape[1] // KW
     hp = base.shape[2] // HD
     grid = pltpu.PrefetchScalarGridSpec(
-        num_scalar_prefetch=1, grid=(KH,),
+        num_scalar_prefetch=1, grid=(KH // hp,),
         in_specs=[
-            pl.BlockSpec((T, group * HD), lambda g, p: (0, g)),
-            pl.BlockSpec((T, group * HD), lambda g, p: (0, g)),
-            pl.BlockSpec((T, HD), lambda g, p: (0, g)),
-            pl.BlockSpec((1, T, HD), lambda g, p: (p[0] ^ (g // hp), 0, g % hp)),
+            pl.BlockSpec((T, hp * group * HD), lambda g, p: (0, g)),
+            pl.BlockSpec((T, hp * group * HD), lambda g, p: (0, g)),
+            pl.BlockSpec((T, hp * HD), lambda g, p: (0, g)),
+            pl.BlockSpec((1, T, hp * HD), lambda g, p: (p[0] ^ g, 0, 0)),
             pl.BlockSpec(lr.shape, lambda g, p: (0, 0)),
             pl.BlockSpec(b.shape, lambda g, p: (0, 0, 0)),
         ],
         out_specs=[
             pl.BlockSpec(lr.shape, lambda g, p: (0, 0)),
-            pl.BlockSpec((1, nchain, RANK, HD), lambda g, p: (g, 0, 0, 0)),
+            pl.BlockSpec((hp, nchain, RANK, HD), lambda g, p: (g, 0, 0, 0)),
         ],
         scratch_shapes=[pltpu.VMEM(lr.shape, f32)],
     )
     return pl.pallas_call(
         functools.partial(attention_kernel, scale, nchain, group, pair), grid_spec=grid,
         out_shape=[jax.ShapeDtypeStruct(lr.shape, bf16), jax.ShapeDtypeStruct((KH, nchain, RANK, HD), f32)],
-        compiler_params=pltpu.CompilerParams(vmem_limit_bytes=28 * 1024 * 1024),
+        compiler_params=pltpu.CompilerParams(vmem_limit_bytes=40 * 1024 * 1024),
         cost_estimate=pl.CostEstimate(flops=10_000_000_000, bytes_accessed=20_000_000, transcendentals=T * T * 64 * nchain),
         name="attention",
     )(pos, q, do, v, base, lr, b)
@@ -268,7 +270,7 @@
     mine = gradients(around * 2 + core, layer_activations, low_grad, right, nz, f32)
     total = mine[0] + theirs[0]
     send = (mine[1:] + theirs[1:]).astype(bf16)
-    for k in range(1, nz):
+    for k in sorted(range(1, nz), key=lambda k: min(k, nz - k)):
         total = total + shift(send[k - 1], k).astype(f32)
     new = rest.astype(f32) - STRIDE_LENGTH * total
     return new[:, :, :arows].transpose(0, 2, 1), new[:, :, arows:]

time: 123 us -> 121 us (0.984)
  the two profiles are of different devices: /device:TPU:0 before, /device:TPU:8 now
where the time goes in v4:
time: 121 us
  waiting for transfers between devices  55 us (45%)
  starting transfers between devices  23.3 us (19%)
  Pallas kernels  23 us (19%)
  between operations  6.09 us (5%)
  matrix products  4.93 us (4%)
  local copies, waits for them, and re-layouts  4.56 us (4%)
  other arithmetic  3.69 us (3%)
    ppermute x9, waiting for transfers between devices, shift(): return lax.ppermute(x, 'tok', [(i, (i + 2 * k) % nt) for i in range(nt)])  38.1 us
    pallas_call x1, Pallas kernels, attention(): pl.pallas_call(functools.partial(attention_kernel, scale, nchain, group,...  17.9 us
    ppermute x9, waiting for transfers between devices, exchange(): return lax.ppermute(x, 'chain', [(i, i ^ k) for i in range(nc)])  12.6 us
    ppermute x9, starting transfers between devices, exchange(): return lax.ppermute(x, 'chain', [(i, i ^ k) for i in range(nc)])  10.6 us
    ppermute x9, starting transfers between devices, shift(): return lax.ppermute(x, 'tok', [(i, (i + 2 * k) % nt) for i in range(nt)])  10.2 us
    dot_general x16, matrix products, dot(): return lax.dot_general(a, b, dims, preferred_element_type=f32)  4.93 us
    ppermute x9, waiting for transfers between devices, swap_cores(): return lax.ppermute(x, 'tok', [(i, i ^ 1) for i in range(nt)])  4.28 us
    pallas_call x2, Pallas kernels, gradients(): pl.pallas_call(functools.partial(gradient_kernel, n, nrank), grid_spec=gr...  3.54 us
  transfers between devices with their start and end apart: 27, of which 15 were waited for; matrix products, arithmetic and copies ran while one was open for 9% of the time, Pallas kernels for 3%

profile of v4, /device:TPU:8, one launch (start us, length us, event | category | flops | bytes accessed | tf_op | source)
XLA Modules:
  0.0 120.7 jit_solution(10612516532057406191)
XLA Ops:
  0.6 1.6 %collective-permute-start = (bf16[1024,256]{1,0:T(8,128)(2,1)}, bf16[1024,256]{1,0:T(8,128)(2,1)S(1)}, u32[]{:S(2)}, u32[]{:S(2)}) collective-permute-start(bf16[1024,256]{1,0:T(8,128)(2,1)} %param.16), channel_id=1, source_target_pairs={{0,2},{1,3},{2,4},{3,5},{4,6},{5,7},{6,0},{7,1},{8,10},{9,11},{10,... | collective-permute-start | bytes 1572872 | tf_op jit(solution)/shard_map/ppermute | solution.py:174
  5.4 2.4 %collective-permute-start.4 = (bf16[2,64,1152]{2,1,0:T(8,128)(2,1)}, bf16[2,64,1152]{2,1,0:T(8,128)(2,1)S(1)}, u32[]{:S(2)}, u32[]{:S(2)}) collective-permute-start(bf16[2,64,1152]{2,1,0:T(8,128)(2,1)} %pad_maximum_fusion.2), channel_id=1, source_target_pairs={{0,24},{8,16},{16,8},{24,0},{1,25},{9,17},{17,9},{25,1},{2,26},{10... | collective-permute-start | bytes 884744 | tf_op jit(solution)/shard_map/ppermute | solution.py:180
  15.3 1.3 %gather_fusion = s32[8]{0:T(128)S(1)} fusion(s32[4]{0:T(128)} %constant.144.clone, s32[1024]{0:T(1024)S(1)} %pad_clamp_fusion), kind=kCustom, calls=%fused_computation | custom fusion | bytes 96 | tf_op jit(solution)/shard_map/gather | solution.py:261
  16.8 4.3 %collective-permute-done.3 = bf16[2,64,1152]{2,1,0:T(8,128)(2,1)S(1)} collective-permute-done((bf16[2,64,1152]{2,1,0:T(8,128)(2,1)}, bf16[2,64,1152]{2,1,0:T(8,128)(2,1)S(1)}, u32[]{:S(2)}, u32[]{:S(2)}) %collective-permute-start.3) | collective-permute-done | bytes 294944 | tf_op jit(solution)/shard_map/ppermute | solution.py:180
  21.3 5.3 %collective-permute-done.1 = bf16[1024,256]{1,0:T(8,128)(2,1)S(1)} collective-permute-done((bf16[1024,256]{1,0:T(8,128)(2,1)}, bf16[1024,256]{1,0:T(8,128)(2,1)S(1)}, u32[]{:S(2)}, u32[]{:S(2)}) %collective-permute-start.1) | collective-permute-done | bytes 524320 | tf_op jit(solution)/shard_map/ppermute | solution.py:174
  28.8 2.4 %collective-permute-done.19 = bf16[128,1152]{1,0:T(8,128)(2,1)S(1)} collective-permute-done((bf16[128,1152]{1,0:T(8,128)(2,1)S(1)}, bf16[128,1152]{1,0:T(8,128)(2,1)S(1)}, u32[]{:S(2)}, u32[]{:S(2)}) %collective-permute-start.19) | collective-permute-done | bytes 294944 | tf_op jit(solution)/shard_map/ppermute | solution.py:177
  31.2 1.6 %collective-permute-start.9 = (bf16[128,1152]{1,0:T(8,128)(2,1)S(1)}, bf16[128,1152]{1,0:T(8,128)(2,1)S(1)}, u32[]{:S(2)}, u32[]{:S(2)}) collective-permute-start(bf16[128,1152]{1,0:T(8,128)(2,1)S(1)} %bitcast.77), channel_id=1, source_target_pairs={{0,2},{1,3},{2,4},{3,5},{4,6},{5,7},{6,0},{7,1},{8,10},{9,11},{10,... | collective-permute-start | bytes 884744 | tf_op jit(solution)/shard_map/ppermute | solution.py:174
  32.8 1.6 %collective-permute-start.10 = (bf16[2,64,1152]{2,1,0:T(8,128)(2,1)S(1)}, bf16[2,64,1152]{2,1,0:T(8,128)(2,1)S(1)}, u32[]{:S(2)}, u32[]{:S(2)}) collective-permute-start(bf16[2,64,1152]{2,1,0:T(8,128)(2,1)S(1)} %pad_maximum_fusion.4), channel_id=1, source_target_pairs={{0,8},{8,0},{16,24},{24,16},{1,9},{9,1},{17,25},{25,17},{2,10},{10... | collective-permute-start | bytes 884744 | tf_op jit(solution)/shard_map/ppermute | solution.py:180
  34.4 1.5 %collective-permute-start.11 = (bf16[2,64,1152]{2,1,0:T(8,128)(2,1)S(1)}, bf16[2,64,1152]{2,1,0:T(8,128)(2,1)S(1)}, u32[]{:S(2)}, u32[]{:S(2)}) collective-permute-start(bf16[2,64,1152]{2,1,0:T(8,128)(2,1)S(1)} %pad_maximum_fusion.4), channel_id=1, source_target_pairs={{0,16},{8,24},{16,0},{24,8},{1,17},{9,25},{17,1},{25,9},{2,18},{10... | collective-permute-start | bytes 884744 | tf_op jit(solution)/shard_map/ppermute | solution.py:180
  36.4 1.6 %reorder.1 = bf16[256,8192]{1,0:T(8,128)(2,1)S(1)} custom-call(s32[8]{0:T(128)S(1)} %stack.77.pos_ref, bf16[256,8192]{1,0:T(8,128)(2,1)S(1)} %copy-done), custom_call_target="tpu_custom_call" | custom-call | bytes 134217728 | tf_op jit(solution)/shard_map/reorder/pallas_call | solution.py:154
  40.1 6.7 %collective-permute-done.9 = bf16[128,1152]{1,0:T(8,128)(2,1)S(1)} collective-permute-done((bf16[128,1152]{1,0:T(8,128)(2,1)S(1)}, bf16[128,1152]{1,0:T(8,128)(2,1)S(1)}, u32[]{:S(2)}, u32[]{:S(2)}) %collective-permute-start.9) | collective-permute-done | bytes 294944 | tf_op jit(solution)/shard_map/ppermute | solution.py:174
  46.8 2.4 %collective-permute-done.11 = bf16[2,64,1152]{2,1,0:T(8,128)(2,1)S(1)} collective-permute-done((bf16[2,64,1152]{2,1,0:T(8,128)(2,1)S(1)}, bf16[2,64,1152]{2,1,0:T(8,128)(2,1)S(1)}, u32[]{:S(2)}, u32[]{:S(2)}) %collective-permute-start.11) | collective-permute-done | bytes 294944 | tf_op jit(solution)/shard_map/ppermute | solution.py:180
  49.2 1.5 %collective-permute-start.18 = (bf16[128,1152]{1,0:T(8,128)(2,1)S(1)}, bf16[128,1152]{1,0:T(8,128)(2,1)S(1)}, u32[]{:S(2)}, u32[]{:S(2)}) collective-permute-start(bf16[128,1152]{1,0:T(8,128)(2,1)S(1)} %collective-permute-done.9), channel_id=1, source_target_pairs={{0,2},{1,3},{2,4},{3,5},{4,6},{5,7},{6,0},{7,1},{8,10},{9,11},{10,... | collective-permute-start | bytes 884744 | tf_op jit(solution)/shard_map/ppermute | solution.py:174
  53.7 1.6 %collective-permute-start.16 = (bf16[256,256]{1,0:T(8,128)(2,1)S(1)}, bf16[256,256]{1,0:T(8,128)(2,1)S(1)}, u32[]{:S(2)}, u32[]{:S(2)}) collective-permute-start(bf16[256,256]{1,0:T(8,128)(2,1)S(1)} %fusion.7), channel_id=1, source_target_pairs={{0,24},{8,16},{16,8},{24,0},{1,25},{9,17},{17,9},{25,1},{2,26},{10... | collective-permute-start | bytes 393224 | tf_op jit(solution)/shard_map/ppermute | solution.py:180
  55.2 1.2 collective-permute-start.15
  57.3 3.8 %collective-permute-done.16 = bf16[256,256]{1,0:T(8,128)(2,1)S(1)} collective-permute-done((bf16[256,256]{1,0:T(8,128)(2,1)S(1)}, bf16[256,256]{1,0:T(8,128)(2,1)S(1)}, u32[]{:S(2)}, u32[]{:S(2)}) %collective-permute-start.16) | collective-permute-done | bytes 131104 | tf_op jit(solution)/shard_map/ppermute | solution.py:180
  61.0 2.0 %collective-permute-done.15 = bf16[256,256]{1,0:T(8,128)(2,1)S(1)} collective-permute-done((bf16[256,256]{1,0:T(8,128)(2,1)S(1)}, bf16[256,256]{1,0:T(8,128)(2,1)S(1)}, u32[]{:S(2)}, u32[]{:S(2)}) %collective-permute-start.15) | collective-permute-done | bytes 131104 | tf_op jit(solution)/shard_map/ppermute | solution.py:180
  66.8 17.9 %attention.1 = (bf16[256,128]{1,0:T(8,128)(2,1)S(1)}, f32[8,2,64,128]{3,2,1,0:T(8,128)S(1)}) custom-call(s32[9]{0:T(128)S(1)} %pad_add_fusion.pos_ref, bf16[256,8192]{1,0:T(8,128)(2,1)S(1)} %copy-done.1, bf16[256,8192]{1,0:T(8,128)(2,1)S(1)} %copy-done.2, bf16[256,1024]{1,0:T(8,128)(2,1)S(1)} %copy-done.3, ...), custom_call_target="tpu_custom_call" | custom-call | flops 10000000000 | bytes 20000000 | tf_op jit(solution)/shard_map/attention/pallas_call | solution.py:97
  84.7 1.8 %gradients.3 = bf16[4,2,64,1152]{3,2,1,0:T(8,128)(2,1)S(1)} custom-call(s32[4]{0:T(128)S(1)} %add_subtract_fusion.pos_ref, bf16[256,8192]{1,0:T(8,128)(2,1)S(1)} %copy-done, bf16[256,128]{1,0:T(8,128)(2,1)S(1)} %get-tuple-element.58.lg_ref, f32[8,2,64,128]{3,2,1,0:T(8,128)S(1)} %get-tuple-element.59.rt_ref), custom_call_target="tpu_custom_call" | custom-call | flops 268435456 | bytes 3000000 | tf_op jit(solution)/shard_map/gradients/pallas_call | solution.py:134
  87.0 1.8 %gradients.2 = f32[4,2,64,1152]{3,2,1,0:T(8,128)S(1)} custom-call(s32[4]{0:T(128)S(1)} %broadcast_add_fusion.pos_ref, bf16[256,8192]{1,0:T(8,128)(2,1)S(1)} %copy-done, bf16[256,128]{1,0:T(8,128)(2,1)S(1)} %get-tuple-element.58.lg_ref, f32[8,2,64,128]{3,2,1,0:T(8,128)S(1)} %get-tuple-element.59.rt_ref), custom_call_target="tpu_custom_call" | custom-call | flops 268435456 | bytes 3000000 | tf_op jit(solution)/shard_map/gradients/pallas_call | solution.py:134
  89.8 1.7 %collective-permute-start.26 = (bf16[2,64,1152]{2,1,0:T(8,128)(2,1)S(1)}, bf16[2,64,1152]{2,1,0:T(8,128)(2,1)S(1)}, u32[]{:S(2)}, u32[]{:S(2)}) collective-permute-start(bf16[2,64,1152]{2,1,0:T(8,128)(2,1)S(1)} %get-tuple-element.65), channel_id=1, source_target_pairs={{0,4},{1,5},{2,6},{3,7},{4,0},{5,1},{6,2},{7,3},{8,12},{9,13},{10,... | collective-permute-start | bytes 884744 | tf_op jit(solution)/shard_map/ppermute | solution.py:174
  91.9 1.6 %collective-permute-start.24 = (bf16[2,64,1152]{2,1,0:T(8,128)(2,1)S(1)}, bf16[2,64,1152]{2,1,0:T(8,128)(2,1)S(1)}, u32[]{:S(2)}, u32[]{:S(2)}) collective-permute-start(bf16[2,64,1152]{2,1,0:T(8,128)(2,1)S(1)} %get-tuple-element.64), channel_id=1, source_target_pairs={{0,2},{1,3},{2,4},{3,5},{4,6},{5,7},{6,0},{7,1},{8,10},{9,11},{10,... | collective-permute-start | bytes 884744 | tf_op jit(solution)/shard_map/ppermute | solution.py:174
  93.6 17.3 %collective-permute-done.26 = bf16[2,64,1152]{2,1,0:T(8,128)(2,1)S(1)} collective-permute-done((bf16[2,64,1152]{2,1,0:T(8,128)(2,1)S(1)}, bf16[2,64,1152]{2,1,0:T(8,128)(2,1)S(1)}, u32[]{:S(2)}, u32[]{:S(2)}) %collective-permute-start.26) | collective-permute-done | bytes 294944 | tf_op jit(solution)/shard_map/ppermute | solution.py:174
  110.8 8.1 %collective-permute-done.25 = bf16[2,64,1152]{2,1,0:T(8,128)(2,1)S(1)} collective-permute-done((bf16[2,64,1152]{2,1,0:T(8,128)(2,1)S(1)}, bf16[2,64,1152]{2,1,0:T(8,128)(2,1)S(1)}, u32[]{:S(2)}, u32[]{:S(2)}) %collective-permute-start.25) | collective-permute-done | bytes 294944 | tf_op jit(solution)/shard_map/ppermute | solution.py:174
  (109 shorter events, 21.7 us)
Async XLA Ops:
  0.6 20.7 %collective-permute-start = (bf16[1024,256]{1,0:T(8,128)(2,1)}, bf16[1024,256]{1,0:T(8,128)(2,1)S(1)}, u32[]{:S(2)}, u32[]{:S(2)}) collective-permute-start(bf16[1024,256]{1,0:T(8,128)(2,1)} %param.16), channel_id=1, source_target_pairs={{0,2},{1,3},{2,4},{3,5},{4,6},{5,7},{6,0},{7,1},{8,10},{9,11},{10,... | collective-permute-start | bytes 1572872 | tf_op jit(solution)/shard_map/ppermute | solution.py:174
  2.3 24.4 %collective-permute-start.1 = (bf16[1024,256]{1,0:T(8,128)(2,1)}, bf16[1024,256]{1,0:T(8,128)(2,1)S(1)}, u32[]{:S(2)}, u32[]{:S(2)}) collective-permute-start(bf16[1024,256]{1,0:T(8,128)(2,1)} %param.16), channel_id=1, source_target_pairs={{0,6},{1,7},{2,0},{3,1},{4,2},{5,3},{6,4},{7,5},{8,14},{9,15},{10,... | collective-permute-start | bytes 1572872 | tf_op jit(solution)/shard_map/ppermute | solution.py:174
  5.4 11.4 %collective-permute-start.4 = (bf16[2,64,1152]{2,1,0:T(8,128)(2,1)}, bf16[2,64,1152]{2,1,0:T(8,128)(2,1)S(1)}, u32[]{:S(2)}, u32[]{:S(2)}) collective-permute-start(bf16[2,64,1152]{2,1,0:T(8,128)(2,1)} %pad_maximum_fusion.2), channel_id=1, source_target_pairs={{0,24},{8,16},{16,8},{24,0},{1,25},{9,17},{17,9},{25,1},{2,26},{10... | collective-permute-start | bytes 884744 | tf_op jit(solution)/shard_map/ppermute | solution.py:180
  7.9 13.2 %collective-permute-start.3 = (bf16[2,64,1152]{2,1,0:T(8,128)(2,1)}, bf16[2,64,1152]{2,1,0:T(8,128)(2,1)S(1)}, u32[]{:S(2)}, u32[]{:S(2)}) collective-permute-start(bf16[2,64,1152]{2,1,0:T(8,128)(2,1)} %pad_maximum_fusion.2), channel_id=1, source_target_pairs={{0,16},{8,24},{16,0},{24,8},{1,17},{9,25},{17,1},{25,9},{2,18},{10... | collective-permute-start | bytes 884744 | tf_op jit(solution)/shard_map/ppermute | solution.py:180
  8.4 12.8 %collective-permute-start.2 = (bf16[2,64,1152]{2,1,0:T(8,128)(2,1)}, bf16[2,64,1152]{2,1,0:T(8,128)(2,1)S(1)}, u32[]{:S(2)}, u32[]{:S(2)}) collective-permute-start(bf16[2,64,1152]{2,1,0:T(8,128)(2,1)} %pad_maximum_fusion.2), channel_id=1, source_target_pairs={{0,8},{8,0},{16,24},{24,16},{1,9},{9,1},{17,25},{25,17},{2,10},{10... | collective-permute-start | bytes 884744 | tf_op jit(solution)/shard_map/ppermute | solution.py:180
  26.6 20.2 %collective-permute-start.8 = (bf16[1024,256]{1,0:T(8,128)(2,1)S(1)}, bf16[1024,256]{1,0:T(8,128)(2,1)S(1)}, u32[]{:S(2)}, u32[]{:S(2)}) collective-permute-start(bf16[1024,256]{1,0:T(8,128)(2,1)S(1)} %collective-permute-done), channel_id=1, source_target_pairs={{0,2},{1,3},{2,4},{3,5},{4,6},{5,7},{6,0},{7,1},{8,10},{9,11},{10,... | collective-permute-start | bytes 1572872 | tf_op jit(solution)/shard_map/ppermute | solution.py:174
  27.4 5.4 %collective-permute-start.6 = (bf16[1024,256]{1,0:T(8,128)(2,1)S(1)}, bf16[1024,256]{1,0:T(8,128)(2,1)S(1)}, u32[]{:S(2)}, u32[]{:S(2)}) collective-permute-start(bf16[1024,256]{1,0:T(8,128)(2,1)S(1)} %collective-permute-done), channel_id=1, source_target_pairs={{0,1},{1,0},{2,3},{3,2},{4,5},{5,4},{6,7},{7,6},{8,9},{9,8},{10,11... | collective-permute-start | bytes 1572872 | tf_op jit(solution)/shard_map/ppermute | solution.py:177
  27.7 5.1 %collective-permute-start.5 = (bf16[1024,256]{1,0:T(8,128)(2,1)S(1)}, bf16[1024,256]{1,0:T(8,128)(2,1)S(1)}, u32[]{:S(2)}, u32[]{:S(2)}) collective-permute-start(bf16[1024,256]{1,0:T(8,128)(2,1)S(1)} %copy-done.6), channel_id=1, source_target_pairs={{0,1},{1,0},{2,3},{3,2},{4,5},{5,4},{6,7},{7,6},{8,9},{9,8},{10,11... | collective-permute-start | bytes 1572872 | tf_op jit(solution)/shard_map/ppermute | solution.py:177
  28.2 4.6 %collective-permute-start.7 = (bf16[1024,256]{1,0:T(8,128)(2,1)S(1)}, bf16[1024,256]{1,0:T(8,128)(2,1)S(1)}, u32[]{:S(2)}, u32[]{:S(2)}) collective-permute-start(bf16[1024,256]{1,0:T(8,128)(2,1)S(1)} %collective-permute-done.1), channel_id=1, source_target_pairs={{0,1},{1,0},{2,3},{3,2},{4,5},{5,4},{6,7},{7,6},{8,9},{9,8},{10,11... | collective-permute-start | bytes 1572872 | tf_op jit(solution)/shard_map/ppermute | solution.py:177
  28.3 2.9 %collective-permute-start.19 = (bf16[128,1152]{1,0:T(8,128)(2,1)S(1)}, bf16[128,1152]{1,0:T(8,128)(2,1)S(1)}, u32[]{:S(2)}, u32[]{:S(2)}) collective-permute-start(bf16[128,1152]{1,0:T(8,128)(2,1)S(1)} %bitcast.75), channel_id=1, source_target_pairs={{0,1},{1,0},{2,3},{3,2},{4,5},{5,4},{6,7},{7,6},{8,9},{9,8},{10,11... | collective-permute-start | bytes 884744 | tf_op jit(solution)/shard_map/ppermute | solution.py:177
  31.2 15.6 %collective-permute-start.9 = (bf16[128,1152]{1,0:T(8,128)(2,1)S(1)}, bf16[128,1152]{1,0:T(8,128)(2,1)S(1)}, u32[]{:S(2)}, u32[]{:S(2)}) collective-permute-start(bf16[128,1152]{1,0:T(8,128)(2,1)S(1)} %bitcast.77), channel_id=1, source_target_pairs={{0,2},{1,3},{2,4},{3,5},{4,6},{5,7},{6,0},{7,1},{8,10},{9,11},{10,... | collective-permute-start | bytes 884744 | tf_op jit(solution)/shard_map/ppermute | solution.py:174
  32.8 14.0 %collective-permute-start.10 = (bf16[2,64,1152]{2,1,0:T(8,128)(2,1)S(1)}, bf16[2,64,1152]{2,1,0:T(8,128)(2,1)S(1)}, u32[]{:S(2)}, u32[]{:S(2)}) collective-permute-start(bf16[2,64,1152]{2,1,0:T(8,128)(2,1)S(1)} %pad_maximum_fusion.4), channel_id=1, source_target_pairs={{0,8},{8,0},{16,24},{24,16},{1,9},{9,1},{17,25},{25,17},{2,10},{10... | collective-permute-start | bytes 884744 | tf_op jit(solution)/shard_map/ppermute | solution.py:180
  34.4 14.8 %collective-permute-start.11 = (bf16[2,64,1152]{2,1,0:T(8,128)(2,1)S(1)}, bf16[2,64,1152]{2,1,0:T(8,128)(2,1)S(1)}, u32[]{:S(2)}, u32[]{:S(2)}) collective-permute-start(bf16[2,64,1152]{2,1,0:T(8,128)(2,1)S(1)} %pad_maximum_fusion.4), channel_id=1, source_target_pairs={{0,16},{8,24},{16,0},{24,8},{1,17},{9,25},{17,1},{25,9},{2,18},{10... | collective-permute-start | bytes 884744 | tf_op jit(solution)/shard_map/ppermute | solution.py:180
  35.9 13.3 %collective-permute-start.12 = (bf16[2,64,1152]{2,1,0:T(8,128)(2,1)S(1)}, bf16[2,64,1152]{2,1,0:T(8,128)(2,1)S(1)}, u32[]{:S(2)}, u32[]{:S(2)}) collective-permute-start(bf16[2,64,1152]{2,1,0:T(8,128)(2,1)S(1)} %pad_maximum_fusion.4), channel_id=1, source_target_pairs={{0,24},{8,16},{16,8},{24,0},{1,25},{9,17},{17,9},{25,1},{2,26},{10... | collective-permute-start | bytes 884744 | tf_op jit(solution)/shard_map/ppermute | solution.py:180
  49.2 14.8 %collective-permute-start.18 = (bf16[128,1152]{1,0:T(8,128)(2,1)S(1)}, bf16[128,1152]{1,0:T(8,128)(2,1)S(1)}, u32[]{:S(2)}, u32[]{:S(2)}) collective-permute-start(bf16[128,1152]{1,0:T(8,128)(2,1)S(1)} %collective-permute-done.9), channel_id=1, source_target_pairs={{0,2},{1,3},{2,4},{3,5},{4,6},{5,7},{6,0},{7,1},{8,10},{9,11},{10,... | collective-permute-start | bytes 884744 | tf_op jit(solution)/shard_map/ppermute | solution.py:174
  51.2 12.8 %collective-permute-start.17 = (bf16[128,1152]{1,0:T(8,128)(2,1)S(1)}, bf16[128,1152]{1,0:T(8,128)(2,1)S(1)}, u32[]{:S(2)}, u32[]{:S(2)}) collective-permute-start(bf16[128,1152]{1,0:T(8,128)(2,1)S(1)} %bitcast.79), channel_id=1, source_target_pairs={{0,6},{1,7},{2,0},{3,1},{4,2},{5,3},{6,4},{7,5},{8,14},{9,15},{10,... | collective-permute-start | bytes 884744 | tf_op jit(solution)/shard_map/ppermute | solution.py:174
  53.7 7.3 %collective-permute-start.16 = (bf16[256,256]{1,0:T(8,128)(2,1)S(1)}, bf16[256,256]{1,0:T(8,128)(2,1)S(1)}, u32[]{:S(2)}, u32[]{:S(2)}) collective-permute-start(bf16[256,256]{1,0:T(8,128)(2,1)S(1)} %fusion.7), channel_id=1, source_target_pairs={{0,24},{8,16},{16,8},{24,0},{1,25},{9,17},{17,9},{25,1},{2,26},{10... | collective-permute-start | bytes 393224 | tf_op jit(solution)/shard_map/ppermute | solution.py:180
  55.2 7.8 %collective-permute-start.15 = (bf16[256,256]{1,0:T(8,128)(2,1)S(1)}, bf16[256,256]{1,0:T(8,128)(2,1)S(1)}, u32[]{:S(2)}, u32[]{:S(2)}) collective-permute-start(bf16[256,256]{1,0:T(8,128)(2,1)S(1)} %fusion.7), channel_id=1, source_target_pairs={{0,16},{8,24},{16,0},{24,8},{1,17},{9,25},{17,1},{25,9},{2,18},{10... | collective-permute-start | bytes 393224 | tf_op jit(solution)/shard_map/ppermute | solution.py:180
  56.5 6.7 %collective-permute-start.14 = (bf16[256,256]{1,0:T(8,128)(2,1)S(1)}, bf16[256,256]{1,0:T(8,128)(2,1)S(1)}, u32[]{:S(2)}, u32[]{:S(2)}) collective-permute-start(bf16[256,256]{1,0:T(8,128)(2,1)S(1)} %fusion.7), channel_id=1, source_target_pairs={{0,8},{8,0},{16,24},{24,16},{1,9},{9,1},{17,25},{25,17},{2,10},{10... | collective-permute-start | bytes 393224 | tf_op jit(solution)/shard_map/ppermute | solution.py:180
  64.0 2.4 %collective-permute-start.22 = (bf16[128,1152]{1,0:T(8,128)(2,1)S(1)}, bf16[128,1152]{1,0:T(8,128)(2,1)S(1)}, u32[]{:S(2)}, u32[]{:S(2)}) collective-permute-start(bf16[128,1152]{1,0:T(8,128)(2,1)S(1)} %collective-permute-done.18), channel_id=1, source_target_pairs={{0,1},{1,0},{2,3},{3,2},{4,5},{5,4},{6,7},{7,6},{8,9},{9,8},{10,11... | collective-permute-start | bytes 884744 | tf_op jit(solution)/shard_map/ppermute | solution.py:177
  86.5 2.9 %collective-permute-start.23 = (bf16[4,2,64,1152]{3,2,1,0:T(8,128)(2,1)S(1)}, bf16[4,2,64,1152]{3,2,1,0:T(8,128)(2,1)S(1)}, u32[]{:S(2)}, u32[]{:S(2)}) collective-permute-start(bf16[4,2,64,1152]{3,2,1,0:T(8,128)(2,1)S(1)} %gradients.3), channel_id=1, source_target_pairs={{0,1},{1,0},{2,3},{3,2},{4,5},{5,4},{6,7},{7,6},{8,9},{9,8},{10,11... | collective-permute-start | bytes 3538952 | tf_op jit(solution)/shard_map/ppermute | solution.py:177
  89.8 21.1 %collective-permute-start.26 = (bf16[2,64,1152]{2,1,0:T(8,128)(2,1)S(1)}, bf16[2,64,1152]{2,1,0:T(8,128)(2,1)S(1)}, u32[]{:S(2)}, u32[]{:S(2)}) collective-permute-start(bf16[2,64,1152]{2,1,0:T(8,128)(2,1)S(1)} %get-tuple-element.65), channel_id=1, source_target_pairs={{0,4},{1,5},{2,6},{3,7},{4,0},{5,1},{6,2},{7,3},{8,12},{9,13},{10,... | collective-permute-start | bytes 884744 | tf_op jit(solution)/shard_map/ppermute | solution.py:174
  91.5 27.5 %collective-permute-start.25 = (bf16[2,64,1152]{2,1,0:T(8,128)(2,1)S(1)}, bf16[2,64,1152]{2,1,0:T(8,128)(2,1)S(1)}, u32[]{:S(2)}, u32[]{:S(2)}) collective-permute-start(bf16[2,64,1152]{2,1,0:T(8,128)(2,1)S(1)} %get-tuple-element.66), channel_id=1, source_target_pairs={{0,6},{1,7},{2,0},{3,1},{4,2},{5,3},{6,4},{7,5},{8,14},{9,15},{10,... | collective-permute-start | bytes 884744 | tf_op jit(solution)/shard_map/ppermute | solution.py:174
  91.9 27.1 %collective-permute-start.24 = (bf16[2,64,1152]{2,1,0:T(8,128)(2,1)S(1)}, bf16[2,64,1152]{2,1,0:T(8,128)(2,1)S(1)}, u32[]{:S(2)}, u32[]{:S(2)}) collective-permute-start(bf16[2,64,1152]{2,1,0:T(8,128)(2,1)S(1)} %get-tuple-element.64), channel_id=1, source_target_pairs={{0,2},{1,3},{2,4},{3,5},{4,6},{5,7},{6,0},{7,1},{8,10},{9,11},{10,... | collective-permute-start | bytes 884744 | tf_op jit(solution)/shard_map/ppermute | solution.py:174
  (13 other events, 169.2 us)

commit v5 on v4

--- a/solution.py
+++ b/solution.py
@@ -225,6 +225,7 @@
     rest_own = jnp.concatenate([pre_a, pre_b], axis=2).astype(bf16)
     rest_own, w_there, order = lax.optimization_barrier((rest_own, w_there, jnp.stack(order).astype(jnp.int32)))
     x_ordered = reorder(order, layer_activations, arows)
+    x_ordered, down = lax.optimization_barrier((x_ordered, down))
 
     def x_piece(s, theirs):
         return x_ordered[:, (2 * s + theirs) * arows:(2 * s + theirs + 1) * arows]
@@ -238,7 +239,7 @@
     for s in range(nz - 1):
         plain = add(plain, s, w[s], w_there[s], NN)
     rest_parts = gather_slots(rest_own)
-    w[-1], up, w_there, down, rest_parts = lax.optimization_barrier((w[-1], up, w_there, down, rest_parts))
+    w[-1], up, w_there, rest_parts = lax.optimization_barrier((w[-1], up, w_there, rest_parts))
     up.append(shift(up[-1], 1))
     for k in range(1, nz // 2):
         down.append(shift(down[-1], -1))

time: 121 us -> 119 us (0.983)
  waiting for transfers between devices: 55 us -> 52.1 us
  starting transfers between devices: 23.3 us -> 24.6 us
    ppermute x9, waiting for transfers between devices: 12.6 us -> 10.5 us  [exchange(): return lax.ppermute(x, 'chain', [(i, i ^ k) for i in range(nc)])]
    ppermute x9, waiting for transfers between devices: 38.1 us -> 36.8 us  [shift(): return lax.ppermute(x, 'tok', [(i, (i + 2 * k) % nt) for i in range(nt)])]
    ppermute x9, starting transfers between devices: 10.2 us -> 11.4 us  [shift(): return lax.ppermute(x, 'tok', [(i, (i + 2 * k) % nt) for i in range(nt)])]
where the time goes in v5:
time: 119 us
  waiting for transfers between devices  52.1 us (44%)
  starting transfers between devices  24.6 us (21%)
  Pallas kernels  23 us (19%)
  between operations  6.1 us (5%)
  matrix products  4.92 us (4%)
  local copies, waits for them, and re-layouts  4.56 us (4%)
  other arithmetic  3.69 us (3%)
    ppermute x9, waiting for transfers between devices, shift(): return lax.ppermute(x, 'tok', [(i, (i + 2 * k) % nt) for i in range(nt)])  36.8 us
    pallas_call x1, Pallas kernels, attention(): pl.pallas_call(functools.partial(attention_kernel, scale, nchain, group,...  17.9 us
    ppermute x9, starting transfers between devices, shift(): return lax.ppermute(x, 'tok', [(i, (i + 2 * k) % nt) for i in range(nt)])  11.4 us
    ppermute x9, starting transfers between devices, exchange(): return lax.ppermute(x, 'chain', [(i, i ^ k) for i in range(nc)])  10.6 us
    ppermute x9, waiting for transfers between devices, exchange(): return lax.ppermute(x, 'chain', [(i, i ^ k) for i in range(nc)])  10.5 us
    dot_general x16, matrix products, dot(): return lax.dot_general(a, b, dims, preferred_element_type=f32)  4.92 us
    ppermute x9, waiting for transfers between devices, swap_cores(): return lax.ppermute(x, 'tok', [(i, i ^ 1) for i in range(nt)])  4.81 us
    pallas_call x2, Pallas kernels, gradients(): pl.pallas_call(functools.partial(gradient_kernel, n, nrank), grid_spec=gr...  3.54 us
  transfers between devices with their start and end apart: 27, of which 15 were waited for; matrix products, arithmetic and copies ran while one was open for 9% of the time, Pallas kernels for 3%

profile of v5, /device:TPU:8, one launch (start us, length us, event | category | flops | bytes accessed | tf_op | source)
XLA Modules:
  0.0 119.0 jit_solution(5866910687231273240)
XLA Ops:
  0.6 1.6 %collective-permute-start = (bf16[1024,256]{1,0:T(8,128)(2,1)}, bf16[1024,256]{1,0:T(8,128)(2,1)S(1)}, u32[]{:S(2)}, u32[]{:S(2)}) collective-permute-start(bf16[1024,256]{1,0:T(8,128)(2,1)} %param.16), channel_id=1, source_target_pairs={{0,2},{1,3},{2,4},{3,5},{4,6},{5,7},{6,0},{7,1},{8,10},{9,11},{10,... | collective-permute-start | bytes 1572872 | tf_op jit(solution)/shard_map/ppermute | solution.py:174
  5.4 2.4 %collective-permute-start.4 = (bf16[2,64,1152]{2,1,0:T(8,128)(2,1)}, bf16[2,64,1152]{2,1,0:T(8,128)(2,1)S(1)}, u32[]{:S(2)}, u32[]{:S(2)}) collective-permute-start(bf16[2,64,1152]{2,1,0:T(8,128)(2,1)} %pad_maximum_fusion.2), channel_id=1, source_target_pairs={{0,24},{8,16},{16,8},{24,0},{1,25},{9,17},{17,9},{25,1},{2,26},{10... | collective-permute-start | bytes 884744 | tf_op jit(solution)/shard_map/ppermute | solution.py:180
  15.3 1.3 %gather_fusion = s32[8]{0:T(128)S(1)} fusion(s32[4]{0:T(128)} %constant.144.clone, s32[1024]{0:T(1024)S(1)} %pad_clamp_fusion), kind=kCustom, calls=%fused_computation | custom fusion | bytes 96 | tf_op jit(solution)/shard_map/gather | solution.py:262
  16.8 4.3 %collective-permute-done.3 = bf16[2,64,1152]{2,1,0:T(8,128)(2,1)S(1)} collective-permute-done((bf16[2,64,1152]{2,1,0:T(8,128)(2,1)}, bf16[2,64,1152]{2,1,0:T(8,128)(2,1)S(1)}, u32[]{:S(2)}, u32[]{:S(2)}) %collective-permute-start.3) | collective-permute-done | bytes 294944 | tf_op jit(solution)/shard_map/ppermute | solution.py:180
  21.3 5.3 %collective-permute-done.1 = bf16[1024,256]{1,0:T(8,128)(2,1)S(1)} collective-permute-done((bf16[1024,256]{1,0:T(8,128)(2,1)}, bf16[1024,256]{1,0:T(8,128)(2,1)S(1)}, u32[]{:S(2)}, u32[]{:S(2)}) %collective-permute-start.1) | collective-permute-done | bytes 524320 | tf_op jit(solution)/shard_map/ppermute | solution.py:174
  28.8 2.4 %collective-permute-done.19 = bf16[128,1152]{1,0:T(8,128)(2,1)S(1)} collective-permute-done((bf16[128,1152]{1,0:T(8,128)(2,1)S(1)}, bf16[128,1152]{1,0:T(8,128)(2,1)S(1)}, u32[]{:S(2)}, u32[]{:S(2)}) %collective-permute-start.19) | collective-permute-done | bytes 294944 | tf_op jit(solution)/shard_map/ppermute | solution.py:177
  31.2 1.6 %collective-permute-start.9 = (bf16[128,1152]{1,0:T(8,128)(2,1)S(1)}, bf16[128,1152]{1,0:T(8,128)(2,1)S(1)}, u32[]{:S(2)}, u32[]{:S(2)}) collective-permute-start(bf16[128,1152]{1,0:T(8,128)(2,1)S(1)} %bitcast.77), channel_id=1, source_target_pairs={{0,2},{1,3},{2,4},{3,5},{4,6},{5,7},{6,0},{7,1},{8,10},{9,11},{10,... | collective-permute-start | bytes 884744 | tf_op jit(solution)/shard_map/ppermute | solution.py:174
  32.8 1.6 %collective-permute-start.10 = (bf16[2,64,1152]{2,1,0:T(8,128)(2,1)S(1)}, bf16[2,64,1152]{2,1,0:T(8,128)(2,1)S(1)}, u32[]{:S(2)}, u32[]{:S(2)}) collective-permute-start(bf16[2,64,1152]{2,1,0:T(8,128)(2,1)S(1)} %pad_maximum_fusion.4), channel_id=1, source_target_pairs={{0,8},{8,0},{16,24},{24,16},{1,9},{9,1},{17,25},{25,17},{2,10},{10... | collective-permute-start | bytes 884744 | tf_op jit(solution)/shard_map/ppermute | solution.py:180
  34.4 1.5 %collective-permute-start.11 = (bf16[2,64,1152]{2,1,0:T(8,128)(2,1)S(1)}, bf16[2,64,1152]{2,1,0:T(8,128)(2,1)S(1)}, u32[]{:S(2)}, u32[]{:S(2)}) collective-permute-start(bf16[2,64,1152]{2,1,0:T(8,128)(2,1)S(1)} %pad_maximum_fusion.4), channel_id=1, source_target_pairs={{0,16},{8,24},{16,0},{24,8},{1,17},{9,25},{17,1},{25,9},{2,18},{10... | collective-permute-start | bytes 884744 | tf_op jit(solution)/shard_map/ppermute | solution.py:180
  36.4 1.6 %reorder.1 = bf16[256,8192]{1,0:T(8,128)(2,1)S(1)} custom-call(s32[8]{0:T(128)S(1)} %stack.77.pos_ref, bf16[256,8192]{1,0:T(8,128)(2,1)S(1)} %copy-done), custom_call_target="tpu_custom_call" | custom-call | bytes 134217728 | tf_op jit(solution)/shard_map/reorder/pallas_call | solution.py:154
  40.1 6.7 %collective-permute-done.9 = bf16[128,1152]{1,0:T(8,128)(2,1)S(1)} collective-permute-done((bf16[128,1152]{1,0:T(8,128)(2,1)S(1)}, bf16[128,1152]{1,0:T(8,128)(2,1)S(1)}, u32[]{:S(2)}, u32[]{:S(2)}) %collective-permute-start.9) | collective-permute-done | bytes 294944 | tf_op jit(solution)/shard_map/ppermute | solution.py:174
  46.8 2.1 %collective-permute-start.17 = (bf16[128,1152]{1,0:T(8,128)(2,1)S(1)}, bf16[128,1152]{1,0:T(8,128)(2,1)S(1)}, u32[]{:S(2)}, u32[]{:S(2)}) collective-permute-start(bf16[128,1152]{1,0:T(8,128)(2,1)S(1)} %bitcast.79), channel_id=1, source_target_pairs={{0,6},{1,7},{2,0},{3,1},{4,2},{5,3},{6,4},{7,5},{8,14},{9,15},{10,... | collective-permute-start | bytes 884744 | tf_op jit(solution)/shard_map/ppermute | solution.py:174
  49.2 1.5 %collective-permute-start.18 = (bf16[128,1152]{1,0:T(8,128)(2,1)S(1)}, bf16[128,1152]{1,0:T(8,128)(2,1)S(1)}, u32[]{:S(2)}, u32[]{:S(2)}) collective-permute-start(bf16[128,1152]{1,0:T(8,128)(2,1)S(1)} %collective-permute-done.9), channel_id=1, source_target_pairs={{0,2},{1,3},{2,4},{3,5},{4,6},{5,7},{6,0},{7,1},{8,10},{9,11},{10,... | collective-permute-start | bytes 884744 | tf_op jit(solution)/shard_map/ppermute | solution.py:174
  53.7 1.6 %collective-permute-start.16 = (bf16[256,256]{1,0:T(8,128)(2,1)S(1)}, bf16[256,256]{1,0:T(8,128)(2,1)S(1)}, u32[]{:S(2)}, u32[]{:S(2)}) collective-permute-start(bf16[256,256]{1,0:T(8,128)(2,1)S(1)} %fusion.7), channel_id=1, source_target_pairs={{0,24},{8,16},{16,8},{24,0},{1,25},{9,17},{17,9},{25,1},{2,26},{10... | collective-permute-start | bytes 393224 | tf_op jit(solution)/shard_map/ppermute | solution.py:180
  55.2 1.2 %collective-permute-start.15 = (bf16[256,256]{1,0:T(8,128)(2,1)S(1)}, bf16[256,256]{1,0:T(8,128)(2,1)S(1)}, u32[]{:S(2)}, u32[]{:S(2)}) collective-permute-start(bf16[256,256]{1,0:T(8,128)(2,1)S(1)} %fusion.7), channel_id=1, source_target_pairs={{0,16},{8,24},{16,0},{24,8},{1,17},{9,25},{17,1},{25,9},{2,18},{10... | collective-permute-start | bytes 393224 | tf_op jit(solution)/shard_map/ppermute | solution.py:180
  57.3 3.8 %collective-permute-done.16 = bf16[256,256]{1,0:T(8,128)(2,1)S(1)} collective-permute-done((bf16[256,256]{1,0:T(8,128)(2,1)S(1)}, bf16[256,256]{1,0:T(8,128)(2,1)S(1)}, u32[]{:S(2)}, u32[]{:S(2)}) %collective-permute-start.16) | collective-permute-done | bytes 131104 | tf_op jit(solution)/shard_map/ppermute | solution.py:180
  61.0 2.0 %collective-permute-done.15 = bf16[256,256]{1,0:T(8,128)(2,1)S(1)} collective-permute-done((bf16[256,256]{1,0:T(8,128)(2,1)S(1)}, bf16[256,256]{1,0:T(8,128)(2,1)S(1)}, u32[]{:S(2)}, u32[]{:S(2)}) %collective-permute-start.15) | collective-permute-done | bytes 131104 | tf_op jit(solution)/shard_map/ppermute | solution.py:180
  66.1 17.9 %attention.1 = (bf16[256,128]{1,0:T(8,128)(2,1)S(1)}, f32[8,2,64,128]{3,2,1,0:T(8,128)S(1)}) custom-call(s32[9]{0:T(128)S(1)} %pad_add_fusion.pos_ref, bf16[256,8192]{1,0:T(8,128)(2,1)S(1)} %copy-done.1, bf16[256,8192]{1,0:T(8,128)(2,1)S(1)} %copy-done.2, bf16[256,1024]{1,0:T(8,128)(2,1)S(1)} %copy-done.3, ...), custom_call_target="tpu_custom_call" | custom-call | flops 10000000000 | bytes 20000000 | tf_op jit(solution)/shard_map/attention/pallas_call | solution.py:97
  84.0 1.8 %gradients.3 = bf16[4,2,64,1152]{3,2,1,0:T(8,128)(2,1)S(1)} custom-call(s32[4]{0:T(128)S(1)} %add_subtract_fusion.pos_ref, bf16[256,8192]{1,0:T(8,128)(2,1)S(1)} %copy-done, bf16[256,128]{1,0:T(8,128)(2,1)S(1)} %get-tuple-element.60.lg_ref, f32[8,2,64,128]{3,2,1,0:T(8,128)S(1)} %get-tuple-element.61.rt_ref), custom_call_target="tpu_custom_call" | custom-call | flops 268435456 | bytes 3000000 | tf_op jit(solution)/shard_map/gradients/pallas_call | solution.py:134
  86.3 1.8 %gradients.2 = f32[4,2,64,1152]{3,2,1,0:T(8,128)S(1)} custom-call(s32[4]{0:T(128)S(1)} %broadcast_add_fusion.pos_ref, bf16[256,8192]{1,0:T(8,128)(2,1)S(1)} %copy-done, bf16[256,128]{1,0:T(8,128)(2,1)S(1)} %get-tuple-element.60.lg_ref, f32[8,2,64,128]{3,2,1,0:T(8,128)S(1)} %get-tuple-element.61.rt_ref), custom_call_target="tpu_custom_call" | custom-call | flops 268435456 | bytes 3000000 | tf_op jit(solution)/shard_map/gradients/pallas_call | solution.py:134
  89.1 1.4 %collective-permute-start.26 = (bf16[2,64,1152]{2,1,0:T(8,128)(2,1)S(1)}, bf16[2,64,1152]{2,1,0:T(8,128)(2,1)S(1)}, u32[]{:S(2)}, u32[]{:S(2)}) collective-permute-start(bf16[2,64,1152]{2,1,0:T(8,128)(2,1)S(1)} %get-tuple-element.67), channel_id=1, source_target_pairs={{0,4},{1,5},{2,6},{3,7},{4,0},{5,1},{6,2},{7,3},{8,12},{9,13},{10,... | collective-permute-start | bytes 884744 | tf_op jit(solution)/shard_map/ppermute | solution.py:174
  90.4 1.3 %collective-permute-start.25 = (bf16[2,64,1152]{2,1,0:T(8,128)(2,1)S(1)}, bf16[2,64,1152]{2,1,0:T(8,128)(2,1)S(1)}, u32[]{:S(2)}, u32[]{:S(2)}) collective-permute-start(bf16[2,64,1152]{2,1,0:T(8,128)(2,1)S(1)} %get-tuple-element.68), channel_id=1, source_target_pairs={{0,6},{1,7},{2,0},{3,1},{4,2},{5,3},{6,4},{7,5},{8,14},{9,15},{10,... | collective-permute-start | bytes 884744 | tf_op jit(solution)/shard_map/ppermute | solution.py:174
  92.5 17.9 %collective-permute-done.26 = bf16[2,64,1152]{2,1,0:T(8,128)(2,1)S(1)} collective-permute-done((bf16[2,64,1152]{2,1,0:T(8,128)(2,1)S(1)}, bf16[2,64,1152]{2,1,0:T(8,128)(2,1)S(1)}, u32[]{:S(2)}, u32[]{:S(2)}) %collective-permute-start.26) | collective-permute-done | bytes 294944 | tf_op jit(solution)/shard_map/ppermute | solution.py:174
  110.4 6.9 %collective-permute-done.25 = bf16[2,64,1152]{2,1,0:T(8,128)(2,1)S(1)} collective-permute-done((bf16[2,64,1152]{2,1,0:T(8,128)(2,1)S(1)}, bf16[2,64,1152]{2,1,0:T(8,128)(2,1)S(1)}, u32[]{:S(2)}, u32[]{:S(2)}) %collective-permute-start.25) | collective-permute-done | bytes 294944 | tf_op jit(solution)/shard_map/ppermute | solution.py:174
  (109 shorter events, 21.6 us)
Async XLA Ops:
  0.6 20.7 %collective-permute-start = (bf16[1024,256]{1,0:T(8,128)(2,1)}, bf16[1024,256]{1,0:T(8,128)(2,1)S(1)}, u32[]{:S(2)}, u32[]{:S(2)}) collective-permute-start(bf16[1024,256]{1,0:T(8,128)(2,1)} %param.16), channel_id=1, source_target_pairs={{0,2},{1,3},{2,4},{3,5},{4,6},{5,7},{6,0},{7,1},{8,10},{9,11},{10,... | collective-permute-start | bytes 1572872 | tf_op jit(solution)/shard_map/ppermute | solution.py:174
  2.3 24.4 %collective-permute-start.1 = (bf16[1024,256]{1,0:T(8,128)(2,1)}, bf16[1024,256]{1,0:T(8,128)(2,1)S(1)}, u32[]{:S(2)}, u32[]{:S(2)}) collective-permute-start(bf16[1024,256]{1,0:T(8,128)(2,1)} %param.16), channel_id=1, source_target_pairs={{0,6},{1,7},{2,0},{3,1},{4,2},{5,3},{6,4},{7,5},{8,14},{9,15},{10,... | collective-permute-start | bytes 1572872 | tf_op jit(solution)/shard_map/ppermute | solution.py:174
  5.4 11.4 %collective-permute-start.4 = (bf16[2,64,1152]{2,1,0:T(8,128)(2,1)}, bf16[2,64,1152]{2,1,0:T(8,128)(2,1)S(1)}, u32[]{:S(2)}, u32[]{:S(2)}) collective-permute-start(bf16[2,64,1152]{2,1,0:T(8,128)(2,1)} %pad_maximum_fusion.2), channel_id=1, source_target_pairs={{0,24},{8,16},{16,8},{24,0},{1,25},{9,17},{17,9},{25,1},{2,26},{10... | collective-permute-start | bytes 884744 | tf_op jit(solution)/shard_map/ppermute | solution.py:180
  7.9 13.2 %collective-permute-start.3 = (bf16[2,64,1152]{2,1,0:T(8,128)(2,1)}, bf16[2,64,1152]{2,1,0:T(8,128)(2,1)S(1)}, u32[]{:S(2)}, u32[]{:S(2)}) collective-permute-start(bf16[2,64,1152]{2,1,0:T(8,128)(2,1)} %pad_maximum_fusion.2), channel_id=1, source_target_pairs={{0,16},{8,24},{16,0},{24,8},{1,17},{9,25},{17,1},{25,9},{2,18},{10... | collective-permute-start | bytes 884744 | tf_op jit(solution)/shard_map/ppermute | solution.py:180
  8.4 12.8 %collective-permute-start.2 = (bf16[2,64,1152]{2,1,0:T(8,128)(2,1)}, bf16[2,64,1152]{2,1,0:T(8,128)(2,1)S(1)}, u32[]{:S(2)}, u32[]{:S(2)}) collective-permute-start(bf16[2,64,1152]{2,1,0:T(8,128)(2,1)} %pad_maximum_fusion.2), channel_id=1, source_target_pairs={{0,8},{8,0},{16,24},{24,16},{1,9},{9,1},{17,25},{25,17},{2,10},{10... | collective-permute-start | bytes 884744 | tf_op jit(solution)/shard_map/ppermute | solution.py:180
  26.6 22.2 %collective-permute-start.8 = (bf16[1024,256]{1,0:T(8,128)(2,1)S(1)}, bf16[1024,256]{1,0:T(8,128)(2,1)S(1)}, u32[]{:S(2)}, u32[]{:S(2)}) collective-permute-start(bf16[1024,256]{1,0:T(8,128)(2,1)S(1)} %collective-permute-done), channel_id=1, source_target_pairs={{0,2},{1,3},{2,4},{3,5},{4,6},{5,7},{6,0},{7,1},{8,10},{9,11},{10,... | collective-permute-start | bytes 1572872 | tf_op jit(solution)/shard_map/ppermute | solution.py:174
  27.4 5.4 %collective-permute-start.6 = (bf16[1024,256]{1,0:T(8,128)(2,1)S(1)}, bf16[1024,256]{1,0:T(8,128)(2,1)S(1)}, u32[]{:S(2)}, u32[]{:S(2)}) collective-permute-start(bf16[1024,256]{1,0:T(8,128)(2,1)S(1)} %collective-permute-done), channel_id=1, source_target_pairs={{0,1},{1,0},{2,3},{3,2},{4,5},{5,4},{6,7},{7,6},{8,9},{9,8},{10,11... | collective-permute-start | bytes 1572872 | tf_op jit(solution)/shard_map/ppermute | solution.py:177
  27.7 5.1 %collective-permute-start.5 = (bf16[1024,256]{1,0:T(8,128)(2,1)S(1)}, bf16[1024,256]{1,0:T(8,128)(2,1)S(1)}, u32[]{:S(2)}, u32[]{:S(2)}) collective-permute-start(bf16[1024,256]{1,0:T(8,128)(2,1)S(1)} %copy-done.6), channel_id=1, source_target_pairs={{0,1},{1,0},{2,3},{3,2},{4,5},{5,4},{6,7},{7,6},{8,9},{9,8},{10,11... | collective-permute-start | bytes 1572872 | tf_op jit(solution)/shard_map/ppermute | solution.py:177
  28.2 4.6 %collective-permute-start.7 = (bf16[1024,256]{1,0:T(8,128)(2,1)S(1)}, bf16[1024,256]{1,0:T(8,128)(2,1)S(1)}, u32[]{:S(2)}, u32[]{:S(2)}) collective-permute-start(bf16[1024,256]{1,0:T(8,128)(2,1)S(1)} %collective-permute-done.1), channel_id=1, source_target_pairs={{0,1},{1,0},{2,3},{3,2},{4,5},{5,4},{6,7},{7,6},{8,9},{9,8},{10,11... | collective-permute-start | bytes 1572872 | tf_op jit(solution)/shard_map/ppermute | solution.py:177
  28.3 2.9 %collective-permute-start.19 = (bf16[128,1152]{1,0:T(8,128)(2,1)S(1)}, bf16[128,1152]{1,0:T(8,128)(2,1)S(1)}, u32[]{:S(2)}, u32[]{:S(2)}) collective-permute-start(bf16[128,1152]{1,0:T(8,128)(2,1)S(1)} %bitcast.75), channel_id=1, source_target_pairs={{0,1},{1,0},{2,3},{3,2},{4,5},{5,4},{6,7},{7,6},{8,9},{9,8},{10,11... | collective-permute-start | bytes 884744 | tf_op jit(solution)/shard_map/ppermute | solution.py:177
  31.2 15.6 %collective-permute-start.9 = (bf16[128,1152]{1,0:T(8,128)(2,1)S(1)}, bf16[128,1152]{1,0:T(8,128)(2,1)S(1)}, u32[]{:S(2)}, u32[]{:S(2)}) collective-permute-start(bf16[128,1152]{1,0:T(8,128)(2,1)S(1)} %bitcast.77), channel_id=1, source_target_pairs={{0,2},{1,3},{2,4},{3,5},{4,6},{5,7},{6,0},{7,1},{8,10},{9,11},{10,... | collective-permute-start | bytes 884744 | tf_op jit(solution)/shard_map/ppermute | solution.py:174
  32.8 16.1 %collective-permute-start.10 = (bf16[2,64,1152]{2,1,0:T(8,128)(2,1)S(1)}, bf16[2,64,1152]{2,1,0:T(8,128)(2,1)S(1)}, u32[]{:S(2)}, u32[]{:S(2)}) collective-permute-start(bf16[2,64,1152]{2,1,0:T(8,128)(2,1)S(1)} %pad_maximum_fusion.4), channel_id=1, source_target_pairs={{0,8},{8,0},{16,24},{24,16},{1,9},{9,1},{17,25},{25,17},{2,10},{10... | collective-permute-start | bytes 884744 | tf_op jit(solution)/shard_map/ppermute | solution.py:180
  34.4 14.8 %collective-permute-start.11 = (bf16[2,64,1152]{2,1,0:T(8,128)(2,1)S(1)}, bf16[2,64,1152]{2,1,0:T(8,128)(2,1)S(1)}, u32[]{:S(2)}, u32[]{:S(2)}) collective-permute-start(bf16[2,64,1152]{2,1,0:T(8,128)(2,1)S(1)} %pad_maximum_fusion.4), channel_id=1, source_target_pairs={{0,16},{8,24},{16,0},{24,8},{1,17},{9,25},{17,1},{25,9},{2,18},{10... | collective-permute-start | bytes 884744 | tf_op jit(solution)/shard_map/ppermute | solution.py:180
  35.9 13.3 %collective-permute-start.12 = (bf16[2,64,1152]{2,1,0:T(8,128)(2,1)S(1)}, bf16[2,64,1152]{2,1,0:T(8,128)(2,1)S(1)}, u32[]{:S(2)}, u32[]{:S(2)}) collective-permute-start(bf16[2,64,1152]{2,1,0:T(8,128)(2,1)S(1)} %pad_maximum_fusion.4), channel_id=1, source_target_pairs={{0,24},{8,16},{16,8},{24,0},{1,25},{9,17},{17,9},{25,1},{2,26},{10... | collective-permute-start | bytes 884744 | tf_op jit(solution)/shard_map/ppermute | solution.py:180
  46.8 16.4 %collective-permute-start.17 = (bf16[128,1152]{1,0:T(8,128)(2,1)S(1)}, bf16[128,1152]{1,0:T(8,128)(2,1)S(1)}, u32[]{:S(2)}, u32[]{:S(2)}) collective-permute-start(bf16[128,1152]{1,0:T(8,128)(2,1)S(1)} %bitcast.79), channel_id=1, source_target_pairs={{0,6},{1,7},{2,0},{3,1},{4,2},{5,3},{6,4},{7,5},{8,14},{9,15},{10,... | collective-permute-start | bytes 884744 | tf_op jit(solution)/shard_map/ppermute | solution.py:174
  49.2 14.0 %collective-permute-start.18 = (bf16[128,1152]{1,0:T(8,128)(2,1)S(1)}, bf16[128,1152]{1,0:T(8,128)(2,1)S(1)}, u32[]{:S(2)}, u32[]{:S(2)}) collective-permute-start(bf16[128,1152]{1,0:T(8,128)(2,1)S(1)} %collective-permute-done.9), channel_id=1, source_target_pairs={{0,2},{1,3},{2,4},{3,5},{4,6},{5,7},{6,0},{7,1},{8,10},{9,11},{10,... | collective-permute-start | bytes 884744 | tf_op jit(solution)/shard_map/ppermute | solution.py:174
  53.7 7.3 %collective-permute-start.16 = (bf16[256,256]{1,0:T(8,128)(2,1)S(1)}, bf16[256,256]{1,0:T(8,128)(2,1)S(1)}, u32[]{:S(2)}, u32[]{:S(2)}) collective-permute-start(bf16[256,256]{1,0:T(8,128)(2,1)S(1)} %fusion.7), channel_id=1, source_target_pairs={{0,24},{8,16},{16,8},{24,0},{1,25},{9,17},{17,9},{25,1},{2,26},{10... | collective-permute-start | bytes 393224 | tf_op jit(solution)/shard_map/ppermute | solution.py:180
  55.2 7.8 %collective-permute-start.15 = (bf16[256,256]{1,0:T(8,128)(2,1)S(1)}, bf16[256,256]{1,0:T(8,128)(2,1)S(1)}, u32[]{:S(2)}, u32[]{:S(2)}) collective-permute-start(bf16[256,256]{1,0:T(8,128)(2,1)S(1)} %fusion.7), channel_id=1, source_target_pairs={{0,16},{8,24},{16,0},{24,8},{1,17},{9,25},{17,1},{25,9},{2,18},{10... | collective-permute-start | bytes 393224 | tf_op jit(solution)/shard_map/ppermute | solution.py:180
  56.5 6.7 %collective-permute-start.14 = (bf16[256,256]{1,0:T(8,128)(2,1)S(1)}, bf16[256,256]{1,0:T(8,128)(2,1)S(1)}, u32[]{:S(2)}, u32[]{:S(2)}) collective-permute-start(bf16[256,256]{1,0:T(8,128)(2,1)S(1)} %fusion.7), channel_id=1, source_target_pairs={{0,8},{8,0},{16,24},{24,16},{1,9},{9,1},{17,25},{25,17},{2,10},{10... | collective-permute-start | bytes 393224 | tf_op jit(solution)/shard_map/ppermute | solution.py:180
  63.2 2.5 %collective-permute-start.22 = (bf16[128,1152]{1,0:T(8,128)(2,1)S(1)}, bf16[128,1152]{1,0:T(8,128)(2,1)S(1)}, u32[]{:S(2)}, u32[]{:S(2)}) collective-permute-start(bf16[128,1152]{1,0:T(8,128)(2,1)S(1)} %collective-permute-done.18), channel_id=1, source_target_pairs={{0,1},{1,0},{2,3},{3,2},{4,5},{5,4},{6,7},{7,6},{8,9},{9,8},{10,11... | collective-permute-start | bytes 884744 | tf_op jit(solution)/shard_map/ppermute | solution.py:177
  85.8 2.9 %collective-permute-start.23 = (bf16[4,2,64,1152]{3,2,1,0:T(8,128)(2,1)S(1)}, bf16[4,2,64,1152]{3,2,1,0:T(8,128)(2,1)S(1)}, u32[]{:S(2)}, u32[]{:S(2)}) collective-permute-start(bf16[4,2,64,1152]{3,2,1,0:T(8,128)(2,1)S(1)} %gradients.3), channel_id=1, source_target_pairs={{0,1},{1,0},{2,3},{3,2},{4,5},{5,4},{6,7},{7,6},{8,9},{9,8},{10,11... | collective-permute-start | bytes 3538952 | tf_op jit(solution)/shard_map/ppermute | solution.py:177
  89.1 21.4 %collective-permute-start.26 = (bf16[2,64,1152]{2,1,0:T(8,128)(2,1)S(1)}, bf16[2,64,1152]{2,1,0:T(8,128)(2,1)S(1)}, u32[]{:S(2)}, u32[]{:S(2)}) collective-permute-start(bf16[2,64,1152]{2,1,0:T(8,128)(2,1)S(1)} %get-tuple-element.67), channel_id=1, source_target_pairs={{0,4},{1,5},{2,6},{3,7},{4,0},{5,1},{6,2},{7,3},{8,12},{9,13},{10,... | collective-permute-start | bytes 884744 | tf_op jit(solution)/shard_map/ppermute | solution.py:174
  90.4 26.9 %collective-permute-start.25 = (bf16[2,64,1152]{2,1,0:T(8,128)(2,1)S(1)}, bf16[2,64,1152]{2,1,0:T(8,128)(2,1)S(1)}, u32[]{:S(2)}, u32[]{:S(2)}) collective-permute-start(bf16[2,64,1152]{2,1,0:T(8,128)(2,1)S(1)} %get-tuple-element.68), channel_id=1, source_target_pairs={{0,6},{1,7},{2,0},{3,1},{4,2},{5,3},{6,4},{7,5},{8,14},{9,15},{10,... | collective-permute-start | bytes 884744 | tf_op jit(solution)/shard_map/ppermute | solution.py:174
  91.7 25.6 %collective-permute-start.24 = (bf16[2,64,1152]{2,1,0:T(8,128)(2,1)S(1)}, bf16[2,64,1152]{2,1,0:T(8,128)(2,1)S(1)}, u32[]{:S(2)}, u32[]{:S(2)}) collective-permute-start(bf16[2,64,1152]{2,1,0:T(8,128)(2,1)S(1)} %get-tuple-element.66), channel_id=1, source_target_pairs={{0,2},{1,3},{2,4},{3,5},{4,6},{5,7},{6,0},{7,1},{8,10},{9,11},{10,... | collective-permute-start | bytes 884744 | tf_op jit(solution)/shard_map/ppermute | solution.py:174
  (13 other events, 167.1 us)
